TPU v7x, 32 devices: a whole 2x2x4 slice. The times are simulated.
32 devices in a mesh: ctx: 2 (over y), fsdp: 16 (over z, x, core).
Axes of the slice: x: 2, y: 2, z: 4, core: 2. Of those that a mesh axis runs over, the one named last changes fastest.
Arguments:
- tokens: bfloat16 [2, 16, 1536, 1024], P(None, 'fsdp', 'ctx'), may hold values from -6 to 6
- encoded: bfloat16 [2, 16, 1024, 1024], P(None, 'fsdp', 'ctx'), may hold values from -6 to 6
- cotangent: bfloat16 [2, 16, 1536, 1024], P(None, 'fsdp', 'ctx'), may hold values from -6 to 6
- order: int32 [2, 16, 1536], P(None, 'fsdp'), may hold values from 0 to 1535, as said below
- target_lengths: int32 [2, 16, 4], P(None, 'fsdp'), may hold values from 1 to 1152, as said below
- source_lengths: int32 [2, 16, 4], P(None, 'fsdp'), may hold values from 1 to 512, 1024 in all within a row
- self_project: bfloat16 [1024, 3072], P('fsdp'), may hold values from -0.25 to 0.25
- self_output: bfloat16 [1024, 1024], P('fsdp'), may hold values from -0.75 to 0.75
- cross_query: bfloat16 [1024, 1024], P('fsdp'), may hold values from -0.25 to 0.25
- cross_source: bfloat16 [1024, 2048], P('fsdp'), may hold values from -0.25 to 0.25
- cross_output: bfloat16 [1024, 1024], P('fsdp'), may hold values from -0.75 to 0.75
- feed_in: bfloat16 [1024, 4096], P('fsdp'), may hold values from -0.1875 to 0.1875
- feed_out: bfloat16 [4096, 1024], P('fsdp'), may hold values from -0.09375 to 0.09375
- norm_gain: bfloat16 [3, 1024], P(None, 'fsdp'), may hold values from 0.5 to 1.5
- norm_bias: bfloat16 [3, 1024], P(None, 'fsdp'), may hold values from -2 to 2
Outputs:
- output: bfloat16 [2, 16, 1536, 1024], P(None, 'fsdp', 'ctx')
- grad_tokens: bfloat16 [2, 16, 1536, 1024], P(None, 'fsdp', 'ctx')
- grad_encoded: bfloat16 [2, 16, 1024, 1024], P(None, 'fsdp', 'ctx')
- grad_self_project: float32 [1024, 3072], P('fsdp')
- grad_self_output: float32 [1024, 1024], P('fsdp')
- grad_cross_query: float32 [1024, 1024], P('fsdp')
- grad_cross_source: float32 [1024, 2048], P('fsdp')
- grad_cross_output: float32 [1024, 1024], P('fsdp')
- grad_feed_in: float32 [1024, 4096], P('fsdp')
- grad_feed_out: float32 [4096, 1024], P('fsdp')
- grad_norm_gain: float32 [3, 1024], P(None, 'fsdp')
- grad_norm_bias: float32 [2, 1024], P(None, 'fsdp')
- grad_feed_norm_bias: float32 [1024], P('fsdp')
Inputs may be any that keep to these rules, and one draw needn't show every extreme that they name: Within a pack the slots form blocks of 384 in a row; each pair of blocks 2i, 2i + 1 holds, in increasing order, the positions of one of the first 1536 / 768 position blocks and of one of the later ones; each position once. `target_lengths`: A pack's lengths sum to 1536; its first document has exactly 1152 positions. `source_lengths`: A pack's lengths sum to 1024; source document k belongs to target document k.
All inputs are finite; a program needn't handle non-finite values.
Results may differ from a plain program's by a relative error of at most 0.029.
Values may be sent and summed in bfloat16 or wider, within the bound.
No kernel may reach another device: no remote copies, remote signals or barrier semaphores. Data moves between devices by JAX's collectives and lax.ppermute only.
A program may use at most 232 MiB of HBM per device.

v0:
```python
import math

import jax
import jax.numpy as jnp
from jax import lax
from jax.sharding import PartitionSpec as P

HEAD = 64


MASKED = -1e30


def as_sent(x):

    def short(part):
        return part.astype(jnp.bfloat16) if part.dtype == jnp.float32 else part

    return jax.tree.map(short, x)


def norm_apply(values, gain, bias):
    mean = jnp.mean(values, axis=-1, keepdims=True)
    centred = values - mean
    spread = jnp.mean(centred * centred, axis=-1, keepdims=True)
    return centred * lax.rsqrt(spread + 1e-05) * gain + bias


def gelu_exact(values):
    return jax.nn.gelu(values, approximate=False)


def docs_of(places, lengths):
    ends = jnp.cumsum(lengths)
    return jnp.sum((places[:, None] >= ends[None, :]).astype(jnp.int32), axis=1)


def split_heads(values):
    return values.reshape(values.shape[0], -1, HEAD)


def block_scores(query, pairs, allowed, start, count):
    model = query.shape[1]
    block = lax.dynamic_slice_in_dim(pairs, start, count, 0)
    scores = jnp.einsum(
        "qhd,khd->hqk",
        split_heads(query),
        split_heads(block[:, :model]),
        preferred_element_type=jnp.float32,
    )
    scores = jnp.where(allowed(start, count)[None], scores * HEAD ** (-0.5), MASKED)
    return (scores, block)


def log_mass(query, pairs, allowed, width):
    rows, model = query.shape
    heads = model // HEAD

    def step(index, carry):
        peak, total = carry
        scores, _ = block_scores(query, pairs, allowed, index * width, width)
        new_peak = jnp.maximum(peak, jnp.max(scores, axis=2))
        total = total * jnp.exp(peak - new_peak) + jnp.sum(
            jnp.exp(scores - new_peak[:, :, None]), axis=2
        )
        return (new_peak, total)

    begin = (jnp.full((heads, rows), MASKED, jnp.float32), jnp.zeros((heads, rows), jnp.float32))
    peak, total = lax.fori_loop(0, pairs.shape[0] // width, step, begin)
    return peak + jnp.log(total)


def attend_forward(query, pairs, allowed, width, log_total):
    rows, model = query.shape

    def step(index, mixed):
        scores, block = block_scores(query, pairs, allowed, index * width, width)
        probs = jnp.exp(scores - log_total[:, :, None]).astype(jnp.bfloat16)
        return mixed + jnp.einsum(
            "hqk,khd->qhd", probs, split_heads(block[:, model:]), preferred_element_type=jnp.float32
        )

    mixed = lax.fori_loop(
        0, pairs.shape[0] // width, step, jnp.zeros((rows, model // HEAD, HEAD), jnp.float32)
    )
    return mixed.reshape(rows, model).astype(jnp.bfloat16)


def score_grads(query, pairs, allowed, grad_mixed, log_total, start, count):
    model = query.shape[1]
    scores, block = block_scores(query, pairs, allowed, start, count)
    probs = jnp.exp(scores - log_total[:, :, None])
    grad_probs = jnp.einsum(
        "qhd,khd->hqk",
        split_heads(grad_mixed),
        split_heads(block[:, model:]),
        preferred_element_type=jnp.float32,
    )
    return (probs, grad_probs, block)


def attend_delta(query, pairs, allowed, grad_mixed, log_total, width):
    rows, model = query.shape

    def step(index, delta):
        probs, grad_probs, _ = score_grads(
            query, pairs, allowed, grad_mixed, log_total, index * width, width
        )
        return delta + jnp.sum(probs * grad_probs, axis=2)

    return lax.fori_loop(
        0, pairs.shape[0] // width, step, jnp.zeros((model // HEAD, rows), jnp.float32)
    )


def attend_query_grad(query, pairs, allowed, grad_mixed, log_total, delta, width):
    rows, model = query.shape

    def step(index, grad):
        probs, grad_probs, block = score_grads(
            query, pairs, allowed, grad_mixed, log_total, index * width, width
        )
        grad_scores = (probs * (grad_probs - delta[:, :, None])).astype(jnp.bfloat16)
        return grad + jnp.einsum(
            "hqk,khd->qhd",
            grad_scores,
            split_heads(block[:, :model]),
            preferred_element_type=jnp.float32,
        )

    grad = lax.fori_loop(
        0, pairs.shape[0] // width, step, jnp.zeros((rows, model // HEAD, HEAD), jnp.float32)
    )
    return (grad.reshape(rows, model) * HEAD ** (-0.5)).astype(jnp.bfloat16)


def key_terms(query, pairs, allowed, grad_mixed, log_total, delta, width, count):
    model = query.shape[1]
    step_width = math.gcd(count, width)

    def step(index, terms):
        probs, grad_probs, _ = score_grads(
            query, pairs, allowed, grad_mixed, log_total, index * step_width, step_width
        )
        grad_scores = (probs * (grad_probs - delta[:, :, None])).astype(jnp.bfloat16)
        grad_keys = jnp.einsum(
            "hqk,qhd->khd", grad_scores, split_heads(query), preferred_element_type=jnp.float32
        ) * HEAD ** (-0.5)
        grad_values = jnp.einsum(
            "hqk,qhd->khd",
            probs.astype(jnp.bfloat16),
            split_heads(grad_mixed),
            preferred_element_type=jnp.float32,
        )
        piece = jnp.concatenate(
            [grad_keys.reshape(step_width, model), grad_values.reshape(step_width, model)], axis=1
        )
        return lax.dynamic_update_slice_in_dim(terms, piece, index * step_width, 0)

    return lax.fori_loop(0, count // step_width, step, jnp.zeros((count, 2 * model), jnp.float32))


def body(
    tokens,
    encoded,
    cotangent,
    order,
    target_lengths,
    source_lengths,
    self_project,
    self_output,
    cross_query,
    cross_source,
    cross_output,
    feed_in,
    feed_out,
    norm_gain,
    norm_bias,
):
    micro = tokens.shape[0]
    rows = tokens.shape[2]
    model = tokens.shape[3]
    source_rows = encoded.shape[2]
    place = lax.axis_index("ctx")
    group = lax.axis_size("ctx")
    pack_total = rows * group
    source_total = source_rows * group
    self_width = math.gcd(pack_total, 512)
    cross_width = math.gcd(source_total, 512)
    results = []
    grad_values_all = []
    grad_encoded_all = []
    totals = ()
    for index in range(micro):
        attention_part = (
            lax.all_gather(self_project, "fsdp", axis=0, tiled=True),
            lax.all_gather(self_output, "fsdp", axis=0, tiled=True),
            lax.all_gather(cross_query, "fsdp", axis=0, tiled=True),
            lax.all_gather(cross_source, "fsdp", axis=0, tiled=True),
            lax.all_gather(cross_output, "fsdp", axis=0, tiled=True),
            lax.all_gather(norm_gain, "fsdp", axis=1, tiled=True),
            lax.all_gather(norm_bias, "fsdp", axis=1, tiled=True),
        )
        feed_part = (
            lax.all_gather(feed_in, "fsdp", axis=0, tiled=True),
            lax.all_gather(feed_out, "fsdp", axis=0, tiled=True),
        )
        weights = tuple(attention_part) + tuple(feed_part)
        (
            self_in_full,
            self_out_full,
            cross_query_full,
            cross_source_full,
            cross_out_full,
            gain_full,
            bias_full,
            feed_in_full,
            feed_out_full,
        ) = weights
        gains = gain_full.astype(jnp.float32)
        biases = bias_full.astype(jnp.float32)
        values = tokens[index, 0].astype(jnp.float32)
        source = encoded[index, 0]
        grad_out = cotangent[index, 0]
        places = order[index, 0]
        target_docs = docs_of(places, target_lengths[index, 0])
        query_places = lax.dynamic_slice_in_dim(places, place * rows, rows)
        query_docs = lax.dynamic_slice_in_dim(target_docs, place * rows, rows)
        source_docs = docs_of(jnp.arange(source_total, dtype=jnp.int32), source_lengths[index, 0])

        def self_allowed(start, count):
            key_docs = lax.dynamic_slice_in_dim(target_docs, start, count)
            key_places = lax.dynamic_slice_in_dim(places, start, count)
            return (query_docs[:, None] == key_docs[None, :]) & (
                key_places[None, :] <= query_places[:, None]
            )

        def cross_allowed(start, count):
            return (
                query_docs[:, None] == lax.dynamic_slice_in_dim(source_docs, start, count)[None, :]
            )

        first = norm_apply(values, gains[0], biases[0]).astype(jnp.bfloat16)
        query = jnp.dot(first, self_in_full[:, :model], preferred_element_type=jnp.float32).astype(
            jnp.bfloat16
        )
        local_pairs = jnp.dot(
            first, self_in_full[:, model:], preferred_element_type=jnp.float32
        ).astype(jnp.bfloat16)
        self_pairs = lax.all_gather(local_pairs, "ctx", axis=0, tiled=True)
        self_total = log_mass(query, self_pairs, self_allowed, self_width)
        self_mixed = attend_forward(query, self_pairs, self_allowed, self_width, self_total)
        after_self = values + jnp.dot(self_mixed, self_out_full, preferred_element_type=jnp.float32)
        second = norm_apply(after_self, gains[1], biases[1]).astype(jnp.bfloat16)
        cross_queries = jnp.dot(
            second, cross_query_full, preferred_element_type=jnp.float32
        ).astype(jnp.bfloat16)
        cross_local = jnp.dot(source, cross_source_full, preferred_element_type=jnp.float32).astype(
            jnp.bfloat16
        )
        cross_pairs = lax.all_gather(cross_local, "ctx", axis=0, tiled=True)
        cross_total = log_mass(cross_queries, cross_pairs, cross_allowed, cross_width)
        cross_mixed = attend_forward(
            cross_queries, cross_pairs, cross_allowed, cross_width, cross_total
        )
        after_cross = after_self + jnp.dot(
            cross_mixed, cross_out_full, preferred_element_type=jnp.float32
        )
        third = norm_apply(after_cross, gains[2], biases[2]).astype(jnp.bfloat16)
        hidden = jnp.dot(third, feed_in_full, preferred_element_type=jnp.float32)
        active = gelu_exact(hidden).astype(jnp.bfloat16)
        result = (
            after_cross + jnp.dot(active, feed_out_full, preferred_element_type=jnp.float32)
        ).astype(jnp.bfloat16)
        grad_feed_out = jnp.einsum(
            "rf,rd->fd", active, grad_out, preferred_element_type=jnp.float32
        )
        grad_active = jnp.einsum(
            "rd,fd->rf", grad_out, feed_out_full, preferred_element_type=jnp.float32
        ).astype(jnp.bfloat16)
        _, gelu_pull = jax.vjp(gelu_exact, hidden)
        grad_hidden = gelu_pull(grad_active.astype(jnp.float32))[0].astype(jnp.bfloat16)
        grad_feed_in = jnp.einsum(
            "rd,rf->df", third, grad_hidden, preferred_element_type=jnp.float32
        )
        grad_third = jnp.einsum(
            "rf,df->rd", grad_hidden, feed_in_full, preferred_element_type=jnp.float32
        )
        _, norm_pull = jax.vjp(norm_apply, after_cross, gains[2], biases[2])
        norm_part, gain_two, bias_two = norm_pull(grad_third)
        grad_after_cross = grad_out.astype(jnp.float32) + norm_part
        cross_branch = grad_after_cross.astype(jnp.bfloat16)
        grad_cross_output = jnp.einsum(
            "rd,re->de", cross_mixed, cross_branch, preferred_element_type=jnp.float32
        )
        grad_cross_mixed = jnp.einsum(
            "re,de->rd", cross_branch, cross_out_full, preferred_element_type=jnp.float32
        ).astype(jnp.bfloat16)
        cross_delta = attend_delta(
            cross_queries, cross_pairs, cross_allowed, grad_cross_mixed, cross_total, cross_width
        )
        grad_cross_queries = attend_query_grad(
            cross_queries,
            cross_pairs,
            cross_allowed,
            grad_cross_mixed,
            cross_total,
            cross_delta,
            cross_width,
        )
        grad_source = lax.psum_scatter(
            key_terms(
                cross_queries,
                cross_pairs,
                cross_allowed,
                grad_cross_mixed,
                cross_total,
                cross_delta,
                cross_width,
                source_rows * lax.axis_size("ctx"),
            ).astype(jnp.bfloat16),
            "ctx",
            scatter_dimension=0,
            tiled=True,
        )
        grad_cross_source = jnp.einsum(
            "sd,se->de", source, grad_source, preferred_element_type=jnp.float32
        )
        grad_encoded = jnp.einsum(
            "se,de->sd", grad_source, cross_source_full, preferred_element_type=jnp.float32
        ).astype(jnp.bfloat16)
        grad_cross_query = jnp.einsum(
            "rd,re->de", second, grad_cross_queries, preferred_element_type=jnp.float32
        )
        grad_second = jnp.einsum(
            "re,de->rd", grad_cross_queries, cross_query_full, preferred_element_type=jnp.float32
        )
        _, norm_pull = jax.vjp(norm_apply, after_self, gains[1], biases[1])
        norm_part, gain_one, bias_one = norm_pull(grad_second)
        grad_after_self = grad_after_cross + norm_part
        self_branch = grad_after_self.astype(jnp.bfloat16)
        grad_self_output = jnp.einsum(
            "rd,re->de", self_mixed, self_branch, preferred_element_type=jnp.float32
        )
        grad_self_mixed = jnp.einsum(
            "re,de->rd", self_branch, self_out_full, preferred_element_type=jnp.float32
        ).astype(jnp.bfloat16)
        self_delta = attend_delta(
            query, self_pairs, self_allowed, grad_self_mixed, self_total, self_width
        )
        grad_query = attend_query_grad(
            query, self_pairs, self_allowed, grad_self_mixed, self_total, self_delta, self_width
        )
        grad_pairs = lax.psum_scatter(
            key_terms(
                query,
                self_pairs,
                self_allowed,
                grad_self_mixed,
                self_total,
                self_delta,
                self_width,
                rows * lax.axis_size("ctx"),
            ).astype(jnp.bfloat16),
            "ctx",
            scatter_dimension=0,
            tiled=True,
        )
        grad_projected = jnp.concatenate([grad_query, grad_pairs], axis=1)
        grad_self_project = jnp.einsum(
            "rd,re->de", first, grad_projected, preferred_element_type=jnp.float32
        )
        grad_first = jnp.einsum(
            "re,de->rd", grad_projected, self_in_full, preferred_element_type=jnp.float32
        )
        _, norm_pull = jax.vjp(norm_apply, values, gains[0], biases[0])
        norm_part, gain_zero, bias_zero = norm_pull(grad_first)
        grad_values = (grad_after_self + norm_part).astype(jnp.bfloat16)
        grads = (
            grad_self_project,
            grad_self_output,
            grad_cross_query,
            grad_cross_source,
            grad_cross_output,
            grad_feed_in,
            grad_feed_out,
            jnp.stack([gain_zero, gain_one, gain_two]),
            jnp.stack([bias_zero, bias_one, bias_two]),
        )
        result, grad_values, grad_encoded, grads = (result, grad_values, grad_encoded, grads)
        totals = (
            grads
            if index == 0
            else tuple((jnp.add(left, right) for left, right in zip(totals, grads)))
        )
        results.append(result)
        grad_values_all.append(grad_values)
        grad_encoded_all.append(grad_encoded)
    shares = (
        lax.psum_scatter(
            totals[0].astype(jnp.bfloat16), "fsdp", scatter_dimension=0, tiled=True
        ).astype(jnp.float32),
        lax.psum_scatter(
            totals[1].astype(jnp.bfloat16), "fsdp", scatter_dimension=0, tiled=True
        ).astype(jnp.float32),
        lax.psum_scatter(
            totals[2].astype(jnp.bfloat16), "fsdp", scatter_dimension=0, tiled=True
        ).astype(jnp.float32),
        lax.psum_scatter(
            totals[3].astype(jnp.bfloat16), "fsdp", scatter_dimension=0, tiled=True
        ).astype(jnp.float32),
        lax.psum_scatter(
            totals[4].astype(jnp.bfloat16), "fsdp", scatter_dimension=0, tiled=True
        ).astype(jnp.float32),
        lax.psum_scatter(
            totals[5].astype(jnp.bfloat16), "fsdp", scatter_dimension=0, tiled=True
        ).astype(jnp.float32),
        lax.psum_scatter(
            totals[6].astype(jnp.bfloat16), "fsdp", scatter_dimension=0, tiled=True
        ).astype(jnp.float32),
        lax.psum_scatter(
            totals[7].astype(jnp.bfloat16), "fsdp", scatter_dimension=1, tiled=True
        ).astype(jnp.float32),
        lax.psum_scatter(
            totals[8].astype(jnp.bfloat16), "fsdp", scatter_dimension=1, tiled=True
        ).astype(jnp.float32),
    )
    totals = tuple(
        jax.tree.map(lambda part: part.astype(jnp.float32), lax.psum(as_sent(tuple(shares)), "ctx"))
    )
    output = jnp.stack(results)[:, None]
    grad_tokens = jnp.stack(grad_values_all)[:, None]
    grad_source_rows = jnp.stack(grad_encoded_all)[:, None]
    return (
        output,
        grad_tokens,
        grad_source_rows,
        totals[0],
        totals[1],
        totals[2],
        totals[3],
        totals[4],
        totals[5],
        totals[6],
        totals[7],
        totals[8][:2],
        totals[8][2],
    )


def solution(mesh):
    return jax.shard_map(
        body,
        mesh=mesh,
        in_specs=(
            P(None, "fsdp", "ctx", None),
            P(None, "fsdp", "ctx", None),
            P(None, "fsdp", "ctx", None),
            P(None, "fsdp", None),
            P(None, "fsdp", None),
            P(None, "fsdp", None),
            P("fsdp", None),
            P("fsdp", None),
            P("fsdp", None),
            P("fsdp", None),
            P("fsdp", None),
            P("fsdp", None),
            P("fsdp", None),
            P(None, "fsdp"),
            P(None, "fsdp"),
        ),
        out_specs=(
            P(None, "fsdp", "ctx", None),
            P(None, "fsdp", "ctx", None),
            P(None, "fsdp", "ctx", None),
            P("fsdp", None),
            P("fsdp", None),
            P("fsdp", None),
            P("fsdp", None),
            P("fsdp", None),
            P("fsdp", None),
            P("fsdp", None),
            P(None, "fsdp"),
            P(None, "fsdp"),
            P("fsdp"),
        ),
        check_vma=False,
    )
```

profile of v0, /device:TPU:0, one launch (start us, length us, event | category | flops | bytes accessed | tf_op | source)
XLA Modules:
  0.0 2653.8 jit_solution(12585363505498472861)
XLA Ops:
  8.7 54.8 %all-gather.20.cloned.1.call-done = bf16[1024,2048]{1,0:T(8,128)(2,1)} async-done(((bf16[64,2048]{1,0:T(8,128)(2,1)}), bf16[1024,2048]{1,0:T(8,128)(2,1)}) %all-gather.20.cloned.1.call-update) | async-done | bytes 4194320 | tf_op jit(solution)/shard_map/all_gather | solution.py:199
  76.3 18.7 all-gather
  95.2 17.9 all-gather.1
  161.5 21.8 all-gather.22.cloned.1.call-done
  189.7 52.3 %all-gather.34.cloned.1.call-done = bf16[1024,2048]{1,0:T(8,128)(2,1)} async-done(((bf16[512,2048]{1,0:T(8,128)(2,1)}), bf16[1024,2048]{1,0:T(8,128)(2,1)}) %all-gather.34.cloned.1.call-update) | async-done | bytes 4194320 | tf_op jit(solution)/shard_map/all_gather | solution.py:261
  248.5 75.4 %all-gather.16.cloned.1.call-done = bf16[1536,2048]{1,0:T(8,128)(2,1)} async-done(((bf16[768,2048]{1,0:T(8,128)(2,1)}), bf16[1536,2048]{1,0:T(8,128)(2,1)}) %all-gather.16.cloned.1.call-update) | async-done | bytes 6291472 | tf_op jit(solution)/shard_map/all_gather | solution.py:250
  332.5 70.6 %while.288 = (s32[]{:T(128)}, f32[16,768]{1,0:T(8,128)S(1)}, f32[16,768]{1,0:T(8,128)S(1)}, s32[768]{0:T(1024)S(1)}, s32[1536]{0:T(1024)S(1)}, /*index=5*/s32[15...) while((s32[]{:T(128)}, f32[16,768]{1,0:T(8,128)S(1)}, ...), condition=%wide.region_7.8_spmd.clone, body=%wide.region_4.0_spmd.clone.sunk | while | flops 850587648 | bytes 56887488 | solution.py:69
  403.2 41.9 %while.289 = (s32[]{:T(128)}, f32[768,16,64]{0,2,1:T(8,128)}, bf16[1536,2048]{0,1:T(8,128)(2,1)}, s32[768]{0:T(1024)S(1)}, s32[1536]{0:T(1024)S(1)}, /*index=5*/...) while((s32[]{:T(128)}, f32[768,16,64]{0,2,1:T(8,128)}, ...), condition=%wide.region_9.10_spmd.clone, body=%wide.region_8.9_spmd.clone.sunk | while | flops 1638531072 | bytes 15010009 | solution.py:83
  462.9 46.4 %while.290 = (s32[]{:T(128)}, f32[16,768]{1,0:T(8,128)S(1)}, f32[16,768]{1,0:T(8,128)S(1)}, s32[768]{0:T(1024)S(1)}, s32[1024]{0:T(1024)S(1)}, /*index=5*/bf16[1...) while((s32[]{:T(128)}, f32[16,768]{1,0:T(8,128)S(1)}, ...), condition=%wide.region_17.18_spmd.clone, body=%wide.region_14.0_spmd.clone.sunk | while | flops 849801216 | bytes 56878252 | solution.py:69
  509.4 27.3 %while.291 = (s32[]{:T(128)}, f32[768,16,64]{0,2,1:T(8,128)}, bf16[1024,2048]{0,1:T(8,128)(2,1)}, s32[768]{0:T(1024)S(1)}, s32[1024]{0:T(1024)S(1)}, /*index=5*/...) while((s32[]{:T(128)}, f32[768,16,64]{0,2,1:T(8,128)}, ...), condition=%wide.region_19.20_spmd.clone, body=%wide.region_18.19_spmd.clone.sunk | while | flops 1637744640 | bytes 15000773 | solution.py:83
  557.7 75.6 %while.292 = (s32[]{:T(128)}, f32[16,768]{1,0:T(8,128)S(1)}, f32[16,768]{1,0:T(8,128)S(1)}, s32[768]{0:T(1024)S(1)}, s32[1536]{0:T(1024)}, /*index=5*/s32[1536]{...) while((s32[]{:T(128)}, f32[16,768]{1,0:T(8,128)S(1)}, ...), condition=%wide.region_29.30_spmd.clone, body=%wide.region_26.29_spmd.clone.sunk | while | flops 850587648 | bytes 56887488 | solution.py:69
  633.3 45.7 %while.293 = (s32[]{:T(128)}, f32[768,16,64]{0,2,1:T(8,128)}, bf16[1536,2048]{0,1:T(8,128)(2,1)}, s32[768]{0:T(1024)S(1)}, s32[1536]{0:T(1024)}, /*index=5*/s32[...) while((s32[]{:T(128)}, f32[768,16,64]{0,2,1:T(8,128)}, ...), condition=%wide.region_31.32_spmd.clone, body=%wide.region_30.31_spmd.clone.sunk | while | flops 1638531072 | bytes 15010009 | solution.py:83
  693.8 46.2 %while.294 = (s32[]{:T(128)}, f32[16,768]{1,0:T(8,128)S(1)}, f32[16,768]{1,0:T(8,128)S(1)}, s32[768]{0:T(1024)S(1)}, s32[1024]{0:T(1024)S(1)}, /*index=5*/bf16[1...) while((s32[]{:T(128)}, f32[16,768]{1,0:T(8,128)S(1)}, ...), condition=%wide.region_39.40_spmd.clone, body=%wide.region_36.39_spmd.clone.sunk | while | flops 849801216 | bytes 56878252 | solution.py:69
  740.1 27.6 %while.295 = (s32[]{:T(128)}, f32[768,16,64]{0,2,1:T(8,128)}, bf16[1024,2048]{0,1:T(8,128)(2,1)}, s32[768]{0:T(1024)S(1)}, s32[1024]{0:T(1024)S(1)}, /*index=5*/...) while((s32[]{:T(128)}, f32[768,16,64]{0,2,1:T(8,128)}, ...), condition=%wide.region_41.42_spmd.clone, body=%wide.region_40.41_spmd.clone.sunk | while | flops 1637744640 | bytes 15000773 | solution.py:83
  777.8 38.4 %multiply_convert_fusion.1 = (bf16[768,4096]{1,0:T(8,128)(2,1)}, f32[768,4096]{1,0:T(8,128)}, f32[768,4096]{1,0:T(8,128)}) fusion(bf16[1024,4096]{1,0:T(8,128)(2,1)} %all-gather.28.cloned.1.call-done, f32[768,1024]{1,0:T(8,128)S(1)} %copy-done.21, f32[1024]{0:T(1024)S(1)} %bitcast.1215, f32[1024]{0:T(1024)S(1)} %bitcast.1209, f32[768]{0:T(1024)S(1)} %copy-done.134, ...), kind=kOutput, calls=%fused_computation.278 | convolution fusion | flops 6650855424 | bytes 43005952 | tf_op jit(solution)/shard_map/dot_general | solution.py:270
  816.2 36.8 %multiply_convert_fusion = (bf16[768,4096]{1,0:T(8,128)(2,1)}, f32[768,4096]{1,0:T(8,128)}, f32[768,4096]{1,0:T(8,128)}) fusion(bf16[1024,4096]{1,0:T(8,128)(2,1)S(1)} %copy-done.222, f32[768,1024]{1,0:T(8,128)S(1)} %copy-done.44, f32[768]{0:T(1024)S(1)} %fusion.306, f32[768]{0:T(1024)S(1)} %broadcast_multiply_fusion, f32[1024]{0:T(1024)S(1)} %bitcast.1216, ...), kind=kOutput, calls=%fused_computation.265 | convolution fusion | flops 6650855424 | bytes 43005952 | tf_op jit(solution)/shard_map/dot_general | solution.py:270
  853.0 19.8 fusion.204
  872.8 12.3 fusion.359
  885.2 19.9 fusion.197
  905.1 15.6 multiply_reduce_fusion.2
  935.4 48.4 %while.296 = (s32[]{:T(128)}, f32[16,768]{1,0:T(8,128)S(1)}, s32[768]{0:T(1024)S(1)}, s32[1024]{0:T(1024)S(1)}, bf16[1024,2048]{0,1:T(8,128)(2,1)}, /*index=5*/b...) while((s32[]{:T(128)}, f32[16,768]{1,0:T(8,128)S(1)}, ...), condition=%wide.region_48.49_spmd.clone, body=%wide.region_46.48_spmd.clone.sunk | while | flops 1642475520 | bytes 67101928 | solution.py:111
  983.8 59.8 %while.297 = (s32[]{:T(128)}, f32[768,16,64]{0,2,1:T(8,128)}, bf16[1024,2048]{0,1:T(8,128)(2,1)}, s32[768]{0:T(1024)S(1)}, s32[1024]{0:T(1024)S(1)}, /*index=5*/...) while((s32[]{:T(128)}, f32[768,16,64]{0,2,1:T(8,128)}, ...), condition=%wide.region_50.51_spmd.clone, body=%wide.region_49.50_spmd.clone.sunk | while | flops 2455633920 | bytes 68003032 | solution.py:131
  997.3 16.3 bitcast_add_fusion.20
  1026.9 16.7 bitcast_add_fusion.20
  1053.4 48.6 %while.300 = (s32[]{:T(128)}, f32[16,768]{1,0:T(8,128)S(1)}, s32[768]{0:T(1024)S(1)}, s32[1024]{0:T(1024)S(1)}, bf16[1024,2048]{0,1:T(8,128)(2,1)}, /*index=5*/b...) while((s32[]{:T(128)}, f32[16,768]{1,0:T(8,128)S(1)}, ...), condition=%wide.region_67.68_spmd.clone, body=%wide.region_65.67_spmd.clone.sunk | while | flops 1642475520 | bytes 67101928 | solution.py:111
  1102.0 60.0 %while.301 = (s32[]{:T(128)}, f32[768,16,64]{0,2,1:T(8,128)}, bf16[1024,2048]{0,1:T(8,128)(2,1)}, s32[768]{0:T(1024)S(1)}, s32[1024]{0:T(1024)S(1)}, /*index=5*/...) while((s32[]{:T(128)}, f32[768,16,64]{0,2,1:T(8,128)}, ...), condition=%wide.region_69.70_spmd.clone, body=%wide.region_68.69_spmd.clone.sunk | while | flops 2455633920 | bytes 68003032 | solution.py:131
  1115.3 16.3 bitcast_add_fusion.22
  1144.9 16.7 bitcast_add_fusion.22
  1186.9 77.2 %while.298 = (s32[]{:T(128)}, f32[16,768]{1,0:T(8,128)S(1)}, s32[768]{0:T(1024)S(1)}, s32[1536]{0:T(1024)}, s32[1536]{0:T(1024)}, /*index=5*/s32[768]{0:T(1024)S...) while((s32[]{:T(128)}, f32[16,768]{1,0:T(8,128)S(1)}, ...), condition=%wide.region_55.56_spmd.clone, body=%wide.region_53.55_spmd.clone.sunk | while | flops 1643261952 | bytes 67111160 | solution.py:111
  1267.1 131.3 %while.284 = (s32[]{:T(128)}, bf16[1536,2048]{0,1:T(8,128)(2,1)}, s32[768]{0:T(1024)S(1)}, s32[1536]{0:T(1024)}, s32[1536]{0:T(1024)}, /*index=5*/s32[768]{0:T(1...) while((s32[]{:T(128)}, bf16[1536,2048]{0,1:T(8,128)(2,1)}, ...), condition=%wide.region_59.60_spmd, body=%wide.region_58.59_spmd.sunk | while | flops 3290562560 | bytes 95717608 | solution.py:160
  1282.0 15.9 fusion.647
  1325.8 15.9 fusion.647
  1369.4 15.9 fusion.647
  1409.8 84.2 %while.286 = (s32[]{:T(128)}, bf16[1024,2048]{0,1:T(8,128)(2,1)}, s32[768]{0:T(1024)S(1)}, s32[1024]{0:T(1024)S(1)}, bf16[1024,2048]{0,1:T(8,128)(2,1)}, /*index...) while((s32[]{:T(128)}, bf16[1024,2048]{0,1:T(8,128)(2,1)}, ...), condition=%wide.region_83.84_spmd, body=%wide.region_82.83_spmd.sunk | while | flops 3289776128 | bytes 99902696 | solution.py:160
  1422.6 16.4 fusion.671
  1464.4 16.4 fusion.671
  1496.7 84.4 %while.287 = (s32[]{:T(128)}, bf16[1024,2048]{0,1:T(8,128)(2,1)}, s32[768]{0:T(1024)S(1)}, s32[1024]{0:T(1024)S(1)}, bf16[1024,2048]{0,1:T(8,128)(2,1)}, /*index...) while((s32[]{:T(128)}, bf16[1024,2048]{0,1:T(8,128)(2,1)}, ...), condition=%wide.region_86.87_spmd, body=%wide.region_85.86_spmd.sunk | while | flops 3289776128 | bytes 99902696 | solution.py:160
  1509.2 16.5 fusion.683
  1551.5 16.5 fusion.683
  1582.6 77.6 %while.302 = (s32[]{:T(128)}, f32[16,768]{1,0:T(8,128)S(1)}, s32[768]{0:T(1024)S(1)}, s32[1536]{0:T(1024)}, s32[1536]{0:T(1024)}, /*index=5*/s32[768]{0:T(1024)S...) while((s32[]{:T(128)}, f32[16,768]{1,0:T(8,128)S(1)}, ...), condition=%wide.region_74.75_spmd.clone, body=%wide.region_72.74_spmd.clone.sunk | while | flops 1643261952 | bytes 67111160 | solution.py:111
  1663.2 132.2 %while.285 = (s32[]{:T(128)}, bf16[1536,2048]{0,1:T(8,128)(2,1)}, s32[768]{0:T(1024)S(1)}, s32[1536]{0:T(1024)}, s32[1536]{0:T(1024)}, /*index=5*/s32[768]{0:T(1...) while((s32[]{:T(128)}, bf16[1536,2048]{0,1:T(8,128)(2,1)}, ...), condition=%wide.region_78.79_spmd, body=%wide.region_77.78_spmd.sunk | while | flops 3290562560 | bytes 95717608 | solution.py:160
  1678.5 16.0 fusion.659
  1722.9 15.8 fusion.659
  1766.5 15.8 fusion.659
  1841.7 13.6 fusion.314
  1855.2 14.7 add_convert_fusion.1
  1871.3 95.8 %while.299 = (s32[]{:T(128)}, f32[768,16,64]{0,2,1:T(8,128)}, bf16[1536,2048]{0,1:T(8,128)(2,1)}, s32[768]{0:T(1024)S(1)}, s32[1536]{0:T(1024)}, /*index=5*/s32[...) while((s32[]{:T(128)}, f32[768,16,64]{0,2,1:T(8,128)}, ...), condition=%wide.region_57.58_spmd.clone, body=%wide.region_56.57_spmd.clone.sunk | while | flops 2456420352 | bytes 68012264 | solution.py:131
  1886.5 16.9 bitcast_add_fusion.21
  1918.7 16.9 bitcast_add_fusion.21
  1950.5 16.7 bitcast_add_fusion.21
  1970.7 13.4 fusion.274
  1984.1 12.9 add_convert_fusion
  1998.4 94.5 %while.303 = (s32[]{:T(128)}, f32[768,16,64]{0,2,1:T(8,128)}, bf16[1536,2048]{0,1:T(8,128)(2,1)}, s32[768]{0:T(1024)S(1)}, s32[1536]{0:T(1024)}, /*index=5*/s32[...) while((s32[]{:T(128)}, f32[768,16,64]{0,2,1:T(8,128)}, ...), condition=%wide.region_76.77_spmd.clone, body=%wide.region_75.76_spmd.clone.sunk | while | flops 2456420352 | bytes 68012264 | solution.py:131
  2013.4 16.2 bitcast_add_fusion.23
  2044.7 16.6 bitcast_add_fusion.23
  2076.2 16.7 bitcast_add_fusion.23
  2096.7 12.7 fusion.256
  2121.2 12.1 fusion.277
  2177.1 73.8 %reduce-scatter.36.cloned.1.call-done = bf16[64,4096]{1,0:T(8,128)(2,1)} async-done(((bf16[1024,4096]{1,0:T(8,128)(2,1)}), bf16[64,4096]{1,0:T(8,128)(2,1)}) %reduce-scatter.36.cloned.1.call-update) | async-done | bytes 524304 | tf_op jit(solution)/shard_map/reduce_scatter | solution.py:415
  2250.8 108.5 %reduce-scatter.38.cloned.1.call-done = bf16[256,1024]{1,0:T(8,128)(2,1)} async-done(((bf16[4096,1024]{1,0:T(8,128)(2,1)}), bf16[256,1024]{1,0:T(8,128)(2,1)}) %reduce-scatter.38.cloned.1.call-update) | async-done | bytes 524304 | tf_op jit(solution)/shard_map/reduce_scatter | solution.py:418
  2359.3 88.9 %reduce-scatter.28.cloned.1.call-done = bf16[64,3072]{1,0:T(8,128)(2,1)} async-done(((bf16[1024,3072]{1,0:T(8,128)(2,1)}), bf16[64,3072]{1,0:T(8,128)(2,1)}) %reduce-scatter.28.cloned.1.call-update) | async-done | bytes 393232 | tf_op jit(solution)/shard_map/reduce_scatter | solution.py:400
  2460.8 46.5 %reduce-scatter.44.cloned.1.call-done = bf16[64,3]{1,0:T(8,128)(2,1)} async-done(((bf16[1024,3]{1,0:T(8,128)(2,1)}), bf16[64,3]{1,0:T(8,128)(2,1)}) %reduce-scatter.44.cloned.1.call-update) | async-done | bytes 400
  2508.1 58.0 %reduce-scatter.42.cloned.1.call-done = bf16[64,3]{1,0:T(8,128)(2,1)} async-done(((bf16[1024,3]{1,0:T(8,128)(2,1)}), bf16[64,3]{1,0:T(8,128)(2,1)}) %reduce-scatter.42.cloned.1.call-update) | async-done | bytes 400
  2573.5 64.9 %all-reduce.4.cloned.1.call-done = (bf16[64,2048]{0,1:T(8,128)(2,1)}, bf16[64,3072]{1,0:T(8,128)(2,1)}, bf16[64,1024]{1,0:T(8,128)(2,1)}, bf16[64,1024]{1,0:T(8,...) async-done(((bf16[64,2048]{0,1:T(8,128)(2,1)}, bf16[64,3072]{1,0:T(8,128)(2,1)}, bf16[64,1024]{1,0:T(8,128)(2,1)}, ...) | async-done | bytes 2097168 | tf_op jit(solution)/shard_map/psum | solution.py:429
  (1022 shorter events, 1400.7 us)
Async XLA Ops:
  7.2 56.3 %all-gather.20.cloned.1.call-start = ((), (), s32[]{:S(2)}) async-start(), calls=%async_computation.16 | async-start | bytes 4456448 | tf_op jit(solution)/shard_map/all_gather | solution.py:199
  7.9 118.5 %all-gather.14.cloned.1.call-start = ((), (), s32[]{:S(2)}) async-start(), calls=%async_computation.13 | async-start | bytes 6684672 | tf_op jit(solution)/shard_map/all_gather | solution.py:196
  8.7 174.7 %all-gather.22.cloned.1.call-start = ((), (), s32[]{:S(2)}) async-start(), calls=%async_computation.17 | async-start | bytes 6291456 | tf_op jit(solution)/shard_map/all_gather | solution.py:261
  69.6 25.5 copy-start.219
  69.7 172.4 %all-gather.34.cloned.1.call-start = ((), (), s32[]{:S(2)}) async-start(), calls=%async_computation.23 | async-start | bytes 6291456 | tf_op jit(solution)/shard_map/all_gather | solution.py:261
  69.7 43.4 %copy-start.17 = (bf16[2,1,768,1024]{3,2,1,0:T(8,128)(2,1)S(1)}, bf16[2,1,768,1024]{3,2,1,0:T(8,128)(2,1)}, u32[]{:S(2)}) copy-start(bf16[2,1,768,1024]{3,2,1,0:T(8,128)(2,1)} %param.55) | copy-start | bytes 9437188
  76.3 247.6 %all-gather.16.cloned.1.call-start = ((), (), s32[]{:S(2)}) async-start(), calls=%async_computation.14 | async-start | bytes 9437184 | tf_op jit(solution)/shard_map/all_gather | solution.py:250
  113.6 35.8 %copy-start.144 = (f32[768]{0:T(1024)}, f32[768]{0:T(1024)S(1)}, u32[]{:S(2)}) copy-start(f32[768]{0:T(1024)S(1)} %get-tuple-element.5045) | copy-start | bytes 9220
  113.6 42.3 %copy-start.142 = (f32[768]{0:T(1024)}, f32[768]{0:T(1024)S(1)}, u32[]{:S(2)}) copy-start(f32[768]{0:T(1024)S(1)} %get-tuple-element.5044) | copy-start | bytes 9220
  114.6 19.1 copy-start.166
  114.6 21.2 copy-start.168
  114.6 34.8 %copy-start.178 = (f32[768]{0:T(1024)}, f32[768]{0:T(1024)S(1)}, u32[]{:S(2)}) copy-start(f32[768]{0:T(1024)S(1)} %fusion.301) | copy-start | bytes 9220
  115.2 40.7 %copy-start.182 = (f32[1,1024]{1,0:T(1,128)}, f32[1,1024]{1,0:T(1,128)S(1)}, u32[]{:S(2)}) copy-start(f32[1,1024]{1,0:T(1,128)S(1)} %get-tuple-element.5011) | copy-start | bytes 12292
  115.8 40.1 %copy-start.205 = (f32[1,1024]{1,0:T(1,128)}, f32[1,1024]{1,0:T(1,128)S(1)}, u32[]{:S(2)}) copy-start(f32[1,1024]{1,0:T(1,128)S(1)} %get-tuple-element.5014) | copy-start | bytes 12292
  133.7 314.7 %all-gather.18.cloned.1.call-start = ((), (), s32[]{:S(2)}) async-start(), calls=%async_computation.15 | async-start | bytes 2228224 | tf_op jit(solution)/shard_map/all_gather | solution.py:197
  134.3 321.0 %all-gather.24.cloned.1.call-start = ((), (), s32[]{:S(2)}) async-start(), calls=%async_computation.18 | async-start | bytes 2228224 | tf_op jit(solution)/shard_map/all_gather | solution.py:198
  135.0 405.5 %all-gather.26.cloned.1.call-start = ((), (), s32[]{:S(2)}) async-start(), calls=%async_computation.19 | async-start | bytes 2228224 | tf_op jit(solution)/shard_map/all_gather | solution.py:200
  135.8 413.1 %all-gather.32.cloned.1.call-start = ((), (), s32[]{:S(2)}) async-start(), calls=%async_computation.22 | async-start | bytes 9437184 | tf_op jit(solution)/shard_map/all_gather | solution.py:250
  135.9 20.1 copy-start.180
  143.5 633.9 %all-gather.28.cloned.1.call-start = ((), (), s32[]{:S(2)}) async-start(), calls=%async_computation.20 | async-start | bytes 8912896 | tf_op jit(solution)/shard_map/all_gather | solution.py:205
  144.1 708.9 %all-gather.30.cloned.1.call-start = ((), (), s32[]{:S(2)}) async-start(), calls=%async_computation.21 | async-start | bytes 8912896 | tf_op jit(solution)/shard_map/all_gather | solution.py:206
  144.8 1652.3 %reduce-scatter.24.cloned.1.call-start = ((), (), s32[]{:S(2)}) async-start(), calls=%async_computation.26 | async-start | bytes 6291456 | tf_op jit(solution)/shard_map/reduce_scatter | solution.py:311
  774.8 146.0 %copy-start.190 = (f32[768]{0:T(1024)}, f32[768]{0:T(1024)S(1)}, u32[]{:S(2)}) copy-start(f32[768]{0:T(1024)S(1)} %broadcast_multiply_fusion) | copy-start | bytes 9220
  777.4 143.3 %copy-start.198 = (f32[768]{0:T(1024)}, f32[768]{0:T(1024)S(1)}, u32[]{:S(2)}) copy-start(f32[768]{0:T(1024)S(1)} %fusion.306) | copy-start | bytes 9220
  777.8 38.4 %copy-start.44 = (f32[768,1024]{1,0:T(8,128)S(1)}, f32[768,1024]{1,0:T(8,128)}, u32[]{:S(2)}) copy-start(f32[768,1024]{1,0:T(8,128)} %copy-done.43) | copy-start | bytes 9437188
  777.8 38.4 %copy-start.222 = (bf16[1024,4096]{1,0:T(8,128)(2,1)S(1)}, bf16[1024,4096]{1,0:T(8,128)(2,1)}, u32[]{:S(2)}) copy-start(bf16[1024,4096]{1,0:T(8,128)(2,1)} %all-gather.28.cloned.1.call-done) | copy-start | bytes 25165828
  905.1 15.7 copy-start.177
  905.1 15.7 copy-start.175
  905.1 15.7 copy-start.45
  905.1 15.7 copy-start.68
  937.1 10.6 copy-start.83
  961.3 10.6 copy-start.83
  1055.4 10.6 copy-start.84
  1079.6 10.6 copy-start.84
  1190.5 10.3 copy-start.81
  1439.0 11.6 copy-start.27
  1480.8 11.6 copy-start.27
  1494.1 310.8 %reduce-scatter.26.cloned.1.call-start = ((), (), s32[]{:S(2)}) async-start(), calls=%async_computation.27 | async-start | bytes 6291456 | tf_op jit(solution)/shard_map/reduce_scatter | solution.py:311
  1525.8 11.8 copy-start.28
  1568.0 11.6 copy-start.28
  1581.2 515.4 %reduce-scatter.20.cloned.1.call-start = ((), (), s32[]{:S(2)}) async-start(), calls=%async_computation.24 | async-start | bytes 9437184 | tf_op jit(solution)/shard_map/reduce_scatter | solution.py:354
  1586.2 10.3 copy-start.82
  1612.1 10.4 copy-start.82
  1660.2 449.2 %reduce-scatter.22.cloned.1.call-start = ((), (), s32[]{:S(2)}) async-start(), calls=%async_computation.25 | async-start | bytes 9437184 | tf_op jit(solution)/shard_map/reduce_scatter | solution.py:354
  1796.6 378.5 %reduce-scatter.40.cloned.1.call-start = ((), (), s32[]{:S(2)}) async-start(), calls=%async_computation.34 | async-start | bytes 4456448
  1820.1 357.0 %reduce-scatter.34.cloned.1.call-start = ((), (), s32[]{:S(2)}) async-start(), calls=%async_computation.31 | async-start | bytes 2228224 | tf_op jit(solution)/shard_map/reduce_scatter | solution.py:412
  1827.2 349.9 %reduce-scatter.32.cloned.1.call-start = ((), (), s32[]{:S(2)}) async-start(), calls=%async_computation.30 | async-start | bytes 2228224 | tf_op jit(solution)/shard_map/reduce_scatter | solution.py:406
  1834.7 342.4 %reduce-scatter.30.cloned.1.call-start = ((), (), s32[]{:S(2)}) async-start(), calls=%async_computation.29 | async-start | bytes 2228224 | tf_op jit(solution)/shard_map/reduce_scatter | solution.py:403
  1841.5 13.7 copy-start.191
  1841.5 13.7 copy-start.199
  1841.6 409.3 %reduce-scatter.36.cloned.1.call-start = ((), (), s32[]{:S(2)}) async-start(), calls=%async_computation.32 | async-start | bytes 8912896 | tf_op jit(solution)/shard_map/reduce_scatter | solution.py:415
  1841.7 13.6 copy-start.46
  1870.0 489.4 %reduce-scatter.38.cloned.1.call-start = ((), (), s32[]{:S(2)}) async-start(), calls=%async_computation.33 | async-start | bytes 8912896 | tf_op jit(solution)/shard_map/reduce_scatter | solution.py:418
  1967.1 16.9 slice-start.2
  1970.7 13.4 slice-start.3
  1997.1 451.2 %reduce-scatter.28.cloned.1.call-start = ((), (), s32[]{:S(2)}) async-start(), calls=%async_computation.28 | async-start | bytes 6684672 | tf_op jit(solution)/shard_map/reduce_scatter | solution.py:400
  2096.6 12.7 copy-start.143
  2096.7 12.7 copy-start.181
  2121.2 386.2 %reduce-scatter.44.cloned.1.call-start = ((), (), s32[]{:S(2)}) async-start(), calls=%async_computation.36 | async-start | bytes 278528
  2121.2 12.1 copy-start.47
  2121.2 25.2 slice-start
  2133.4 13.1 slice-start.1
  2162.2 403.9 %reduce-scatter.42.cloned.1.call-start = ((), (), s32[]{:S(2)}) async-start(), calls=%async_computation.35 | async-start | bytes 278528
  2168.8 469.5 %all-reduce.4.cloned.1.call-start = ((), (), s32[]{:S(2)}) async-start(), calls=%async_computation.37 | async-start | bytes 4718592 | tf_op jit(solution)/shard_map/psum | solution.py:429
  (204 other events, 813.0 us)
Sparse Core Ops, SparseCore 0:
  10.2 53.2 all-gather.19
  65.7 60.5 all-gather.13
  127.9 55.3 all-gather.21
  185.3 56.7 all-gather.33
  243.5 80.3 all-gather.15
  325.9 41.3 all-gather.17
  369.5 40.1 all-gather.23
  411.8 40.1 all-gather.25
  454.2 79.1 all-gather.31
  535.4 74.8 all-gather.27
  612.4 73.1 all-gather.29
  1494.1 54.3 reduce-scatter.23
  1581.3 54.6 reduce-scatter.25
  1660.3 77.4 reduce-scatter.19
  1795.6 77.1 reduce-scatter.21
  1876.5 72.3 reduce-scatter.39
  1952.9 60.6 reduce-scatter.33
  2017.2 60.5 reduce-scatter.31
  2082.7 60.5 reduce-scatter.29
  2147.1 103.6 reduce-scatter.35
  2254.9 104.3 reduce-scatter.37
  2363.3 84.9 reduce-scatter.27
  2452.7 54.5 reduce-scatter.43
  2511.7 54.3 reduce-scatter.41
  2569.6 68.7 all-reduce.3
where the time goes:
time: 2670 us; the launch traced here: 2650 us
  matrix products  1470 us (55%)
  waiting for transfers between devices  660 us (25%)
  local copies, waits for them, and re-layouts  252 us (9%)
  other arithmetic  206 us (8%)
  blocking collectives  41.5 us (2%)
    dot_general x40, matrix products, block_scores(): jnp.einsum('qhd,khd->hqk', split_heads(query), split_heads(block[:, :mode...  415 us
    dot_general x10, matrix products, step(): jnp.einsum('hqk,khd->qhd', grad_scores, split_heads(block[:, :model]), pr...  166 us
    dot_general x10, matrix products, step(): jnp.einsum('hqk,qhd->khd', grad_scores, split_heads(query), preferred_ele...  161 us
    dot_general x10, matrix products, score_grads(): jnp.einsum('qhd,khd->hqk', split_heads(grad_mixed), split_heads(block[:,...  118 us
    dot_general x10, matrix products, step(): jnp.einsum('hqk,qhd->khd', probs.astype(jnp.bfloat16), split_heads(grad_m...  116 us
    reduce_sum x10, other arithmetic, step(): jnp.sum(jnp.exp(scores - new_peak[:, :, None]), axis=2)  110 us
    unnamed x28, waiting for transfers between devices  109 us
    reduce_scatter x1, waiting for transfers between devices, body(): lax.psum_scatter(totals[6].astype(jnp.bfloat16), 'fsdp', scatter_dimensio...  108 us
  transfers between devices with their start and end apart: 25, of which 11 were waited for; matrix products, arithmetic and copies ran while one was open for 47% of the time, Pallas kernels for 0%

commit v1 on v0

--- a/solution.py
+++ b/solution.py
@@ -1,8 +1,11 @@
+import functools
 import math
 
 import jax
 import jax.numpy as jnp
 from jax import lax
+from jax.experimental import pallas as pl
+from jax.experimental.pallas import tpu as pltpu
 from jax.sharding import PartitionSpec as P
 
 HEAD = 64
@@ -448,9 +451,943 @@
     )
 
 
+BIG = 1e30
+SCALE2 = HEAD ** (-0.5) * math.log2(math.e)
+NT = (((1,), (1,)), ((), ()))
+TN = (((0,), (0,)), ((), ()))
+NN = (((1,), (0,)), ((), ()))
+
+
+def dot(left, right, dims=NN):
+    return lax.dot_general(left, right, dims, preferred_element_type=jnp.float32)
+
+
+def lanes(rows):
+    return lax.broadcasted_iota(jnp.int32, (rows, 128), 1)
+
+
+def parts(x):
+    hi = x.astype(jnp.bfloat16)
+    rest = x - hi.astype(jnp.float32)
+    mid = rest.astype(jnp.bfloat16)
+    lo = (rest - mid.astype(jnp.float32)).astype(jnp.bfloat16)
+    return (hi, mid, lo)
+
+
+def spread(x, base):
+    hi, mid, lo = parts(x)
+    lane = lanes(x.shape[0]) % HEAD
+    return jnp.where(lane == 4, hi, jnp.where(lane == 5, mid, jnp.where(lane == 6, lo, base)))
+
+
+def beyond(size, flip):
+    row = lax.broadcasted_iota(jnp.int32, (size, size), 0)
+    column = lax.broadcasted_iota(jnp.int32, (size, size), 1)
+    return row > column if flip else column > row
+
+
+def two_heads(ref, own, other):
+    left = lanes(own.shape[0]) < HEAD
+    ref[0] = jnp.where(left, own, other)
+    ref[1] = jnp.where(left, other, own)
+
+
+def attend_kernel(plan, q_ref, k_ref, v_ref, qd_ref, kd_ref, out_ref, extra_ref, keys, values):
+    two_heads(keys, k_ref[...], kd_ref[...])
+    two_heads(values, v_ref[...], jnp.ones_like(v_ref))
+    for q0, q1, k0, k1, diagonal in plan:
+        rows, width = (q1 - q0, k1 - k0)
+        left = lanes(rows) < HEAD
+        q, qd = (q_ref[q0:q1], qd_ref[q0:q1])
+        scores = []
+        for h in range(2):
+            s = dot(jnp.where(left == (h == 0), q, qd), keys[h, k0:k1], NT)
+            if diagonal:
+                tail = jnp.where(beyond(rows, False), -BIG, s[:, width - rows :])
+                s = tail if width == rows else jnp.concatenate([s[:, : width - rows], tail], axis=1)
+            scores.append(s)
+        mixed, tops = ([], [])
+        for h in range(2):
+            top = jnp.max(scores[h], axis=1, keepdims=True)
+            probs = jnp.exp2((scores[h] - top) * SCALE2).astype(jnp.bfloat16)
+            mixed.append(dot(probs, values[h, k0:k1]))
+            tops.append(top)
+        mass = jnp.where(left, mixed[1], mixed[0])
+        numer = jnp.where(left, mixed[0], mixed[1])
+        out_ref[q0:q1] = (numer / pltpu.roll(mass, HEAD, 1)).astype(jnp.bfloat16)
+        top = jnp.where(left, tops[1], tops[0])
+        extra_ref[q0:q1] = spread(-(top + HEAD**0.5 * jnp.log(mass)), qd)
+
+
+def attend_back_kernel(
+    plan,
+    q_ref,
+    k_ref,
+    v_ref,
+    extra_ref,
+    kd_ref,
+    out_ref,
+    g_ref,
+    *refs,
+):
+    *outs, keys, values, queries, grads, total = refs
+    if len(outs) == 1:
+        dq_ref, dk_ref, dv_ref = (outs[0].at[i] for i in range(3))
+    else:
+        dq_ref, dk_ref, dv_ref = (outs[0], outs[1].at[0], outs[1].at[1])
+    two_heads(keys, k_ref[...], kd_ref[...])
+    two_heads(values, v_ref[...], jnp.ones_like(v_ref))
+    two_heads(queries, q_ref[...], extra_ref[...])
+    square = (128, 128)
+    row, column = (lax.broadcasted_iota(jnp.int32, square, axis) < HEAD for axis in (0, 1))
+    swap = jnp.where(row != column, 1.0, 0.0).astype(jnp.bfloat16)
+    g = g_ref[...]
+    terms = parts(g.astype(jnp.float32) * out_ref[...].astype(jnp.float32))
+    delta = sum(dot(term, swap) for term in terms)
+    two_heads(grads, g, spread(-delta, jnp.zeros_like(g)))
+    total[...] = jnp.zeros_like(total)
+    for k0, k1, q0, q1, diagonal in plan:
+        rows = k1 - k0
+        left = lanes(rows) < HEAD
+        dks, dvs = ([], [])
+        for h in range(2):
+            s = dot(keys[h, k0:k1], queries[h, q0:q1], NT)
+            if diagonal:
+                head = jnp.where(beyond(rows, True), -BIG, s[:, :rows])
+                s = head if q1 - q0 == rows else jnp.concatenate([head, s[:, rows:]], axis=1)
+            probs = jnp.exp2(s * SCALE2)
+            ds = probs * dot(values[h, k0:k1], grads[h, q0:q1], NT)
+            ds = ds.astype(jnp.bfloat16)
+            dvs.append(dot(probs.astype(jnp.bfloat16), g_ref[q0:q1]))
+            dks.append(dot(ds, q_ref[q0:q1]))
+            total[h, q0:q1] += dot(ds, k_ref[k0:k1], TN)
+        dk_ref[k0:k1] = (jnp.where(left, dks[0], dks[1]) * HEAD ** (-0.5)).astype(jnp.bfloat16)
+        dv_ref[k0:k1] = jnp.where(left, dvs[0], dvs[1]).astype(jnp.bfloat16)
+    left = lanes(total.shape[1]) < HEAD
+    dq_ref[...] = (jnp.where(left, total[0], total[1]) * HEAD ** (-0.5)).astype(jnp.bfloat16)
+
+
+def pair_of_heads(rows):
+    return pl.BlockSpec((rows, 128), lambda i: (0, i))
+
+
+def all_of(rows):
+    return pl.BlockSpec((rows, 128), lambda i: (0, 0))
+
+
+def plan_cost(plan, model, products):
+    area = sum((q1 - q0) * (k1 - k0) for q0, q1, k0, k1, _ in plan) * model
+    return pl.CostEstimate(
+        flops=8 * area * products, bytes_accessed=1 << 24, transcendentals=area // HEAD
+    )
+
+
+def attend(plan, q, k, v, qd, kd):
+    nq, nk, model = (q.shape[0], k.shape[0], q.shape[1])
+    shape = jax.ShapeDtypeStruct((nq, model), jnp.bfloat16)
+    return pl.pallas_call(
+        functools.partial(attend_kernel, plan),
+        grid=(model // 128,),
+        in_specs=[pair_of_heads(n) for n in (nq, nk, nk)] + [all_of(nq), all_of(nk)],
+        out_specs=[pair_of_heads(nq)] * 2,
+        out_shape=[shape] * 2,
+        scratch_shapes=[pltpu.VMEM((2, nk, 128), jnp.bfloat16)] * 2,
+        compiler_params=pltpu.CompilerParams(vmem_limit_bytes=48 * 2**20),
+        cost_estimate=plan_cost(plan, model, 2),
+    )(q, k, v, qd, kd)
+
+
+def stacked(count, rows):
+    return pl.BlockSpec((count, rows, 128), lambda i: (0, 0, i))
+
+
+def attend_back(plan, q, k, v, extra, kd, out, g, together):
+    nq, nk, model = (q.shape[0], k.shape[0], q.shape[1])
+    if together:
+        specs, shapes = ([stacked(3, nq)], [(3, nq, model)])
+    else:
+        specs, shapes = ([pair_of_heads(nq), stacked(2, nk)], [(nq, model), (2, nk, model)])
+    outs = pl.pallas_call(
+        functools.partial(attend_back_kernel, plan),
+        grid=(model // 128,),
+        in_specs=[pair_of_heads(n) for n in (nq, nk, nk, nq)]
+        + [all_of(nk)]
+        + [pair_of_heads(nq)] * 2,
+        out_specs=specs,
+        out_shape=[jax.ShapeDtypeStruct(shape, jnp.bfloat16) for shape in shapes],
+        scratch_shapes=[pltpu.VMEM((2, nk, 128), jnp.bfloat16)] * 2
+        + [pltpu.VMEM((2, nq, 128), jnp.bfloat16)] * 2
+        + [pltpu.VMEM((2, nq, 128), jnp.float32)],
+        compiler_params=pltpu.CompilerParams(vmem_limit_bytes=48 * 2**20),
+        cost_estimate=plan_cost(plan, model, 5),
+    )(q, k, v, extra, kd, out, g)
+    return outs[0] if together else outs
+
+
+def self_plan(first, total, tile, back):
+    plan = []
+    for low, high in ((0, first), (first, total)):
+        for start in range(low, high, tile):
+            end = start + tile
+            plan.append((start, end, start, high, True) if back else (start, end, low, end, True))
+    return plan
+
+
+def cross_plan(first, total, reach, source, tile, back):
+    if back:
+        return [
+            (start, start + tile, 0 if start < reach else first, total, False)
+            for start in range(0, source, tile)
+        ]
+    return [
+        (start, start + tile, 0, reach if start < first else source, False)
+        for start in range(0, total, tile)
+    ]
+
+
+def query_marks(docs):
+    lane = jnp.arange(128) % HEAD
+    return jnp.where(docs[:, None] == lane[None, :], BIG, 0.0).astype(jnp.bfloat16)
+
+
+def key_marks(docs, count):
+    lane = (jnp.arange(128) % HEAD)[None, :]
+    other = jnp.where(docs[:, None] == lane, 0.0, -1.0)
+    return jnp.where(lane < count, other, jnp.where(lane < 7, 1.0, 0.0)).astype(jnp.bfloat16)
+
+
+MODEL = 1024
+TILE = 512
+
+
+def wide(values):
+    return values.astype(jnp.float32)
+
+
+def short(values):
+    return values.astype(jnp.bfloat16)
+
+
+def gathered(ref):
+    return ref[...].reshape(-1, ref.shape[-1])
+
+
+def once(shape, index):
+    return pl.BlockSpec(shape, index, pipeline_mode=pl.Buffered(1))
+
+
+def weight_at(slot):
+    return once((16, 64, MODEL), lambda *_: (0, slot, 0))
+
+
+def norm_rows():
+    return once((8, MODEL), lambda *_: (0, 0))
+
+
+def by_rows(count, width=MODEL):
+    return pl.BlockSpec((count, width), lambda i, *_: (i, 0))
+
+
+def found_rows(count):
+    return pl.BlockSpec((count, MODEL), lambda i, held: (held[i], 0))
+
+
+def sums_out():
+    return pl.BlockSpec((8, MODEL), lambda *_: (0, 0))
+
+
+def struct(shape, kind):
+    return jax.ShapeDtypeStruct(shape, kind)
+
+
+def spread_of(values):
+    mean = jnp.mean(values, axis=-1, keepdims=True)
+    centred = values - mean
+    scale = lax.rsqrt(jnp.mean(centred * centred, axis=-1, keepdims=True) + 1e-05)
+    return (centred * scale, scale)
+
+
+def norm_of(values, norm_ref, k):
+    hat, _ = spread_of(values)
+    return short(hat * norm_ref[k : k + 1] + norm_ref[3 + k : 4 + k])
+
+
+def norm_back(values, grad, norm_ref, k, sums_ref):
+    hat, scale = spread_of(values)
+    each = grad * norm_ref[k : k + 1]
+    inner = each - jnp.mean(each, axis=-1, keepdims=True)
+    inner = inner - hat * jnp.mean(each * hat, axis=-1, keepdims=True)
+
+    @pl.when(pl.program_id(0) == 0)
+    def _():
+        sums_ref[...] = jnp.zeros_like(sums_ref)
+
+    sums_ref[0:1] += jnp.sum(grad * hat, axis=0, keepdims=True)
+    sums_ref[1:2] += jnp.sum(grad, axis=0, keepdims=True)
+    return scale * inner
+
+
+def call(kernel, grid, in_specs, out_specs, out_shape, flops, scratch=(), prefetch=0, aliases=None):
+    return pl.pallas_call(
+        kernel,
+        grid_spec=pltpu.PrefetchScalarGridSpec(
+            num_scalar_prefetch=prefetch,
+            grid=grid,
+            in_specs=in_specs,
+            out_specs=out_specs,
+            scratch_shapes=list(scratch),
+        ),
+        out_shape=out_shape,
+        input_output_aliases=aliases or {},
+        compiler_params=pltpu.CompilerParams(vmem_limit_bytes=58 * 2**20),
+        cost_estimate=pl.CostEstimate(flops=flops, bytes_accessed=1 << 24, transcendentals=0),
+    )
+
+
+def pack_kernel(*refs):
+    attention_ref, feed_ref = refs[-2:]
+    self_in, self_out, cross_q, cross_s, cross_out, feed_in, feed_out, norms = refs[:-2]
+    rows = self_in.shape[0]
+    slot = 0
+    for ref in (self_in, self_out, cross_q, cross_s, cross_out):
+        for start in range(0, ref.shape[1], MODEL):
+            attention_ref[slot * rows : (slot + 1) * rows] = ref[:, start : start + MODEL]
+            slot += 1
+    attention_ref[slot * rows :] = norms[...]
+    piece = feed_out.shape[0] // 2
+    for lot in range(2):
+        for owner in range(16):
+            column = (2 * owner + lot) * piece
+            slot, spot = (2 * lot + owner // 8, owner % 8 * piece)
+            feed_ref[slot * rows : (slot + 1) * rows, spot : spot + piece] = feed_in[
+                :, column : column + piece
+            ]
+    feed_ref[4 * rows : 8 * rows] = feed_out[...]
+    feed_ref[8 * rows :] = jnp.zeros_like(norms)
+
+
+def pack(weights, norms):
+    arrays = tuple(weights) + (norms,)
+    out = struct((528, MODEL), jnp.bfloat16)
+    return call(
+        pack_kernel,
+        (1,),
+        [once(a.shape, lambda i: (0, 0)) for a in arrays],
+        [once(out.shape, lambda i: (0, 0))] * 2,
+        [out] * 2,
+        1 << 20,
+    )(*arrays)
+
+
+def enter_kernel(held, tokens_ref, norm_ref, wq, wk, wv, first_ref, q_ref, k_ref, v_ref):
+    first = norm_of(wide(tokens_ref[...]), norm_ref, 0)
+    first_ref[...] = first
+    for weight, out in ((wq, q_ref), (wk, k_ref), (wv, v_ref)):
+        out[...] = short(dot(first, gathered(weight)))
+
+
+def enter(held, tokens, norms, weights, width):
+    shape = struct(tokens.shape, jnp.bfloat16)
+    return call(
+        enter_kernel,
+        (tokens.shape[0] // width,),
+        [found_rows(width), norm_rows()] + [weight_at(i) for i in range(3)],
+        [by_rows(width)] * 4,
+        [shape] * 4,
+        6 * tokens.size * MODEL,
+        prefetch=1,
+    )(held, tokens, norms, weights, weights, weights)
+
+
+def source_kernel(source_ref, wk, wv, k_ref, v_ref):
+    source = source_ref[...]
+    k_ref[...] = short(dot(source, gathered(wk)))
+    v_ref[...] = short(dot(source, gathered(wv)))
+
+
+def source_pairs(source, weights, width):
+    return call(
+        source_kernel,
+        (source.shape[0] // width,),
+        [by_rows(width), weight_at(5), weight_at(6)],
+        [by_rows(width)] * 2,
+        [struct(source.shape, jnp.bfloat16)] * 2,
+        4 * source.size * MODEL,
+    )(source, weights, weights)
+
+
+def between_kernel(held, mixed_ref, tokens_ref, norm_ref, wo, wq, after_ref, second_ref, q_ref):
+    after = wide(tokens_ref[...]) + dot(mixed_ref[...], gathered(wo))
+    after_ref[...] = after
+    second = norm_of(after, norm_ref, 1)
+    second_ref[...] = second
+    q_ref[...] = short(dot(second, gathered(wq)))
+
+
+def between(held, mixed, tokens, norms, weights, width):
+    return call(
+        between_kernel,
+        (mixed.shape[0] // width,),
+        [by_rows(width), found_rows(width), norm_rows(), weight_at(3), weight_at(4)],
+        [by_rows(width)] * 3,
+        [struct(mixed.shape, kind) for kind in (jnp.float32, jnp.bfloat16, jnp.bfloat16)],
+        4 * mixed.size * MODEL,
+        prefetch=1,
+    )(held, mixed, tokens, norms, weights, weights)
+
+
+def before_feed_kernel(mixed_ref, base_ref, norm_ref, wo, after_ref, third_ref):
+    after = base_ref[...] + dot(mixed_ref[...], gathered(wo))
+    after_ref[...] = after
+    third_ref[...] = norm_of(after, norm_ref, 2)
+
+
+def before_feed(mixed, base, norms, weights, width):
+    return call(
+        before_feed_kernel,
+        (mixed.shape[0] // width,),
+        [by_rows(width), by_rows(width), norm_rows(), weight_at(7)],
+        [by_rows(width)] * 2,
+        [struct(mixed.shape, kind) for kind in (jnp.float32, jnp.bfloat16)],
+        2 * mixed.size * MODEL,
+    )(mixed, base, norms, weights)
+
+
+def gelu_terms(hidden):
+    bell = jnp.exp2(hidden * hidden * (-0.5 * math.log2(math.e)))
+    t = 1.0 / (1.0 + (0.3275911 / math.sqrt(2.0)) * jnp.abs(hidden))
+    series = 1.061405429
+    for term in (-1.453152027, 1.421413741, -0.284496736, 0.254829592):
+        series = series * t + term
+    tail = 0.5 * series * t * bell
+    return (jnp.where(hidden < 0, tail, 1.0 - tail), bell * (1.0 / math.sqrt(2.0 * math.pi)))
+
+
+def deal(place_ref, turned, keep_ref, send_ref, value, core, x, y, index, lead=()):
+    rel_x = jnp.bitwise_xor(place_ref[1], x)
+    rel_y = jnp.bitwise_xor(place_ref[2], y)
+    spot = (rel_y, rel_x) if turned else (rel_x, rel_y)
+
+    @pl.when(place_ref[0] == core)
+    def _():
+        keep_ref[spot + index] = value
+
+    @pl.when(place_ref[0] != core)
+    def _():
+        send_ref[spot + index] = value
+
+
+def feed_kernel(
+    turned,
+    place_ref,
+    third_ref,
+    grad_ref,
+    win_ref,
+    wout_ref,
+    out_ref,
+    back_ref,
+    keep_ref,
+    send_ref,
+    third_t,
+    active_ref,
+    hidden_ref,
+):
+    step = pl.program_id(0)
+
+    @pl.when(step == 0)
+    def _():
+        third_t[...] = third_ref[...].T
+        out_ref[...] = jnp.zeros_like(out_ref)
+        back_ref[...] = jnp.zeros_like(back_ref)
+
+    win, wout = (gathered(win_ref), gathered(wout_ref))
+    rows = third_ref.shape[0]
+    lots = [slice(start, start + TILE) for start in range(0, rows, TILE)]
+
+    def enter(lot):
+        return (dot(third_ref[lot], win), dot(grad_ref[lot], wout, NT))
+
+    def leave(lot, hidden, grad):
+        mass, bell = gelu_terms(hidden)
+        active = short(hidden * mass)
+        grad = short((mass + hidden * bell) * wide(short(grad)))
+        active_ref[lot] = active
+        hidden_ref[lot] = grad
+        out_ref[lot] += dot(active, wout)
+        back_ref[lot] += dot(grad, win, NT)
+
+    ready = enter(lots[0])
+    for index, lot in enumerate(lots):
+        following = enter(lots[index + 1]) if index + 1 < len(lots) else None
+        leave(lot, *ready)
+        ready = following
+    grad_out = short(dot(active_ref[...], grad_ref[...], TN))
+    grad_in = short(dot(third_t[...], hidden_ref[...]))
+    for owner in range(4):
+        for y in range(2):
+            start = owner * 128 + y * 64
+            for half in range(2):
+                value = grad_out[start + 32 * half : start + 32 * half + 32]
+                deal(
+                    place_ref, turned, keep_ref, send_ref, value,
+                    owner % 2, owner // 2, y, (step, 2 + half),
+                )
+    for owner in range(16):
+        for y in range(2):
+            start = owner * 64 + y * 32
+            for side in range(2):
+
+                @pl.when(step % 2 == side)
+                def _(start=start, owner=owner, y=y, side=side):
+                    deal(
+                        place_ref, turned, keep_ref, send_ref, grad_in[start : start + 32],
+                        owner % 2, owner // 2 % 2, y,
+                        (owner // 4, step // 2, slice(None), slice(side * TILE, side * TILE + TILE)),
+                    )
+
+
+def feed(place, third, grad, weights, lot, turned):
+    rows = third.shape[0]
+    full = struct((rows, MODEL), jnp.float32)
+    buffer = struct((2, 2, 4, 4, 32, MODEL), jnp.bfloat16)
+    return call(
+        functools.partial(feed_kernel, turned),
+        (4,),
+        [
+            once((rows, MODEL), lambda t, place: (0, 0)),
+            once((rows, MODEL), lambda t, place: (0, 0)),
+            pl.BlockSpec((16, 64, TILE), lambda t, place: (0, 2 * lot + t // 2, t % 2)),
+            pl.BlockSpec((4, 128, MODEL), lambda t, place: (t, 2 + lot, 0)),
+        ],
+        [once((rows, MODEL), lambda t, place: (0, 0))] * 2
+        + [once(buffer.shape, lambda t, place: (0, 0, 0, 0, 0, 0))] * 2,
+        [full, full, buffer, buffer],
+        12 * rows * MODEL * 2048,
+        scratch=[
+            pltpu.VMEM((MODEL, rows), jnp.bfloat16),
+            pltpu.VMEM((rows, TILE), jnp.bfloat16),
+            pltpu.VMEM((rows, TILE), jnp.bfloat16),
+        ],
+        prefetch=1,
+    )(place, third, grad, weights, weights)
+
+
+def after_feed_kernel(
+    held,
+    after_ref,
+    out_a,
+    out_b,
+    back_a,
+    back_b,
+    grad_ref,
+    norm_ref,
+    wo,
+    result_ref,
+    total_ref,
+    branch_ref,
+    mixed_ref,
+    sums_ref,
+):
+    after = after_ref[...]
+    result_ref[...] = short(after + out_a[...] + out_b[...])
+    part = norm_back(after, back_a[...] + back_b[...], norm_ref, 2, sums_ref)
+    total = wide(grad_ref[...]) + part
+    total_ref[...] = total
+    branch = short(total)
+    branch_ref[...] = branch
+    mixed_ref[...] = short(dot(branch, gathered(wo), NT))
+
+
+def after_feed(held, after, outs, backs, grad, norms, weights, width):
+    narrow = struct(after.shape, jnp.bfloat16)
+    return call(
+        after_feed_kernel,
+        (after.shape[0] // width,),
+        [by_rows(width)] * 6 + [norm_rows(), weight_at(7)],
+        [found_rows(width)] + [by_rows(width)] * 3 + [sums_out()],
+        [narrow, struct(after.shape, jnp.float32), narrow, narrow, struct((8, MODEL), jnp.float32)],
+        2 * after.size * MODEL,
+        prefetch=1,
+    )(held, after, *outs, *backs, grad, norms, weights)
+
+
+def middle_kernel(
+    grad_ref,
+    after_ref,
+    base_ref,
+    norm_ref,
+    wq,
+    wo,
+    total_ref,
+    branch_ref,
+    mixed_ref,
+    sums_ref,
+):
+    grad = dot(grad_ref[...], gathered(wq), NT)
+    total = base_ref[...] + norm_back(after_ref[...], grad, norm_ref, 1, sums_ref)
+    total_ref[...] = total
+    branch = short(total)
+    branch_ref[...] = branch
+    mixed_ref[...] = short(dot(branch, gathered(wo), NT))
+
+
+def middle(grad, after, base, norms, weights, width):
+    narrow = struct(after.shape, jnp.bfloat16)
+    return call(
+        middle_kernel,
+        (after.shape[0] // width,),
+        [by_rows(width)] * 3 + [norm_rows(), weight_at(4), weight_at(3)],
+        [by_rows(width)] * 3 + [sums_out()],
+        [struct(after.shape, jnp.float32), narrow, narrow, struct((8, MODEL), jnp.float32)],
+        4 * after.size * MODEL,
+    )(grad, after, base, norms, weights, weights)
+
+
+def finish_kernel(
+    held, grads_ref, tokens_ref, base_ref, norm_ref, wq, wk, wv, result_ref, sums_ref
+):
+    grad = sum(dot(grads_ref[i], gathered(w), NT) for i, w in enumerate((wq, wk, wv)))
+    part = norm_back(wide(tokens_ref[...]), grad, norm_ref, 0, sums_ref)
+    result_ref[...] = short(base_ref[...] + part)
+
+
+def finish(held, grads, tokens, base, norms, weights, width):
+    return call(
+        finish_kernel,
+        (base.shape[0] // width,),
+        [
+            pl.BlockSpec((3, width, MODEL), lambda i, held: (0, i, 0)),
+            found_rows(width),
+            by_rows(width),
+            norm_rows(),
+        ]
+        + [weight_at(i) for i in range(3)],
+        [found_rows(width), sums_out()],
+        [struct(base.shape, jnp.bfloat16), struct((8, MODEL), jnp.float32)],
+        6 * base.size * MODEL,
+        prefetch=1,
+    )(held, grads, tokens, base, norms, weights, weights, weights)
+
+
+def source_back_kernel(grads_ref, wk, wv, out_ref):
+    grad = dot(grads_ref[0], gathered(wk), NT) + dot(grads_ref[1], gathered(wv), NT)
+    out_ref[...] = short(grad)
+
+
+def source_back(grads, weights, width):
+    rows = grads.shape[1]
+    return call(
+        source_back_kernel,
+        (rows // width,),
+        [pl.BlockSpec((2, width, MODEL), lambda i: (0, i, 0)), weight_at(5), weight_at(6)],
+        [by_rows(width)],
+        [struct((rows, MODEL), jnp.bfloat16)],
+        4 * rows * MODEL * MODEL,
+    )(grads, weights, weights)[0]
+
+
+def weight_grad_kernel(turned, place_ref, left_ref, right_ref, *refs):
+    keep_ref, send_ref = refs[-2:]
+    right = right_ref[0] if len(right_ref.shape) == 3 else right_ref[...]
+    product = short(dot(left_ref[...], right, TN))
+    for owner in range(TILE // 64):
+        for y in range(2):
+            start = owner * 64 + y * 32
+            deal(
+                place_ref, turned, keep_ref, send_ref, product[start : start + 32],
+                owner % 2, owner // 2 % 2, y, (owner // 4, 0),
+            )
+
+
+def weight_grad(place, left, right, turned, held=None, slot=0, slots=1):
+    rows = left.shape[0]
+    several = right.ndim == 3
+    count = right.shape[0] if several else 1
+    shape = struct((2, 2, 4, slots, 32, MODEL), jnp.bfloat16)
+    held = () if held is None else tuple(held)
+    return call(
+        functools.partial(weight_grad_kernel, turned),
+        (count, MODEL // TILE),
+        [
+            pl.BlockSpec((rows, TILE), lambda n, t, place: (0, t)),
+            pl.BlockSpec((1, rows, MODEL), lambda n, t, place: (n, 0, 0))
+            if several
+            else pl.BlockSpec((rows, MODEL), lambda n, t, place: (0, 0)),
+        ]
+        + [pl.BlockSpec(memory_space=pl.ANY)] * len(held),
+        [pl.BlockSpec((2, 2, 2, 1, 32, MODEL), lambda n, t, place: (0, 0, t, slot + n, 0, 0))] * 2,
+        [shape] * 2,
+        2 * rows * MODEL * MODEL * count,
+        prefetch=1,
+        aliases={3 + i: i for i in range(len(held))},
+    )(place, left, right, *held)
+
+
+def pairs(bit):
+    return [(i, i ^ bit) for i in range(16)]
+
+
+def swap(values):
+    return lax.ppermute(values, "ctx", [(0, 1), (1, 0)])
+
+
+def reduce_to_owner(keep, send, turned, z):
+    def over_x(values):
+        return lax.ppermute(values, "fsdp", pairs(2))
+
+    one, two = (swap, over_x) if turned else (over_x, swap)
+    core = lax.ppermute(send, "fsdp", pairs(1))
+    first = short(wide(keep[1]) + wide(core[1]))
+    first = yield (first,)
+    first = one(first[0])
+    second = short(wide(keep[0, 1]) + wide(core[0, 1]) + wide(first[1]))
+    second = yield (second,)
+    second = two(second[0])
+
+    def share(index):
+        terms = (keep[0, 0], core[0, 0], first[0], second)
+        return sum(wide(lax.dynamic_index_in_dim(term, index, 0, False)) for term in terms)
+
+    away = yield tuple(short(share((z + hop) % 4)) for hop in range(1, 4))
+    total = share(z)
+    for hop, values in enumerate(away, 1):
+        cycle = [(i, (i + 4 * hop) % 16) for i in range(16)]
+        total = total + wide(lax.ppermute(values, "fsdp", cycle))
+    (total,) = yield (short(total),)
+    other = swap(total)
+    low = lax.axis_index("ctx") == 0
+    yield (
+        wide(jnp.stack([jnp.where(low, total, other), jnp.where(low, other, total)], axis=1)),
+    )
+
+
+class Steps:
+    def __init__(self, steps):
+        self.steps = steps
+        self.held = next(steps)
+
+    def advance(self):
+        self.held = self.steps.send(self.held)
+
+
+def before(value, *transfers):
+    flat = tuple(item for transfer in transfers for item in transfer.held)
+    value, *flat = lax.optimization_barrier((value,) + flat)
+    for transfer in transfers:
+        count = len(transfer.held)
+        transfer.held, flat = (tuple(flat[:count]), flat[count:])
+    return value
+
+
+def columns(shares, start, stop):
+    part = shares[start:stop].reshape(stop - start, -1, MODEL)
+    return jnp.concatenate(list(part), axis=1)
+
+
+def feed_shares(lots):
+    inner = [lot[:2].reshape(2, 64, 8, 128).transpose(1, 0, 2, 3).reshape(64, 16, 128) for lot in lots]
+    inner = jnp.stack(inner, axis=2).reshape(64, 4 * MODEL)
+    outer = [lot[2:].transpose(1, 0, 2, 3).reshape(128, MODEL) for lot in lots]
+    return inner, jnp.concatenate(outer)
+
+
+def after_all(value, *others):
+    return lax.optimization_barrier((value,) + others)[0]
+
+
+def whole_packs(mesh):
+    return mesh.shape["ctx"] == 2 and mesh.shape["fsdp"] == 16
+
+
+def whole_pack_body(
+    tokens,
+    encoded,
+    cotangent,
+    order,
+    target_lengths,
+    source_lengths,
+    self_project,
+    self_output,
+    cross_query,
+    cross_source,
+    cross_output,
+    feed_in,
+    feed_out,
+    norm_gain,
+    norm_bias,
+):
+    rows = tokens.shape[2]
+    pack_rows, source_rows = (2 * rows, 2 * encoded.shape[2])
+    first_rows = 3 * pack_rows // 4
+    width = rows // 2
+    mine = lax.axis_index("ctx")
+    spot = lax.axis_index("fsdp")
+    z = spot // 4
+    place = jnp.stack([spot % 2, spot // 2 % 2, mine]).astype(jnp.int32)
+    part = self_project.shape[0]
+
+    norms = jnp.pad(jnp.concatenate([norm_gain, norm_bias]), ((0, 10), (0, MODEL - part)))
+    attention_shard, feed_shard = pack(
+        (self_project, self_output, cross_query, cross_source, cross_output, feed_in, feed_out),
+        norms,
+    )
+    weights = lax.all_gather(attention_shard, "fsdp", axis=0)
+    norms = wide(weights[:, 8 * part : 8 * part + 8, :part])
+    norms = norms.transpose(1, 0, 2).reshape(8, MODEL)
+
+    def both_halves(array):
+        own = lax.dynamic_index_in_dim(array, mine, 0, False)[0]
+        return own, swap(lax.dynamic_index_in_dim(array, 1 - mine, 0, False)[0])
+
+    places = lax.dynamic_index_in_dim(order, mine, 0, False)[0]
+    holds = places[::width] // width
+    found = jnp.argsort(holds).astype(jnp.int32)
+    held = jnp.where(found // 2 == mine, found % 2, 2 + found % 2)
+
+    def from_both(own, other):
+        low = mine == 0
+        return jnp.stack([jnp.where(low, own, other), jnp.where(low, other, own)])[:, None]
+
+    def to_slots(halves):
+        return from_both(halves[:rows], swap(halves[rows:]))
+
+    halves = jnp.concatenate(both_halves(tokens))
+    own, other = both_halves(encoded)
+    source = jnp.concatenate([jnp.where(mine == 0, own, other), jnp.where(mine == 0, other, own)])
+    grad_out = jnp.concatenate(both_halves(cotangent))
+    feed_shard = after_all(feed_shard, halves, source, grad_out)
+    grad_out = jnp.concatenate(
+        [lax.dynamic_slice_in_dim(grad_out, held[p] * width, width) for p in range(4)]
+    )
+    feed_weights = lax.all_gather(feed_shard, "fsdp", axis=0)
+
+    lengths = lax.dynamic_index_in_dim(target_lengths, mine, 0, False)[0]
+    target_docs = docs_of(jnp.arange(pack_rows, dtype=jnp.int32), lengths)
+    lengths = lax.dynamic_index_in_dim(source_lengths, mine, 0, False)[0]
+    source_docs = docs_of(jnp.arange(source_rows, dtype=jnp.int32), lengths)
+    docs = lengths.shape[0]
+    marks = query_marks(target_docs)
+    target_marks = key_marks(target_docs, docs)
+    source_marks = key_marks(source_docs, docs)
+    reach = source_rows // 2
+
+    first, query, keys, values = enter(held, halves, norms, weights, width)
+    plan = self_plan(first_rows, pack_rows, width, False)
+    self_mixed, self_extra = attend(plan, query, keys, values, marks, target_marks)
+    cross_keys, cross_values = source_pairs(source, weights, source_rows // 2)
+    after_self, second, cross_queries = between(held, self_mixed, halves, norms, weights, width)
+    plan = cross_plan(first_rows, pack_rows, reach, source_rows, width, False)
+    cross_mixed, cross_extra = attend(
+        plan, cross_queries, cross_keys, cross_values, marks, source_marks
+    )
+    after_cross, third = before_feed(cross_mixed, after_self, norms, weights, width)
+
+    out_a, back_a, *sent = feed(place, third, grad_out, feed_weights, 0, False)
+    first_lot = Steps(reduce_to_owner(*sent, False, z))
+    out_b, back_b, *sent = feed(place, after_all(third, *sent), grad_out, feed_weights, 1, True)
+    second_lot = Steps(reduce_to_owner(*sent, True, z))
+    after_cross = before(after_cross, first_lot)
+    result, grad_after_cross, cross_branch, grad_cross_mixed, sums_two = after_feed(
+        held, after_cross, (out_a, out_b), (back_a, back_b), grad_out, norms, weights, width
+    )
+    result = to_slots(result)
+
+    first_lot.advance()
+    others = weight_grad(place, cross_mixed, cross_branch, False, slots=5)
+    grad_cross_mixed = before(after_all(grad_cross_mixed, *others), second_lot)
+    second_lot.advance()
+    plan = cross_plan(first_rows, pack_rows, reach, source_rows, source_rows // 4, True)
+    grad_cross_queries, grad_source = attend_back(
+        plan,
+        cross_queries,
+        cross_keys,
+        cross_values,
+        cross_extra,
+        source_marks,
+        cross_mixed,
+        grad_cross_mixed,
+        False,
+    )
+    grad_source = before(grad_source, first_lot, second_lot)
+    first_lot.advance()
+    second_lot.advance()
+    others = weight_grad(place, source, grad_source, False, others, 1, 5)
+    others = weight_grad(
+        place, second, after_all(grad_cross_queries, *others), False, others, 3, 5
+    )
+    grad_after_self, self_branch, grad_self_mixed, sums_one = middle(
+        grad_cross_queries, after_self, grad_after_cross, norms, weights, width
+    )
+    others = weight_grad(place, self_mixed, self_branch, False, others, 4, 5)
+    other_weights = Steps(reduce_to_owner(*others, False, z))
+    grad_encoded = source_back(after_all(grad_source, *others), weights, source_rows // 2)
+    grad_self_mixed = after_all(grad_self_mixed, grad_encoded)
+    grad_self_mixed = before(grad_self_mixed, first_lot, second_lot, other_weights)
+    low, high = (grad_encoded[:reach], grad_encoded[reach:])
+    grad_encoded = from_both(
+        jnp.where(mine == 0, low, high), swap(jnp.where(mine == 0, high, low))
+    )
+    first_lot.advance()
+    second_lot.advance()
+    other_weights.advance()
+    plan = self_plan(first_rows, pack_rows, width, True)
+    grads = attend_back(
+        plan,
+        query,
+        keys,
+        values,
+        self_extra,
+        target_marks,
+        self_mixed,
+        grad_self_mixed,
+        True,
+    )
+    grads = before(grads, first_lot, second_lot, other_weights)
+    first_lot.advance()
+    second_lot.advance()
+    other_weights.advance()
+    project = weight_grad(place, first, grads, True, slots=3)
+    last = Steps(reduce_to_owner(*project, True, z))
+    feed_in_grad, feed_out_grad = feed_shares((first_lot.held[0], second_lot.held[0]))
+    grads = before(after_all(grads, feed_in_grad, feed_out_grad), last)
+    last.advance()
+    grad_tokens, sums_zero = finish(
+        held, grads, halves, grad_after_self, norms, weights, width
+    )
+    grad_tokens = to_slots(grad_tokens)
+
+    sums = jnp.concatenate([sums_zero[:2], sums_one[:2], sums_two[:2]])
+    for bit in (1, 2, 4, 8):
+        sums = sums + lax.ppermute(sums, "fsdp", pairs(bit))
+    sums = sums + swap(sums)
+    sums = lax.dynamic_slice_in_dim(sums, spot * part, part, 1)
+    for _ in range(2):
+        other_weights.advance()
+    for _ in range(3):
+        last.advance()
+    others_share, project_share = (other_weights.held[0], last.held[0])
+
+    return (
+        result,
+        grad_tokens,
+        grad_encoded,
+        columns(project_share, 0, 3),
+        columns(others_share, 4, 5),
+        columns(others_share, 3, 4),
+        columns(others_share, 1, 3),
+        columns(others_share, 0, 1),
+        feed_in_grad,
+        feed_out_grad,
+        sums[0::2],
+        sums[1:4:2],
+        sums[5],
+    )
+
+
 def solution(mesh):
+    chosen = whole_pack_body if whole_packs(mesh) else body
     return jax.shard_map(
-        body,
+        chosen,
         mesh=mesh,
         in_specs=(
             P(None, "fsdp", "ctx", None),

time: 2670 us -> 864 us (0.32)
  matrix products: 1470 us -> 0 us
  waiting for transfers between devices: 660 us -> 173 us
  Pallas kernels: 0 us -> 474 us
  local copies, waits for them, and re-layouts: 252 us -> 46.3 us
  other arithmetic: 206 us -> 79.4 us
  starting transfers between devices: 1.8 us -> 65.1 us
  blocking collectives: 41.5 us -> 0 us
    dot_general x134 -> x0, matrix products: 1470 us -> none  [the longest x40 415 us: block_scores(): jnp.einsum('qhd,khd->hqk', split_heads(query), split_heads(block[:, :mode...]
    pallas_call x0 -> x20, Pallas kernels: none -> 474 us  [the longest x2 132 us: feed(): call(functools.partial(feed_kernel, turned), (4,), [once((rows, MODEL), l...]
    reduce_scatter x10 -> x0, waiting for transfers between devices: 271 us -> none  [the longest x1 108 us: body(): lax.psum_scatter(totals[6].astype(jnp.bfloat16), 'fsdp', scatter_dimensio...]
    all_gather x11 -> x2, waiting for transfers between devices: 215 us -> 0.01 us  [the longest x1 0.01 us: whole_pack_body(): feed_weights = lax.all_gather(feed_shard, 'fsdp', axis=0)]
    ppermute x0 -> x39, waiting for transfers between devices: none -> 173 us  [the longest x15 150 us: swap(): return lax.ppermute(values, 'ctx', [(0, 1), (1, 0)])]
    reduce_sum x19 -> x0, other arithmetic: 126 us -> none  [the longest x10 110 us: step(): jnp.sum(jnp.exp(scores - new_peak[:, :, None]), axis=2)]
    unnamed x28 -> x2, waiting for transfers between devices: 109 us -> 0.03 us
    unnamed x477 -> x46, local copies, waits for them, and re-layouts: 91.7 us -> 1.97 us
  transfers between devices with their start and end apart: 25 -> 41, of which waited for: 11 -> 15; matrix products, arithmetic and copies ran while one was open for 47% -> 13% of each run, Pallas kernels for 0% -> 44%
where the time goes in v1:
time: 864 us; the launch traced here: 856 us
  Pallas kernels  474 us (55%)
  waiting for transfers between devices  173 us (20%)
  other arithmetic  79.4 us (9%)
  starting transfers between devices  65.1 us (8%)
  local copies, waits for them, and re-layouts  46.3 us (5%)
  between operations  17.8 us (2%)
    ppermute x15, waiting for transfers between devices, swap(): return lax.ppermute(values, 'ctx', [(0, 1), (1, 0)])  150 us
    pallas_call x2, Pallas kernels, feed(): call(functools.partial(feed_kernel, turned), (4,), [once((rows, MODEL), l...  132 us
    pallas_call x2, Pallas kernels, attend_back(): pl.pallas_call(functools.partial(attend_back_kernel, plan), grid=(model /...  110 us
    pallas_call x2, Pallas kernels, attend(): pl.pallas_call(functools.partial(attend_kernel, plan), grid=(model // 128...  61.6 us
    pallas_call x5, Pallas kernels, weight_grad(): call(functools.partial(weight_grad_kernel, turned), (count, MODEL // TILE...  54.6 us
    convert_element_type x16, other arithmetic, short(): return values.astype(jnp.bfloat16)  45.5 us
    ppermute x12, starting transfers between devices, reduce_to_owner(): total = total + wide(lax.ppermute(values, 'fsdp', cycle))  41.8 us
    pallas_call x1, Pallas kernels, finish(): call(finish_kernel, (base.shape[0] // width,), [pl.BlockSpec((3, width, M...  20.5 us
  transfers between devices with their start and end apart: 41, of which 15 were waited for; matrix products, arithmetic and copies ran while one was open for 13% of the time, Pallas kernels for 44%

profile of v1, /device:TPU:0, one launch (start us, length us, event | category | flops | bytes accessed | tf_op | source)
XLA Modules:
  0.0 856.1 jit_solution(4079775959743964188)
XLA Ops:
  8.6 3.1 shard_map.246
  11.7 3.5 dynamic-slice_bitcast_fusion.3
  15.2 3.0 collective-permute-start
  19.2 56.1 %collective-permute-done.1 = bf16[512,1024]{1,0:T(8,128)(2,1)} collective-permute-done((bf16[512,1024]{1,0:T(8,128)(2,1)}, bf16[512,1024]{1,0:T(8,128)(2,1)}, u32[]{:S(2)}, u32[]{:S(2)}) %collective-permute-start.1) | collective-permute-done | bytes 1048608 | tf_op jit(solution)/shard_map/ppermute | solution.py:1131
  78.6 2.0 pad_maximum_fusion.1.tokens_ref
  80.7 3.3 dynamic-slice_bitcast_fusion
  92.0 27.8 %collective-permute-done.2 = bf16[768,1024]{1,0:T(8,128)(2,1)} collective-permute-done((bf16[768,1024]{1,0:T(8,128)(2,1)}, bf16[768,1024]{1,0:T(8,128)(2,1)}, u32[]{:S(2)}, u32[]{:S(2)}) %collective-permute-start.2) | collective-permute-done | bytes 1572896 | tf_op jit(solution)/shard_map/ppermute | solution.py:1131
  119.8 5.0 fusion.11
  124.8 2.1 pad_maximum_fusion.2.grad_ref
  128.4 8.4 shard_map.250
  136.9 16.9 %shard_map.247 = (bf16[1536,1024]{1,0:T(8,128)(2,1)}, bf16[1536,1024]{1,0:T(8,128)(2,1)}, bf16[1536,1024]{1,0:T(8,128)(2,1)}, bf16[1536,1024]{1,0:T(8,128)(2,1)}) custom-call(s32[4]{0:T(128)} %copy-done.17, bf16[1536,1024]{1,0:T(8,128)(2,1)} %pad_maximum_fusion.1.tokens_ref, f32[8,1024]{1,0:T(8,128)} %reshape.402.norm_ref, bf16[16,528,1024]{2,1,0:T(8,128)(2,1)} %bitcast.281, ...), custom_call_target="tpu_custom_call" | custom-call | flops 9663676416 | bytes 16777216 | tf_op jit(solution)/shard_map/pallas_call | solution.py:791
  153.7 30.5 %shard_map.248 = (bf16[1536,1024]{1,0:T(8,128)(2,1)S(1)}, bf16[1536,1024]{1,0:T(8,128)(2,1)}) custom-call(bf16[1536,1024]{1,0:T(8,128)(2,1)} %get-tuple-element.92.q_ref, bf16[1536,1024]{1,0:T(8,128)(2,1)} %get-tuple-element.93.k_ref, bf16[1536,1024]{1,0:T(8,128)(2,1)} %get-tuple-element.94.v_ref, bf16[1536,128]{1,0:T(8,128)(2,1)S(1)} %fusion.8.qd_ref, ...), custom_call_target="tpu_custom_call" | custom-call | flops 16911433728 | bytes 16777216 | tf_op jit(solution)/shard_map/pallas_call | solution.py:588
  185.9 14.1 %shard_map.249 = (f32[1536,1024]{1,0:T(8,128)}, bf16[1536,1024]{1,0:T(8,128)(2,1)}, bf16[1536,1024]{1,0:T(8,128)(2,1)}) custom-call(s32[4]{0:T(128)} %copy-done.17, bf16[1536,1024]{1,0:T(8,128)(2,1)} %copy-done.2, bf16[1536,1024]{1,0:T(8,128)(2,1)} %pad_maximum_fusion.1.tokens_ref, f32[8,1024]{1,0:T(8,128)} %reshape.402.norm_ref, ...), custom_call_target="tpu_custom_call" | custom-call | flops 6442450944 | bytes 16777216 | tf_op jit(solution)/shard_map/pallas_call | solution.py:828
  199.9 31.2 %shard_map.251 = (bf16[1536,1024]{1,0:T(8,128)(2,1)}, bf16[1536,1024]{1,0:T(8,128)(2,1)}) custom-call(bf16[1536,1024]{1,0:T(8,128)(2,1)} %get-tuple-element.96.q_ref, bf16[1024,1024]{1,0:T(8,128)(2,1)S(1)} %copy-done.4, bf16[1024,1024]{1,0:T(8,128)(2,1)S(1)} %copy-done.5, bf16[1536,128]{1,0:T(8,128)(2,1)S(1)} %fusion.8.qd_ref, ...), custom_call_target="tpu_custom_call" | custom-call | flops 16106127360 | bytes 16777216 | tf_op jit(solution)/shard_map/pallas_call | solution.py:588
  231.1 9.9 %shard_map.252 = (f32[1536,1024]{1,0:T(8,128)}, bf16[1536,1024]{1,0:T(8,128)(2,1)}) custom-call(bf16[1536,1024]{1,0:T(8,128)(2,1)} %get-tuple-element.99.mixed_ref.left_ref.out_ref, f32[1536,1024]{1,0:T(8,128)} %get-tuple-element.100.base_ref.after_ref, f32[8,1024]{1,0:T(8,128)} %reshape.402.norm_ref, bf16[16,528,1024]{2,1,0:T(8,128)(2,1)} %bitcast.286), custom_call_target="tpu_custom_call" | custom-call | flops 3221225472 | bytes 16777216 | tf_op jit(solution)/shard_map/pallas_call | solution.py:846
  241.0 66.3 %shard_map.253 = (f32[1536,1024]{1,0:T(8,128)}, f32[1536,1024]{1,0:T(8,128)}, bf16[2,2,4,4,32,1024]{5,4,3,2,1,0:T(8,128)(2,1)}, bf16[2,2,4,4,32,1024]{5,4,3,2,1,0:T(8,128)(2,1)}) custom-call(s32[3]{0:T(128)} %pad_add_fusion.place_ref, bf16[1536,1024]{1,0:T(8,128)(2,1)} %get-tuple-element.109.third_ref, bf16[1536,1024]{1,0:T(8,128)(2,1)} %pad_maximum_fusion.2.grad_ref, ...), custom_call_target="tpu_custom_call" | custom-call | flops 38654705664 | bytes 16777216 | tf_op jit(solution)/shard_map/pallas_call | solution.py:953
  307.3 65.9 %shard_map.254 = (f32[1536,1024]{1,0:T(8,128)}, f32[1536,1024]{1,0:T(8,128)}, bf16[2,2,4,4,32,1024]{5,4,3,2,1,0:T(8,128)(2,1)}, bf16[2,2,4,4,32,1024]{5,4,3,2,1,0:T(8,128)(2,1)}) custom-call(s32[3]{0:T(128)} %pad_add_fusion.place_ref, bf16[1536,1024]{1,0:T(8,128)(2,1)} %get-tuple-element.109.third_ref, bf16[1536,1024]{1,0:T(8,128)(2,1)} %pad_maximum_fusion.2.grad_ref, ...), custom_call_target="tpu_custom_call" | custom-call | flops 38654705664 | bytes 16777216 | tf_op jit(solution)/shard_map/pallas_call | solution.py:953
  373.8 3.3 fusion.2
  377.1 18.6 %shard_map.255 = (bf16[1536,1024]{1,0:T(8,128)(2,1)}, f32[1536,1024]{1,0:T(8,128)}, bf16[1536,1024]{1,0:T(8,128)(2,1)}, bf16[1536,1024]{1,0:T(8,128)(2,1)}, f32[8,1024]{1,0:T(8,128)}) custom-call(s32[4]{0:T(128)} %copy-done.17, f32[1536,1024]{1,0:T(8,128)} %get-tuple-element.107.after_ref, f32[1536,1024]{1,0:T(8,128)} %get-tuple-element.108.out_a, ...), custom_call_target="tpu_custom_call" | custom-call | flops 3221225472 | bytes 16777216 | tf_op jit(solution)/shard_map/pallas_call | solution.py:1003
  395.7 8.3 shard_map.256
  404.0 4.9 fusion.3
  411.9 54.1 %shard_map.257 = (bf16[1536,1024]{1,0:T(8,128)(2,1)}, bf16[2,1024,1024]{2,1,0:T(8,128)(2,1)}) custom-call(bf16[1536,1024]{1,0:T(8,128)(2,1)} %get-tuple-element.96.q_ref, bf16[1024,1024]{1,0:T(8,128)(2,1)S(1)} %copy-done.4, bf16[1024,1024]{1,0:T(8,128)(2,1)S(1)} %copy-done.6, bf16[1536,1024]{1,0:T(8,128)(2,1)} %get-tuple-element.115.extra_ref, ...), custom_call_target="tpu_custom_call" | custom-call | flops 40265318400 | bytes 16777216 | tf_op jit(solution)/shard_map/pallas_call | solution.py:610
  465.9 15.4 %shard_map.258 = (f32[1536,1024]{1,0:T(8,128)}, bf16[1536,1024]{1,0:T(8,128)(2,1)}, bf16[1536,1024]{1,0:T(8,128)(2,1)}, f32[8,1024]{1,0:T(8,128)}) custom-call(bf16[1536,1024]{1,0:T(8,128)(2,1)} %get-tuple-element.135.grad_ref.right_ref, f32[1536,1024]{1,0:T(8,128)} %get-tuple-element.100.base_ref.after_ref, f32[1536,1024]{1,0:T(8,128)} %get-tuple-element.125.base_ref, ...), custom_call_target="tpu_custom_call" | custom-call | flops 6442450944 | bytes 16777216 | tf_op jit(solution)/shard_map/pallas_call | solution.py:1036
  481.3 3.5 fusion.4
  484.8 3.5 fusion.5
  488.3 10.7 %shard_map.259 = (bf16[2,2,4,5,32,1024]{5,4,3,2,1,0:T(8,128)(2,1)}, bf16[2,2,4,5,32,1024]{5,4,3,2,1,0:T(8,128)(2,1)}) custom-call(s32[3]{0:T(128)} %pad_add_fusion.place_ref, bf16[1024,1024]{1,0:T(8,128)(2,1)} %pad_maximum_fusion.3.source_ref.left_ref, ...), custom_call_target="tpu_custom_call", output_to_operand_aliasing={{0}: (3, {}), {1}: (4, {})} | custom-call | flops 4294967296 | bytes 16777216 | tf_op jit(solution)/shard_map/pallas_call | solution.py:1108
  499.0 8.6 shard_map.260
  507.6 8.3 shard_map.261
  521.8 2.6 slice.224
  527.4 8.6 %shard_map.262 = bf16[1024,1024]{1,0:T(8,128)(2,1)} custom-call(bf16[2,1024,1024]{2,1,0:T(8,128)(2,1)} %get-tuple-element.140.right_ref.grads_ref, bf16[16,528,1024]{2,1,0:T(8,128)(2,1)} %bitcast.290, bf16[16,528,1024]{2,1,0:T(8,128)(2,1)} %bitcast.291), custom_call_target="tpu_custom_call" | custom-call | flops 4294967296 | bytes 16777216 | tf_op jit(solution)/shard_map/pallas_call | solution.py:1079
  538.9 2.9 collective-permute-done.9
  541.8 2.4 fusion.30
  544.3 2.5 fusion.33
  546.7 4.8 fusion
  553.1 2.5 collective-permute-start.15
  559.2 3.4 collective-permute-done.14
  562.6 11.9 %collective-permute-start.12 = (bf16[4,32,1024]{2,1,0:T(8,128)(2,1)S(1)}, bf16[4,32,1024]{2,1,0:T(8,128)(2,1)}, u32[]{:S(2)}, u32[]{:S(2)}) collective-permute-start(bf16[4,32,1024]{2,1,0:T(8,128)(2,1)S(1)} %get-tuple-element.146), channel_id=1, source_target_pairs={{0,8},{1,9},{2,10},{3,11},{4,12},{5,13},{6,14},{7,15},{8,0},{9,1},... | collective-permute-start | bytes 786440 | tf_op jit(solution)/shard_map/ppermute | solution.py:1155
  574.6 14.9 %collective-permute-start.13 = (bf16[4,32,1024]{2,1,0:T(8,128)(2,1)S(1)}, bf16[4,32,1024]{2,1,0:T(8,128)(2,1)}, u32[]{:S(2)}, u32[]{:S(2)}) collective-permute-start(bf16[4,32,1024]{2,1,0:T(8,128)(2,1)S(1)} %get-tuple-element.147), channel_id=1, source_target_pairs={{0,12},{1,13},{2,14},{3,15},{4,0},{5,1},{6,2},{7,3},{8,4},{9,5},{1... | collective-permute-start | bytes 786440 | tf_op jit(solution)/shard_map/ppermute | solution.py:1155
  589.5 56.2 %shard_map.263.right_ref.grads_ref = bf16[3,1536,1024]{2,1,0:T(8,128)(2,1)} custom-call(bf16[1536,1024]{1,0:T(8,128)(2,1)S(1)} %copy-done.3, bf16[1536,1024]{1,0:T(8,128)(2,1)} %get-tuple-element.93.k_ref, bf16[1536,1024]{1,0:T(8,128)(2,1)} %get-tuple-element.94.v_ref, bf16[1536,1024]{1,0:T(8,128)(2,1)} %get-tuple-element.114.extra_ref, ...), custom_call_target="tpu_custom_call" | custom-call | flops 42278584320 | bytes 16777216 | tf_op jit(solution)/shard_map/pallas_call | solution.py:610
  646.2 2.3 fusion.25
  650.0 2.2 fusion.29
  652.3 3.7 fusion.1
  655.9 18.7 %shard_map.264 = (bf16[2,2,4,3,32,1024]{5,4,3,2,1,0:T(8,128)(2,1)}, bf16[2,2,4,3,32,1024]{5,4,3,2,1,0:T(8,128)(2,1)}) custom-call(s32[3]{0:T(128)} %pad_add_fusion.place_ref, bf16[1536,1024]{1,0:T(8,128)(2,1)} %get-tuple-element.156.left_ref, bf16[3,1536,1024]{2,1,0:T(8,128)(2,1)} %shard_map.263.right_ref.grads_ref), custom_call_target="tpu_custom_call" | custom-call | flops 9663676416 | bytes 16777216 | tf_op jit(solution)/shard_map/pallas_call | solution.py:1108
  674.7 7.8 collective-permute-done.4
  684.1 1.9 maximum_bitcast_fusion
  688.0 16.0 %collective-permute-done.22 = bf16[512,1024]{1,0:T(8,128)(2,1)} collective-permute-done((bf16[512,1024]{1,0:T(8,128)(2,1)}, bf16[512,1024]{1,0:T(8,128)(2,1)}, u32[]{:S(2)}, u32[]{:S(2)}) %collective-permute-start.22) | collective-permute-done | bytes 1048608 | tf_op jit(solution)/shard_map/ppermute | solution.py:1131
  711.8 2.6 slice.298
  721.0 3.0 reshape.398
  724.0 2.3 pad_maximum_fusion.5
  726.3 3.9 fusion.6
  730.7 15.4 %collective-permute-done.29 = bf16[4,5,32,1024]{3,2,1,0:T(8,128)(2,1)} collective-permute-done((bf16[4,5,32,1024]{3,2,1,0:T(8,128)(2,1)}, bf16[4,5,32,1024]{3,2,1,0:T(8,128)(2,1)}, u32[]{:S(2)}, u32[]{:S(2)}) %collective-permute-start.29) | collective-permute-done | bytes 1310752 | tf_op jit(solution)/shard_map/ppermute | solution.py:1131
  746.0 2.0 fusion.17
  749.3 2.6 collective-permute-start.32
  751.9 20.5 %shard_map.265 = (bf16[1536,1024]{1,0:T(8,128)(2,1)}, f32[8,1024]{1,0:T(8,128)}) custom-call(s32[4]{0:T(128)} %copy-done.17, bf16[3,1536,1024]{2,1,0:T(8,128)(2,1)} %shard_map.263.right_ref.grads_ref, bf16[1536,1024]{1,0:T(8,128)(2,1)} %pad_maximum_fusion.1.tokens_ref, f32[1536,1024]{1,0:T(8,128)} %get-tuple-element.160.base_ref, ...), custom_call_target="tpu_custom_call" | custom-call | flops 9663676416 | bytes 16777216 | tf_op jit(solution)/shard_map/pallas_call | solution.py:1055
  775.5 2.7 slice.251
  780.3 2.1 fusion.7
  786.4 3.2 collective-permute-done.36
  789.6 2.0 collective-permute-start.37
  792.5 2.2 collective-permute-done.37
  797.3 22.2 %collective-permute-done.38 = f32[6,1024]{1,0:T(8,128)S(1)} collective-permute-done((f32[6,1024]{1,0:T(8,128)S(1)}, f32[6,1024]{1,0:T(8,128)S(1)}, u32[]{:S(2)}, u32[]{:S(2)}) %collective-permute-start.38) | collective-permute-done | bytes 24608 | tf_op jit(solution)/shard_map/ppermute | solution.py:1131
  825.9 2.8 collective-permute-start.27
  829.2 4.2 collective-permute-done.25
  833.4 7.3 collective-permute-done.26
  844.1 1.9 maximum_bitcast_fusion.1
  (189 shorter events, 81.7 us)
Async XLA Ops:
  7.2 78.7 %copy-start = (s32[2,1,1536]{2,1,0:T(1,128)S(1)}, s32[2,1,1536]{2,1,0:T(1,128)}, u32[]{:S(2)}) copy-start(s32[2,1,1536]{2,1,0:T(1,128)} %param.18) | copy-start | bytes 36868
  7.2 119.8 %all-gather.5.cloned.1.call-start = ((), (), s32[]{:S(2)}) async-start(), calls=%async_computation | async-start | bytes 18382848 | tf_op jit(solution)/shard_map/all_gather | solution.py:1234
  11.7 229.3 %all-gather.7.cloned.1.call-start = ((), (), s32[]{:S(2)}) async-start(), calls=%async_computation.1 | async-start | bytes 18382848 | tf_op jit(solution)/shard_map/all_gather | solution.py:1262
  11.7 6.5 copy-start.12
  15.2 63.4 %collective-permute-start = (bf16[768,1024]{1,0:T(8,128)(2,1)}, bf16[768,1024]{1,0:T(8,128)(2,1)S(1)}, u32[]{:S(2)}, u32[]{:S(2)}) collective-permute-start(bf16[768,1024]{1,0:T(8,128)(2,1)} %get-tuple-element.259), channel_id=1, source_target_pairs={{0,16},{16,0},{1,17},{17,1},{2,18},{18,2},{3,19},{19,3},{4,20},{20... | collective-permute-start | bytes 4718600 | tf_op jit(solution)/shard_map/ppermute | solution.py:1131
  19.2 56.1 %collective-permute-start.1 = (bf16[512,1024]{1,0:T(8,128)(2,1)}, bf16[512,1024]{1,0:T(8,128)(2,1)}, u32[]{:S(2)}, u32[]{:S(2)}) collective-permute-start(bf16[512,1024]{1,0:T(8,128)(2,1)} %dynamic-slice_bitcast_fusion.4), channel_id=1, source_target_pairs={{0,16},{16,0},{1,17},{17,1},{2,18},{18,2},{3,19},{19,3},{4,20},{20... | collective-permute-start | bytes 3145736 | tf_op jit(solution)/shard_map/ppermute | solution.py:1131
  80.6 9.4 %copy-start.18 = (s32[2,1,4]{2,1,0:T(1,128)S(1)}, s32[2,1,4]{2,1,0:T(1,128)}, u32[]{:S(2)}) copy-start(s32[2,1,4]{2,1,0:T(1,128)} %param.19) | copy-start | bytes 100
  80.7 9.4 %copy-start.19 = (s32[2,1,4]{2,1,0:T(1,128)S(1)}, s32[2,1,4]{2,1,0:T(1,128)}, u32[]{:S(2)}) copy-start(s32[2,1,4]{2,1,0:T(1,128)} %param.20) | copy-start | bytes 100
  84.0 35.8 %collective-permute-start.2 = (bf16[768,1024]{1,0:T(8,128)(2,1)}, bf16[768,1024]{1,0:T(8,128)(2,1)}, u32[]{:S(2)}, u32[]{:S(2)}) collective-permute-start(bf16[768,1024]{1,0:T(8,128)(2,1)} %get-tuple-element.254), channel_id=1, source_target_pairs={{0,16},{16,0},{1,17},{17,1},{2,18},{18,2},{3,19},{19,3},{4,20},{20... | collective-permute-start | bytes 4718600 | tf_op jit(solution)/shard_map/ppermute | solution.py:1131
  86.8 38.0 %copy-start.17 = (s32[4]{0:T(128)}, s32[4]{0:T(128)S(1)}, u32[]{:S(2)}) copy-start(s32[4]{0:T(128)S(1)} %compare_select_fusion.3.held) | copy-start | bytes 52
  184.2 1.7 copy-start.2
  185.9 14.1 %copy-start.4 = (bf16[1024,1024]{1,0:T(8,128)(2,1)S(1)}, bf16[1024,1024]{1,0:T(8,128)(2,1)}, u32[]{:S(2)}) copy-start(bf16[1024,1024]{1,0:T(8,128)(2,1)} %get-tuple-element.97.k_ref) | copy-start | bytes 6291460
  185.9 14.1 %copy-start.5 = (bf16[1024,1024]{1,0:T(8,128)(2,1)S(1)}, bf16[1024,1024]{1,0:T(8,128)(2,1)}, u32[]{:S(2)}) copy-start(bf16[1024,1024]{1,0:T(8,128)(2,1)} %get-tuple-element.98.v_ref) | copy-start | bytes 6291460
  307.3 66.5 %collective-permute-start.3 = (bf16[2,2,4,4,32,1024]{5,4,3,2,1,0:T(8,128)(2,1)}, bf16[2,2,4,4,32,1024]{5,4,3,2,1,0:T(8,128)(2,1)}, u32[]{:S(2)}, u32[]{:S(2)}) collective-permute-start(bf16[2,2,4,4,32,1024]{5,4,3,2,1,0:T(8,128)(2,1)} %get-tuple-element.106), channel_id=1, source_target_pairs={{0,1},{1,0},{2,3},{3,2},{4,5},{5,4},{6,7},{7,6},{8,9},{9,8},{10,11... | collective-permute-start | bytes 12582920 | tf_op jit(solution)/shard_map/ppermute | solution.py:1139
  373.2 30.8 %collective-permute-start.5 = (bf16[2,2,4,4,32,1024]{5,4,3,2,1,0:T(8,128)(2,1)}, bf16[2,2,4,4,32,1024]{5,4,3,2,1,0:T(8,128)(2,1)}, u32[]{:S(2)}, u32[]{:S(2)}) collective-permute-start(bf16[2,2,4,4,32,1024]{5,4,3,2,1,0:T(8,128)(2,1)} %get-tuple-element.122), channel_id=1, source_target_pairs={{0,1},{1,0},{2,3},{3,2},{4,5},{5,4},{6,7},{7,6},{8,9},{9,8},{10,11... | collective-permute-start | bytes 12582920 | tf_op jit(solution)/shard_map/ppermute | solution.py:1139
  404.0 7.8 copy-start.6
  408.9 72.4 %collective-permute-start.7 = (bf16[2,4,4,32,1024]{4,3,2,1,0:T(8,128)(2,1)}, bf16[2,4,4,32,1024]{4,3,2,1,0:T(8,128)(2,1)}, u32[]{:S(2)}, u32[]{:S(2)}) collective-permute-start(bf16[2,4,4,32,1024]{4,3,2,1,0:T(8,128)(2,1)} %fusion.3), channel_id=1, source_target_pairs={{0,16},{16,0},{1,17},{17,1},{2,18},{18,2},{3,19},{19,3},{4,20},{20... | collective-permute-start | bytes 6291464 | tf_op jit(solution)/shard_map/ppermute | solution.py:1131
  410.3 74.5 %collective-permute-start.6 = (bf16[2,4,4,32,1024]{4,3,2,1,0:T(8,128)(2,1)S(1)}, bf16[2,4,4,32,1024]{4,3,2,1,0:T(8,128)(2,1)}, u32[]{:S(2)}, u32[]{:S(2)}) collective-permute-start(bf16[2,4,4,32,1024]{4,3,2,1,0:T(8,128)(2,1)S(1)} %fusion.2), channel_id=1, source_target_pairs={{0,2},{1,3},{2,0},{3,1},{4,6},{5,7},{6,4},{7,5},{8,10},{9,11},{10,... | collective-permute-start | bytes 6291464 | tf_op jit(solution)/shard_map/ppermute | solution.py:1136
  515.9 30.8 %collective-permute-start.10 = (bf16[2,2,4,5,32,1024]{5,4,3,2,1,0:T(8,128)(2,1)}, bf16[2,2,4,5,32,1024]{5,4,3,2,1,0:T(8,128)(2,1)}, u32[]{:S(2)}, u32[]{:S(2)}) collective-permute-start(bf16[2,2,4,5,32,1024]{5,4,3,2,1,0:T(8,128)(2,1)} %get-tuple-element.139), channel_id=1, source_target_pairs={{0,1},{1,0},{2,3},{3,2},{4,5},{5,4},{6,7},{7,6},{8,9},{9,8},{10,11... | collective-permute-start | bytes 15728648 | tf_op jit(solution)/shard_map/ppermute | solution.py:1139
  515.9 25.9 %collective-permute-start.9 = (bf16[4,4,32,1024]{3,2,1,0:T(8,128)(2,1)}, bf16[4,4,32,1024]{3,2,1,0:T(8,128)(2,1)}, u32[]{:S(2)}, u32[]{:S(2)}) collective-permute-start(bf16[4,4,32,1024]{3,2,1,0:T(8,128)(2,1)} %fusion.4), channel_id=1, source_target_pairs={{0,2},{1,3},{2,0},{3,1},{4,6},{5,7},{6,4},{7,5},{8,10},{9,11},{10,... | collective-permute-start | bytes 3145736 | tf_op jit(solution)/shard_map/ppermute | solution.py:1136
  516.4 27.8 %collective-permute-start.8 = (bf16[4,4,32,1024]{3,2,1,0:T(8,128)(2,1)}, bf16[4,4,32,1024]{3,2,1,0:T(8,128)(2,1)}, u32[]{:S(2)}, u32[]{:S(2)}) collective-permute-start(bf16[4,4,32,1024]{3,2,1,0:T(8,128)(2,1)} %fusion.5), channel_id=1, source_target_pairs={{0,16},{16,0},{1,17},{17,1},{2,18},{18,2},{3,19},{19,3},{4,20},{20... | collective-permute-start | bytes 3145736 | tf_op jit(solution)/shard_map/ppermute | solution.py:1131
  525.7 16.1 %copy-start.9 = (bf16[1,1,4,4,32,1024]{5,4,3,2,1,0:T(8,128)(2,1)}, bf16[1,1,4,4,32,1024]{5,4,3,2,1,0:T(8,128)(2,1)S(1)}, u32[]{:S(2)}) copy-start(bf16[1,1,4,4,32,1024]{5,4,3,2,1,0:T(8,128)(2,1)S(1)} %slice.281) | copy-start | bytes 3145732
  537.4 9.3 %slice-start = ((s8[5242880]{0:T(1024)(128)(4,1)}), s8[4194304]{0:T(1024)(128)(4,1)S(1)}, s32[]{:S(2)}) async-start(s8[5242880]{0:T(1024)(128)(4,1)} %bitcast.295), calls=%async_computation.2 | async-start | bytes 8388608
  538.9 7.9 slice-start.1
  546.7 8.9 %copy-start.7 = (bf16[1024,1024]{1,0:T(8,128)(2,1)S(1)}, bf16[1024,1024]{1,0:T(8,128)(2,1)}, u32[]{:S(2)}) copy-start(bf16[1024,1024]{1,0:T(8,128)(2,1)} %shard_map.262) | copy-start | bytes 6291460
  551.5 38.0 %copy-start.3 = (bf16[1536,1024]{1,0:T(8,128)(2,1)S(1)}, bf16[1536,1024]{1,0:T(8,128)(2,1)}, u32[]{:S(2)}) copy-start(bf16[1536,1024]{1,0:T(8,128)(2,1)} %get-tuple-element.92.q_ref) | copy-start | bytes 9437188
  551.5 11.1 %collective-permute-start.14 = (bf16[4,32,1024]{2,1,0:T(8,128)(2,1)S(1)}, bf16[4,32,1024]{2,1,0:T(8,128)(2,1)S(1)}, u32[]{:S(2)}, u32[]{:S(2)}) collective-permute-start(bf16[4,32,1024]{2,1,0:T(8,128)(2,1)S(1)} %get-tuple-element.148), channel_id=1, source_target_pairs={{0,4},{1,5},{2,6},{3,7},{4,8},{5,9},{6,10},{7,11},{8,12},{9,13},{1... | collective-permute-start | bytes 786440 | tf_op jit(solution)/shard_map/ppermute | solution.py:1155
  553.1 21.5 %collective-permute-start.15 = (bf16[4,32,1024]{2,1,0:T(8,128)(2,1)S(1)}, bf16[4,32,1024]{2,1,0:T(8,128)(2,1)S(1)}, u32[]{:S(2)}, u32[]{:S(2)}) collective-permute-start(bf16[4,32,1024]{2,1,0:T(8,128)(2,1)S(1)} %get-tuple-element.149), channel_id=1, source_target_pairs={{0,8},{1,9},{2,10},{3,11},{4,12},{5,13},{6,14},{7,15},{8,0},{9,1},... | collective-permute-start | bytes 786440 | tf_op jit(solution)/shard_map/ppermute | solution.py:1155
  556.7 95.6 %collective-permute-start.17 = (bf16[2,4,5,32,1024]{4,3,2,1,0:T(8,128)(2,1)}, bf16[2,4,5,32,1024]{4,3,2,1,0:T(8,128)(2,1)}, u32[]{:S(2)}, u32[]{:S(2)}) collective-permute-start(bf16[2,4,5,32,1024]{4,3,2,1,0:T(8,128)(2,1)} %fusion), channel_id=1, source_target_pairs={{0,2},{1,3},{2,0},{3,1},{4,6},{5,7},{6,4},{7,5},{8,10},{9,11},{10,... | collective-permute-start | bytes 7864328 | tf_op jit(solution)/shard_map/ppermute | solution.py:1136
  557.2 88.5 %collective-permute-start.16 = (bf16[4,32,1024]{2,1,0:T(8,128)(2,1)}, bf16[4,32,1024]{2,1,0:T(8,128)(2,1)}, u32[]{:S(2)}, u32[]{:S(2)}) collective-permute-start(bf16[4,32,1024]{2,1,0:T(8,128)(2,1)} %get-tuple-element.150), channel_id=1, source_target_pairs={{0,12},{1,13},{2,14},{3,15},{4,0},{5,1},{6,2},{7,3},{8,4},{9,5},{1... | collective-permute-start | bytes 786440 | tf_op jit(solution)/shard_map/ppermute | solution.py:1155
  558.6 89.9 %collective-permute-start.11 = (bf16[4,32,1024]{2,1,0:T(8,128)(2,1)}, bf16[4,32,1024]{2,1,0:T(8,128)(2,1)}, u32[]{:S(2)}, u32[]{:S(2)}) collective-permute-start(bf16[4,32,1024]{2,1,0:T(8,128)(2,1)} %get-tuple-element.145), channel_id=1, source_target_pairs={{0,4},{1,5},{2,6},{3,7},{4,8},{5,9},{6,10},{7,11},{8,12},{9,13},{1... | collective-permute-start | bytes 786440 | tf_op jit(solution)/shard_map/ppermute | solution.py:1155
  562.6 26.9 %copy-start.14 = (bf16[4,32,1024]{2,1,0:T(8,128)(2,1)}, bf16[4,32,1024]{2,1,0:T(8,128)(2,1)S(1)}, u32[]{:S(2)}) copy-start(bf16[4,32,1024]{2,1,0:T(8,128)(2,1)S(1)} %collective-permute-done.14) | copy-start | bytes 786436
  562.6 87.4 %collective-permute-start.12 = (bf16[4,32,1024]{2,1,0:T(8,128)(2,1)S(1)}, bf16[4,32,1024]{2,1,0:T(8,128)(2,1)}, u32[]{:S(2)}, u32[]{:S(2)}) collective-permute-start(bf16[4,32,1024]{2,1,0:T(8,128)(2,1)S(1)} %get-tuple-element.146), channel_id=1, source_target_pairs={{0,8},{1,9},{2,10},{3,11},{4,12},{5,13},{6,14},{7,15},{8,0},{9,1},... | collective-permute-start | bytes 786440 | tf_op jit(solution)/shard_map/ppermute | solution.py:1155
  574.5 14.9 %copy-start.15 = (bf16[4,32,1024]{2,1,0:T(8,128)(2,1)}, bf16[4,32,1024]{2,1,0:T(8,128)(2,1)S(1)}, u32[]{:S(2)}) copy-start(bf16[4,32,1024]{2,1,0:T(8,128)(2,1)S(1)} %collective-permute-done.15) | copy-start | bytes 786436
  574.6 75.5 %collective-permute-start.13 = (bf16[4,32,1024]{2,1,0:T(8,128)(2,1)S(1)}, bf16[4,32,1024]{2,1,0:T(8,128)(2,1)}, u32[]{:S(2)}, u32[]{:S(2)}) collective-permute-start(bf16[4,32,1024]{2,1,0:T(8,128)(2,1)S(1)} %get-tuple-element.147), channel_id=1, source_target_pairs={{0,12},{1,13},{2,14},{3,15},{4,0},{5,1},{6,2},{7,3},{8,4},{9,5},{1... | collective-permute-start | bytes 786440 | tf_op jit(solution)/shard_map/ppermute | solution.py:1155
  645.7 36.7 %collective-permute-start.4 = (bf16[768,1024]{1,0:T(8,128)(2,1)}, bf16[768,1024]{1,0:T(8,128)(2,1)}, u32[]{:S(2)}, u32[]{:S(2)}) collective-permute-start(bf16[768,1024]{1,0:T(8,128)(2,1)} %slice.224), channel_id=1, source_target_pairs={{0,16},{16,0},{1,17},{17,1},{2,18},{18,2},{3,19},{19,3},{4,20},{20... | collective-permute-start | bytes 4718600 | tf_op jit(solution)/shard_map/ppermute | solution.py:1131
  648.5 55.5 %collective-permute-start.22 = (bf16[512,1024]{1,0:T(8,128)(2,1)}, bf16[512,1024]{1,0:T(8,128)(2,1)}, u32[]{:S(2)}, u32[]{:S(2)}) collective-permute-start(bf16[512,1024]{1,0:T(8,128)(2,1)} %broadcast_select_fusion), channel_id=1, source_target_pairs={{0,16},{16,0},{1,17},{17,1},{2,18},{18,2},{3,19},{19,3},{4,20},{20... | collective-permute-start | bytes 3145736 | tf_op jit(solution)/shard_map/ppermute | solution.py:1131
  655.9 26.5 %copy-start.10 = (bf16[1536,1024]{1,0:T(8,128)(2,1)S(1)}, bf16[1536,1024]{1,0:T(8,128)(2,1)}, u32[]{:S(2)}) copy-start(bf16[1536,1024]{1,0:T(8,128)(2,1)} %get-tuple-element.113) | copy-start | bytes 9437188
  674.6 51.7 %collective-permute-start.20 = (bf16[2,2,4,3,32,1024]{5,4,3,2,1,0:T(8,128)(2,1)}, bf16[2,2,4,3,32,1024]{5,4,3,2,1,0:T(8,128)(2,1)}, u32[]{:S(2)}, u32[]{:S(2)}) collective-permute-start(bf16[2,2,4,3,32,1024]{5,4,3,2,1,0:T(8,128)(2,1)} %get-tuple-element.158), channel_id=1, source_target_pairs={{0,1},{1,0},{2,3},{3,2},{4,5},{5,4},{6,7},{7,6},{8,9},{9,8},{10,11... | collective-permute-start | bytes 9437192 | tf_op jit(solution)/shard_map/ppermute | solution.py:1139
  687.5 26.9 %collective-permute-start.18 = (bf16[4,32,1024]{2,1,0:T(8,128)(2,1)}, bf16[4,32,1024]{2,1,0:T(8,128)(2,1)S(1)}, u32[]{:S(2)}, u32[]{:S(2)}) collective-permute-start(bf16[4,32,1024]{2,1,0:T(8,128)(2,1)} %fusion.29), channel_id=1, source_target_pairs={{0,16},{16,0},{1,17},{17,1},{2,18},{18,2},{3,19},{19,3},{4,20},{20... | collective-permute-start | bytes 786440 | tf_op jit(solution)/shard_map/ppermute | solution.py:1131
  705.5 3.0 copy-start.13
  708.5 9.3 %collective-permute-start.19 = (bf16[4,32,1024]{2,1,0:T(8,128)(2,1)S(1)}, bf16[4,32,1024]{2,1,0:T(8,128)(2,1)S(1)}, u32[]{:S(2)}, u32[]{:S(2)}) collective-permute-start(bf16[4,32,1024]{2,1,0:T(8,128)(2,1)S(1)} %copy-done.13), channel_id=1, source_target_pairs={{0,16},{16,0},{1,17},{17,1},{2,18},{18,2},{3,19},{19,3},{4,20},{20... | collective-permute-start | bytes 786440 | tf_op jit(solution)/shard_map/ppermute | solution.py:1131
  709.1 37.0 %collective-permute-start.29 = (bf16[4,5,32,1024]{3,2,1,0:T(8,128)(2,1)}, bf16[4,5,32,1024]{3,2,1,0:T(8,128)(2,1)}, u32[]{:S(2)}, u32[]{:S(2)}) collective-permute-start(bf16[4,5,32,1024]{3,2,1,0:T(8,128)(2,1)} %fusion.1), channel_id=1, source_target_pairs={{0,16},{16,0},{1,17},{17,1},{2,18},{18,2},{3,19},{19,3},{4,20},{20... | collective-permute-start | bytes 3932168 | tf_op jit(solution)/shard_map/ppermute | solution.py:1131
  726.3 19.7 %copy-start.8 = (bf16[1,4,5,32,1024]{4,3,2,1,0:T(8,128)(2,1)S(1)}, bf16[1,4,5,32,1024]{4,3,2,1,0:T(8,128)(2,1)}, u32[]{:S(2)}) copy-start(bf16[1,4,5,32,1024]{4,3,2,1,0:T(8,128)(2,1)} %slice.298) | copy-start | bytes 3932164
  730.2 50.1 %collective-permute-start.23 = (bf16[2,4,3,32,1024]{4,3,2,1,0:T(8,128)(2,1)}, bf16[2,4,3,32,1024]{4,3,2,1,0:T(8,128)(2,1)}, u32[]{:S(2)}, u32[]{:S(2)}) collective-permute-start(bf16[2,4,3,32,1024]{4,3,2,1,0:T(8,128)(2,1)} %fusion.6), channel_id=1, source_target_pairs={{0,16},{16,0},{1,17},{17,1},{2,18},{18,2},{3,19},{19,3},{4,20},{20... | collective-permute-start | bytes 4718600 | tf_op jit(solution)/shard_map/ppermute | solution.py:1131
  748.1 25.2 %collective-permute-start.30 = (bf16[5,32,1024]{2,1,0:T(8,128)(2,1)S(1)}, bf16[5,32,1024]{2,1,0:T(8,128)(2,1)S(1)}, u32[]{:S(2)}, u32[]{:S(2)}) collective-permute-start(bf16[5,32,1024]{2,1,0:T(8,128)(2,1)S(1)} %get-tuple-element.232), channel_id=1, source_target_pairs={{0,4},{1,5},{2,6},{3,7},{4,8},{5,9},{6,10},{7,11},{8,12},{9,13},{1... | collective-permute-start | bytes 983048 | tf_op jit(solution)/shard_map/ppermute | solution.py:1155
  748.1 25.2 %collective-permute-start.31 = (bf16[5,32,1024]{2,1,0:T(8,128)(2,1)S(1)}, bf16[5,32,1024]{2,1,0:T(8,128)(2,1)}, u32[]{:S(2)}, u32[]{:S(2)}) collective-permute-start(bf16[5,32,1024]{2,1,0:T(8,128)(2,1)S(1)} %get-tuple-element.234), channel_id=1, source_target_pairs={{0,8},{1,9},{2,10},{3,11},{4,12},{5,13},{6,14},{7,15},{8,0},{9,1},... | collective-permute-start | bytes 983048 | tf_op jit(solution)/shard_map/ppermute | solution.py:1155
  749.3 24.0 %collective-permute-start.32 = (bf16[5,32,1024]{2,1,0:T(8,128)(2,1)S(1)}, bf16[5,32,1024]{2,1,0:T(8,128)(2,1)}, u32[]{:S(2)}, u32[]{:S(2)}) collective-permute-start(bf16[5,32,1024]{2,1,0:T(8,128)(2,1)S(1)} %get-tuple-element.233), channel_id=1, source_target_pairs={{0,12},{1,13},{2,14},{3,15},{4,0},{5,1},{6,2},{7,3},{8,4},{9,5},{1... | collective-permute-start | bytes 983048 | tf_op jit(solution)/shard_map/ppermute | solution.py:1155
  751.9 21.3 %copy-start.16 = (f32[2,1024]{1,0:T(2,128)S(1)}, f32[2,1024]{1,0:T(2,128)}, u32[]{:S(2)}) copy-start(f32[2,1024]{1,0:T(2,128)} %slice.268) | copy-start | bytes 24580
  773.2 6.5 collective-permute-start.34
  774.9 10.6 %collective-permute-start.33 = (bf16[5,32,1024]{2,1,0:T(8,128)(2,1)S(1)}, bf16[5,32,1024]{2,1,0:T(8,128)(2,1)S(1)}, u32[]{:S(2)}, u32[]{:S(2)}) collective-permute-start(bf16[5,32,1024]{2,1,0:T(8,128)(2,1)S(1)} %fusion.21), channel_id=1, source_target_pairs={{0,16},{16,0},{1,17},{17,1},{2,18},{18,2},{3,19},{19,3},{4,20},{20... | collective-permute-start | bytes 983048 | tf_op jit(solution)/shard_map/ppermute | solution.py:1131
  778.1 64.3 %collective-permute-start.21 = (bf16[768,1024]{1,0:T(8,128)(2,1)}, bf16[768,1024]{1,0:T(8,128)(2,1)}, u32[]{:S(2)}, u32[]{:S(2)}) collective-permute-start(bf16[768,1024]{1,0:T(8,128)(2,1)} %slice.251), channel_id=1, source_target_pairs={{0,16},{16,0},{1,17},{17,1},{2,18},{18,2},{3,19},{19,3},{4,20},{20... | collective-permute-start | bytes 4718600 | tf_op jit(solution)/shard_map/ppermute | solution.py:1131
  779.7 5.8 collective-permute-start.35
  782.4 39.6 %collective-permute-start.24 = (bf16[4,3,32,1024]{3,2,1,0:T(8,128)(2,1)S(1)}, bf16[4,3,32,1024]{3,2,1,0:T(8,128)(2,1)}, u32[]{:S(2)}, u32[]{:S(2)}) collective-permute-start(bf16[4,3,32,1024]{3,2,1,0:T(8,128)(2,1)S(1)} %fusion.7), channel_id=1, source_target_pairs={{0,2},{1,3},{2,0},{3,1},{4,6},{5,7},{6,4},{7,5},{8,10},{9,11},{10,... | collective-permute-start | bytes 2359304 | tf_op jit(solution)/shard_map/ppermute | solution.py:1136
  785.6 4.0 collective-permute-start.36
  789.6 5.2 collective-permute-start.37
  794.8 24.8 %collective-permute-start.38 = (f32[6,1024]{1,0:T(8,128)S(1)}, f32[6,1024]{1,0:T(8,128)S(1)}, u32[]{:S(2)}, u32[]{:S(2)}) collective-permute-start(f32[6,1024]{1,0:T(8,128)S(1)} %add.609), channel_id=1, source_target_pairs={{0,16},{16,0},{1,17},{17,1},{2,18},{18,2},{3,19},{19,3},{4,20},{20... | collective-permute-start | bytes 73736 | tf_op jit(solution)/shard_map/ppermute | solution.py:1131
  822.0 20.5 %copy-start.11 = (bf16[1536,1024]{1,0:T(8,128)(2,1)S(1)}, bf16[1536,1024]{1,0:T(8,128)(2,1)}, u32[]{:S(2)}) copy-start(bf16[1536,1024]{1,0:T(8,128)(2,1)} %get-tuple-element.161) | copy-start | bytes 9437188
  823.7 9.7 %collective-permute-start.25 = (bf16[3,32,1024]{2,1,0:T(8,128)(2,1)S(1)}, bf16[3,32,1024]{2,1,0:T(8,128)(2,1)S(1)}, u32[]{:S(2)}, u32[]{:S(2)}) collective-permute-start(bf16[3,32,1024]{2,1,0:T(8,128)(2,1)S(1)} %get-tuple-element.245), channel_id=1, source_target_pairs={{0,4},{1,5},{2,6},{3,7},{4,8},{5,9},{6,10},{7,11},{8,12},{9,13},{1... | collective-permute-start | bytes 589832 | tf_op jit(solution)/shard_map/ppermute | solution.py:1155
  824.4 16.4 %collective-permute-start.26 = (bf16[3,32,1024]{2,1,0:T(8,128)(2,1)S(1)}, bf16[3,32,1024]{2,1,0:T(8,128)(2,1)S(1)}, u32[]{:S(2)}, u32[]{:S(2)}) collective-permute-start(bf16[3,32,1024]{2,1,0:T(8,128)(2,1)S(1)} %get-tuple-element.247), channel_id=1, source_target_pairs={{0,8},{1,9},{2,10},{3,11},{4,12},{5,13},{6,14},{7,15},{8,0},{9,1},... | collective-permute-start | bytes 589832 | tf_op jit(solution)/shard_map/ppermute | solution.py:1155
  825.9 14.9 %collective-permute-start.27 = (bf16[3,32,1024]{2,1,0:T(8,128)(2,1)S(1)}, bf16[3,32,1024]{2,1,0:T(8,128)(2,1)S(1)}, u32[]{:S(2)}, u32[]{:S(2)}) collective-permute-start(bf16[3,32,1024]{2,1,0:T(8,128)(2,1)S(1)} %get-tuple-element.246), channel_id=1, source_target_pairs={{0,12},{1,13},{2,14},{3,15},{4,0},{5,1},{6,2},{7,3},{8,4},{9,5},{1... | collective-permute-start | bytes 589832 | tf_op jit(solution)/shard_map/ppermute | solution.py:1155
  842.0 5.7 collective-permute-start.28
  844.1 4.7 copy-start.1
Sparse Core Ops, SparseCore 0:
  11.8 94.2 all-gather.4
  107.7 91.5 all-gather.6

commit v2 on v1

--- a/solution.py
+++ b/solution.py
@@ -480,32 +480,36 @@
     return jnp.where(lane == 4, hi, jnp.where(lane == 5, mid, jnp.where(lane == 6, lo, base)))
 
 
-def beyond(size, flip):
-    row = lax.broadcasted_iota(jnp.int32, (size, size), 0)
-    column = lax.broadcasted_iota(jnp.int32, (size, size), 1)
-    return row > column if flip else column > row
-
-
 def two_heads(ref, own, other):
     left = lanes(own.shape[0]) < HEAD
     ref[0] = jnp.where(left, own, other)
     ref[1] = jnp.where(left, other, own)
 
 
+def tail_masked(scores, rows):
+    width = scores.shape[1] - rows
+    row = lax.broadcasted_iota(jnp.int32, (rows, rows), 0)
+    column = lax.broadcasted_iota(jnp.int32, (rows, rows), 1)
+    tail = jnp.where(column > row, -BIG, scores[:, width:])
+    return tail if width == 0 else jnp.concatenate([scores[:, :width], tail], axis=1)
+
+
 def attend_kernel(plan, q_ref, k_ref, v_ref, qd_ref, kd_ref, out_ref, extra_ref, keys, values):
     two_heads(keys, k_ref[...], kd_ref[...])
     two_heads(values, v_ref[...], jnp.ones_like(v_ref))
-    for q0, q1, k0, k1, diagonal in plan:
-        rows, width = (q1 - q0, k1 - k0)
-        left = lanes(rows) < HEAD
+
+    def scores_of(item):
+        q0, q1, k0, k1, diagonal = item
+        left = lanes(q1 - q0) < HEAD
         q, qd = (q_ref[q0:q1], qd_ref[q0:q1])
-        scores = []
-        for h in range(2):
-            s = dot(jnp.where(left == (h == 0), q, qd), keys[h, k0:k1], NT)
-            if diagonal:
-                tail = jnp.where(beyond(rows, False), -BIG, s[:, width - rows :])
-                s = tail if width == rows else jnp.concatenate([s[:, : width - rows], tail], axis=1)
-            scores.append(s)
+        pair = [dot(jnp.where(left == (h == 0), q, qd), keys[h, k0:k1], NT) for h in range(2)]
+        return [tail_masked(s, q1 - q0) for s in pair] if diagonal else pair
+
+    following = scores_of(plan[0])
+    for index, (q0, q1, k0, k1, _) in enumerate(plan):
+        scores = following
+        following = scores_of(plan[index + 1]) if index + 1 < len(plan) else None
+        left = lanes(q1 - q0) < HEAD
         mixed, tops = ([], [])
         for h in range(2):
             top = jnp.max(scores[h], axis=1, keepdims=True)
@@ -516,7 +520,7 @@
         numer = jnp.where(left, mixed[0], mixed[1])
         out_ref[q0:q1] = (numer / pltpu.roll(mass, HEAD, 1)).astype(jnp.bfloat16)
         top = jnp.where(left, tops[1], tops[0])
-        extra_ref[q0:q1] = spread(-(top + HEAD**0.5 * jnp.log(mass)), qd)
+        extra_ref[q0:q1] = spread(-(top + HEAD**0.5 * jnp.log(mass)), qd_ref[q0:q1])
 
 
 def attend_back_kernel(
@@ -530,7 +534,7 @@
     g_ref,
     *refs,
 ):
-    *outs, keys, values, queries, grads, total = refs
+    *outs, keys, values, queries, grads, g_t, q_t, dk_t, dv_t = refs
     if len(outs) == 1:
         dq_ref, dk_ref, dv_ref = (outs[0].at[i] for i in range(3))
     else:
@@ -540,31 +544,33 @@
     two_heads(queries, q_ref[...], extra_ref[...])
     square = (128, 128)
     row, column = (lax.broadcasted_iota(jnp.int32, square, axis) < HEAD for axis in (0, 1))
-    swap = jnp.where(row != column, 1.0, 0.0).astype(jnp.bfloat16)
+    across = jnp.where(row != column, 1.0, 0.0).astype(jnp.bfloat16)
     g = g_ref[...]
     terms = parts(g.astype(jnp.float32) * out_ref[...].astype(jnp.float32))
-    delta = sum(dot(term, swap) for term in terms)
+    delta = sum(dot(term, across) for term in terms)
     two_heads(grads, g, spread(-delta, jnp.zeros_like(g)))
-    total[...] = jnp.zeros_like(total)
-    for k0, k1, q0, q1, diagonal in plan:
-        rows = k1 - k0
-        left = lanes(rows) < HEAD
-        dks, dvs = ([], [])
+    g_t[...] = g.T
+    q_t[...] = q_ref[...].T
+    dk_t[...] = jnp.zeros_like(dk_t)
+    dv_t[...] = jnp.zeros_like(dv_t)
+    for q0, q1, k0, k1, diagonal in plan:
+        left = lanes(q1 - q0) < HEAD
+        pair = []
         for h in range(2):
-            s = dot(keys[h, k0:k1], queries[h, q0:q1], NT)
-            if diagonal:
-                head = jnp.where(beyond(rows, True), -BIG, s[:, :rows])
-                s = head if q1 - q0 == rows else jnp.concatenate([head, s[:, rows:]], axis=1)
+            s = dot(queries[h, q0:q1], keys[h, k0:k1], NT)
+            s = tail_masked(s, q1 - q0) if diagonal else s
+            pair.append((s, dot(grads[h, q0:q1], values[h, k0:k1], NT)))
+        dqs = []
+        for h, (s, grad_probs) in enumerate(pair):
             probs = jnp.exp2(s * SCALE2)
-            ds = probs * dot(values[h, k0:k1], grads[h, q0:q1], NT)
-            ds = ds.astype(jnp.bfloat16)
-            dvs.append(dot(probs.astype(jnp.bfloat16), g_ref[q0:q1]))
-            dks.append(dot(ds, q_ref[q0:q1]))
-            total[h, q0:q1] += dot(ds, k_ref[k0:k1], TN)
-        dk_ref[k0:k1] = (jnp.where(left, dks[0], dks[1]) * HEAD ** (-0.5)).astype(jnp.bfloat16)
-        dv_ref[k0:k1] = jnp.where(left, dvs[0], dvs[1]).astype(jnp.bfloat16)
-    left = lanes(total.shape[1]) < HEAD
-    dq_ref[...] = (jnp.where(left, total[0], total[1]) * HEAD ** (-0.5)).astype(jnp.bfloat16)
+            ds = (probs * grad_probs).astype(jnp.bfloat16)
+            head = slice(h * HEAD, h * HEAD + HEAD)
+            dv_t[head, k0:k1] += dot(g_t[head, q0:q1], probs.astype(jnp.bfloat16))
+            dk_t[head, k0:k1] += dot(q_t[head, q0:q1], ds)
+            dqs.append(dot(ds, k_ref[k0:k1]))
+        dq_ref[q0:q1] = (jnp.where(left, dqs[0], dqs[1]) * HEAD ** (-0.5)).astype(jnp.bfloat16)
+    dk_ref[...] = (dk_t[...].T * HEAD ** (-0.5)).astype(jnp.bfloat16)
+    dv_ref[...] = dv_t[...].T.astype(jnp.bfloat16)
 
 
 def pair_of_heads(rows):
@@ -575,11 +581,8 @@
     return pl.BlockSpec((rows, 128), lambda i: (0, 0))
 
 
-def plan_cost(plan, model, products):
-    area = sum((q1 - q0) * (k1 - k0) for q0, q1, k0, k1, _ in plan) * model
-    return pl.CostEstimate(
-        flops=8 * area * products, bytes_accessed=1 << 24, transcendentals=area // HEAD
-    )
+def small_cost():
+    return pl.CostEstimate(flops=1 << 10, bytes_accessed=1 << 10, transcendentals=0)
 
 
 def attend(plan, q, k, v, qd, kd):
@@ -592,8 +595,8 @@
         out_specs=[pair_of_heads(nq)] * 2,
         out_shape=[shape] * 2,
         scratch_shapes=[pltpu.VMEM((2, nk, 128), jnp.bfloat16)] * 2,
-        compiler_params=pltpu.CompilerParams(vmem_limit_bytes=48 * 2**20),
-        cost_estimate=plan_cost(plan, model, 2),
+        compiler_params=pltpu.CompilerParams(vmem_limit_bytes=58 * 2**20),
+        cost_estimate=small_cost(),
     )(q, k, v, qd, kd)
 
 
@@ -617,28 +620,23 @@
         out_shape=[jax.ShapeDtypeStruct(shape, jnp.bfloat16) for shape in shapes],
         scratch_shapes=[pltpu.VMEM((2, nk, 128), jnp.bfloat16)] * 2
         + [pltpu.VMEM((2, nq, 128), jnp.bfloat16)] * 2
-        + [pltpu.VMEM((2, nq, 128), jnp.float32)],
-        compiler_params=pltpu.CompilerParams(vmem_limit_bytes=48 * 2**20),
-        cost_estimate=plan_cost(plan, model, 5),
+        + [pltpu.VMEM((128, nq), jnp.bfloat16)] * 2
+        + [pltpu.VMEM((128, nk), jnp.float32)] * 2,
+        compiler_params=pltpu.CompilerParams(vmem_limit_bytes=58 * 2**20),
+        cost_estimate=small_cost(),
     )(q, k, v, extra, kd, out, g)
     return outs[0] if together else outs
 
 
-def self_plan(first, total, tile, back):
-    plan = []
-    for low, high in ((0, first), (first, total)):
-        for start in range(low, high, tile):
-            end = start + tile
-            plan.append((start, end, start, high, True) if back else (start, end, low, end, True))
-    return plan
-
-
-def cross_plan(first, total, reach, source, tile, back):
-    if back:
-        return [
-            (start, start + tile, 0 if start < reach else first, total, False)
-            for start in range(0, source, tile)
-        ]
+def self_plan(first, total, tile):
+    return [
+        (start, start + tile, low, start + tile, True)
+        for low, high in ((0, first), (first, total))
+        for start in range(low, high, tile)
+    ]
+
+
+def cross_plan(first, total, reach, source, tile):
     return [
         (start, start + tile, 0, reach if start < first else source, False)
         for start in range(0, total, tile)
@@ -689,7 +687,7 @@
 
 
 def found_rows(count):
-    return pl.BlockSpec((count, MODEL), lambda i, held: (held[i], 0))
+    return pl.BlockSpec((count, MODEL), lambda i, held, *_: (held[i], 0))
 
 
 def sums_out():
@@ -717,11 +715,6 @@
     each = grad * norm_ref[k : k + 1]
     inner = each - jnp.mean(each, axis=-1, keepdims=True)
     inner = inner - hat * jnp.mean(each * hat, axis=-1, keepdims=True)
-
-    @pl.when(pl.program_id(0) == 0)
-    def _():
-        sums_ref[...] = jnp.zeros_like(sums_ref)
-
     sums_ref[0:1] += jnp.sum(grad * hat, axis=0, keepdims=True)
     sums_ref[1:2] += jnp.sum(grad, axis=0, keepdims=True)
     return scale * inner
@@ -740,7 +733,7 @@
         out_shape=out_shape,
         input_output_aliases=aliases or {},
         compiler_params=pltpu.CompilerParams(vmem_limit_bytes=58 * 2**20),
-        cost_estimate=pl.CostEstimate(flops=flops, bytes_accessed=1 << 24, transcendentals=0),
+        cost_estimate=small_cost(),
     )
 
 
@@ -836,21 +829,40 @@
     )(held, mixed, tokens, norms, weights, weights)
 
 
-def before_feed_kernel(mixed_ref, base_ref, norm_ref, wo, after_ref, third_ref):
+def before_feed_kernel(
+    held, mixed_ref, base_ref, own_ref, other_ref, norm_ref, wo, after_ref, third_ref, grad_ref
+):
     after = base_ref[...] + dot(mixed_ref[...], gathered(wo))
     after_ref[...] = after
     third_ref[...] = norm_of(after, norm_ref, 2)
-
-
-def before_feed(mixed, base, norms, weights, width):
+    own = held[pl.program_id(0)] < 2
+
+    @pl.when(own)
+    def _():
+        grad_ref[...] = own_ref[...]
+
+    @pl.when(jnp.logical_not(own))
+    def _():
+        grad_ref[...] = other_ref[...]
+
+
+def before_feed(held, mixed, base, own, other, norms, weights, width):
     return call(
         before_feed_kernel,
         (mixed.shape[0] // width,),
-        [by_rows(width), by_rows(width), norm_rows(), weight_at(7)],
-        [by_rows(width)] * 2,
-        [struct(mixed.shape, kind) for kind in (jnp.float32, jnp.bfloat16)],
+        [
+            by_rows(width),
+            by_rows(width),
+            pl.BlockSpec((width, MODEL), lambda i, held: (jnp.minimum(held[i], 1), 0)),
+            pl.BlockSpec((width, MODEL), lambda i, held: (jnp.maximum(held[i] - 2, 0), 0)),
+            norm_rows(),
+            weight_at(7),
+        ],
+        [by_rows(width)] * 3,
+        [struct(mixed.shape, kind) for kind in (jnp.float32, jnp.bfloat16, jnp.bfloat16)],
         2 * mixed.size * MODEL,
-    )(mixed, base, norms, weights)
+        prefetch=1,
+    )(held, mixed, base, own, other, norms, weights)
 
 
 def gelu_terms(hidden):
@@ -863,22 +875,31 @@
     return (jnp.where(hidden < 0, tail, 1.0 - tail), bell * (1.0 / math.sqrt(2.0 * math.pi)))
 
 
-def deal(place_ref, turned, keep_ref, send_ref, value, core, x, y, index, lead=()):
-    rel_x = jnp.bitwise_xor(place_ref[1], x)
-    rel_y = jnp.bitwise_xor(place_ref[2], y)
-    spot = (rel_y, rel_x) if turned else (rel_x, rel_y)
-
-    @pl.when(place_ref[0] == core)
-    def _():
-        keep_ref[spot + index] = value
-
-    @pl.when(place_ref[0] != core)
-    def _():
-        send_ref[spot + index] = value
+def deal(place_ref, turned, keep_ref, send_ref, pieces):
+    for own in range(2):
+
+        @pl.when(place_ref[0] == own)
+        def _(own=own):
+            for core, x, y, index, value in pieces:
+                rel_x = jnp.bitwise_xor(place_ref[1], x)
+                rel_y = jnp.bitwise_xor(place_ref[2], y)
+                spot = (rel_y, rel_x) if turned else (rel_x, rel_y)
+                ref = keep_ref if core == own else send_ref
+                ref[spot + index] = value
+
+
+def shard_pieces(product, slot, *rest):
+    pieces = []
+    for owner in range(16):
+        for y in range(2):
+            start = owner * 64 + y * 32
+            index = (owner // 4, slot) + rest
+            value = short(product[start : start + 32])
+            pieces.append((owner % 2, owner // 2 % 2, y, index, value))
+    return pieces
 
 
 def feed_kernel(
-    turned,
     place_ref,
     third_ref,
     grad_ref,
@@ -886,8 +907,10 @@
     wout_ref,
     out_ref,
     back_ref,
-    keep_ref,
-    send_ref,
+    keep_a,
+    send_a,
+    keep_b,
+    send_b,
     third_t,
     active_ref,
     hidden_ref,
@@ -923,46 +946,42 @@
         ready = following
     grad_out = short(dot(active_ref[...], grad_ref[...], TN))
     grad_in = short(dot(third_t[...], hidden_ref[...]))
+    turn = lax.rem(step, 4)
+    side = pl.ds(pl.multiple_of(lax.rem(turn, 2) * TILE, TILE), TILE)
+    pieces = shard_pieces(grad_in, turn // 2, slice(None), side)
     for owner in range(4):
         for y in range(2):
-            start = owner * 128 + y * 64
             for half in range(2):
-                value = grad_out[start + 32 * half : start + 32 * half + 32]
-                deal(
-                    place_ref, turned, keep_ref, send_ref, value,
-                    owner % 2, owner // 2, y, (step, 2 + half),
-                )
-    for owner in range(16):
-        for y in range(2):
-            start = owner * 64 + y * 32
-            for side in range(2):
-
-                @pl.when(step % 2 == side)
-                def _(start=start, owner=owner, y=y, side=side):
-                    deal(
-                        place_ref, turned, keep_ref, send_ref, grad_in[start : start + 32],
-                        owner % 2, owner // 2 % 2, y,
-                        (owner // 4, step // 2, slice(None), slice(side * TILE, side * TILE + TILE)),
-                    )
-
-
-def feed(place, third, grad, weights, lot, turned):
+                start = owner * 128 + y * 64 + 32 * half
+                value = grad_out[start : start + 32]
+                pieces.append((owner % 2, owner // 2, y, (turn, 2 + half), value))
+
+    @pl.when(step < 4)
+    def _():
+        deal(place_ref, False, keep_a, send_a, pieces)
+
+    @pl.when(step >= 4)
+    def _():
+        deal(place_ref, True, keep_b, send_b, pieces)
+
+
+def feed(place, third, grad, weights):
     rows = third.shape[0]
     full = struct((rows, MODEL), jnp.float32)
     buffer = struct((2, 2, 4, 4, 32, MODEL), jnp.bfloat16)
-    return call(
-        functools.partial(feed_kernel, turned),
-        (4,),
+    out, back, *lots = call(
+        feed_kernel,
+        (8,),
         [
             once((rows, MODEL), lambda t, place: (0, 0)),
             once((rows, MODEL), lambda t, place: (0, 0)),
-            pl.BlockSpec((16, 64, TILE), lambda t, place: (0, 2 * lot + t // 2, t % 2)),
-            pl.BlockSpec((4, 128, MODEL), lambda t, place: (t, 2 + lot, 0)),
+            pl.BlockSpec((16, 64, TILE), lambda t, place: (0, t // 2, t % 2)),
+            pl.BlockSpec((4, 128, MODEL), lambda t, place: (t % 4, 2 + t // 4, 0)),
         ],
         [once((rows, MODEL), lambda t, place: (0, 0))] * 2
-        + [once(buffer.shape, lambda t, place: (0, 0, 0, 0, 0, 0))] * 2,
-        [full, full, buffer, buffer],
-        12 * rows * MODEL * 2048,
+        + [once(buffer.shape, lambda t, place: (0, 0, 0, 0, 0, 0))] * 4,
+        [full, full] + [buffer] * 4,
+        24 * rows * MODEL * 2048,
         scratch=[
             pltpu.VMEM((MODEL, rows), jnp.bfloat16),
             pltpu.VMEM((rows, TILE), jnp.bfloat16),
@@ -970,157 +989,211 @@
         ],
         prefetch=1,
     )(place, third, grad, weights, weights)
+    return out, back, lots[:2], lots[2:]
+
+
+def clear(*refs):
+    @pl.when(pl.program_id(0) == 0)
+    def _():
+        for ref in refs:
+            ref[...] = jnp.zeros_like(ref)
+
+
+def add_product(total_ref, left, right):
+    total_ref[...] += dot(left, right, TN)
+
+
+def at_end(store):
+    pl.when(pl.program_id(0) == pl.num_programs(0) - 1)(store)
+
+
+def buffer_of(slots):
+    return struct((2, 2, 4, slots, 32, MODEL), jnp.bfloat16)
+
+
+def slots_at(slots):
+    return once((2, 2, 4, slots, 32, MODEL), lambda *_: (0,) * 6)
 
 
 def after_feed_kernel(
     held,
+    place,
     after_ref,
-    out_a,
-    out_b,
-    back_a,
-    back_b,
+    out_ref,
+    back_ref,
     grad_ref,
+    cross_ref,
     norm_ref,
     wo,
     result_ref,
     total_ref,
-    branch_ref,
     mixed_ref,
     sums_ref,
+    keep_ref,
+    send_ref,
+    weight_ref,
 ):
+    clear(sums_ref, weight_ref)
     after = after_ref[...]
-    result_ref[...] = short(after + out_a[...] + out_b[...])
-    part = norm_back(after, back_a[...] + back_b[...], norm_ref, 2, sums_ref)
+    result_ref[...] = short(after + out_ref[...])
+    part = norm_back(after, back_ref[...], norm_ref, 2, sums_ref)
     total = wide(grad_ref[...]) + part
     total_ref[...] = total
     branch = short(total)
-    branch_ref[...] = branch
     mixed_ref[...] = short(dot(branch, gathered(wo), NT))
-
-
-def after_feed(held, after, outs, backs, grad, norms, weights, width):
+    add_product(weight_ref, cross_ref[...], branch)
+    at_end(lambda: deal(place, False, keep_ref, send_ref, shard_pieces(weight_ref, 0)))
+
+
+def after_feed(held, place, after, out, back, grad, mixed, norms, weights, width):
     narrow = struct(after.shape, jnp.bfloat16)
+    full = struct(after.shape, jnp.float32)
     return call(
         after_feed_kernel,
         (after.shape[0] // width,),
-        [by_rows(width)] * 6 + [norm_rows(), weight_at(7)],
-        [found_rows(width)] + [by_rows(width)] * 3 + [sums_out()],
-        [narrow, struct(after.shape, jnp.float32), narrow, narrow, struct((8, MODEL), jnp.float32)],
-        2 * after.size * MODEL,
-        prefetch=1,
-    )(held, after, *outs, *backs, grad, norms, weights)
+        [by_rows(width)] * 5 + [norm_rows(), weight_at(7)],
+        [found_rows(width)] + [by_rows(width)] * 2 + [sums_out()] + [slots_at(1)] * 2,
+        [narrow, full, narrow, struct((8, MODEL), jnp.float32)] + [buffer_of(1)] * 2,
+        4 * after.size * MODEL,
+        scratch=[pltpu.VMEM((MODEL, MODEL), jnp.float32)],
+        prefetch=2,
+    )(held, place, after, out, back, grad, mixed, norms, weights)
 
 
 def middle_kernel(
+    place,
     grad_ref,
+    second_ref,
     after_ref,
     base_ref,
+    self_ref,
     norm_ref,
     wq,
     wo,
-    total_ref,
-    branch_ref,
-    mixed_ref,
-    sums_ref,
+    *refs,
 ):
-    grad = dot(grad_ref[...], gathered(wq), NT)
+    total_ref, mixed_ref, sums_ref, keep_ref, send_ref, weight_q, weight_o = refs
+    clear(sums_ref, weight_q, weight_o)
+    grad_q = grad_ref[...]
+    grad = dot(grad_q, gathered(wq), NT)
+    add_product(weight_q, second_ref[...], grad_q)
     total = base_ref[...] + norm_back(after_ref[...], grad, norm_ref, 1, sums_ref)
     total_ref[...] = total
     branch = short(total)
-    branch_ref[...] = branch
     mixed_ref[...] = short(dot(branch, gathered(wo), NT))
-
-
-def middle(grad, after, base, norms, weights, width):
+    add_product(weight_o, self_ref[...], branch)
+
+    @at_end
+    def _():
+        deal(place, False, keep_ref, send_ref, shard_pieces(weight_q, 0))
+        deal(place, False, keep_ref, send_ref, shard_pieces(weight_o, 1))
+
+
+def middle(place, grad, second, after, base, mixed, norms, weights, width):
     narrow = struct(after.shape, jnp.bfloat16)
     return call(
         middle_kernel,
         (after.shape[0] // width,),
-        [by_rows(width)] * 3 + [norm_rows(), weight_at(4), weight_at(3)],
-        [by_rows(width)] * 3 + [sums_out()],
-        [struct(after.shape, jnp.float32), narrow, narrow, struct((8, MODEL), jnp.float32)],
-        4 * after.size * MODEL,
-    )(grad, after, base, norms, weights, weights)
+        [by_rows(width)] * 5 + [norm_rows(), weight_at(4), weight_at(3)],
+        [by_rows(width)] * 2 + [sums_out()] + [slots_at(2)] * 2,
+        [struct(after.shape, jnp.float32), narrow, struct((8, MODEL), jnp.float32)]
+        + [buffer_of(2)] * 2,
+        8 * after.size * MODEL,
+        scratch=[pltpu.VMEM((MODEL, MODEL), jnp.float32)] * 2,
+        prefetch=1,
+    )(place, grad, second, after, base, mixed, norms, weights, weights)
 
 
 def finish_kernel(
-    held, grads_ref, tokens_ref, base_ref, norm_ref, wq, wk, wv, result_ref, sums_ref
+    held,
+    place,
+    grads_ref,
+    first_ref,
+    tokens_ref,
+    base_ref,
+    norm_ref,
+    wq,
+    wk,
+    wv,
+    result_ref,
+    sums_ref,
+    keep_ref,
+    send_ref,
+    weight_ref,
 ):
+    clear(sums_ref, weight_ref)
     grad = sum(dot(grads_ref[i], gathered(w), NT) for i, w in enumerate((wq, wk, wv)))
     part = norm_back(wide(tokens_ref[...]), grad, norm_ref, 0, sums_ref)
     result_ref[...] = short(base_ref[...] + part)
-
-
-def finish(held, grads, tokens, base, norms, weights, width):
+    first = first_ref[...].T
+    for i in range(3):
+        weight_ref[i] += dot(first, grads_ref[i])
+
+    @at_end
+    def _():
+        for i in range(3):
+            deal(place, False, keep_ref, send_ref, shard_pieces(weight_ref.at[i], i))
+
+
+def finish(held, place, grads, first, tokens, base, norms, weights, width):
     return call(
         finish_kernel,
         (base.shape[0] // width,),
         [
-            pl.BlockSpec((3, width, MODEL), lambda i, held: (0, i, 0)),
+            pl.BlockSpec((3, width, MODEL), lambda i, *_: (0, i, 0)),
+            by_rows(width),
             found_rows(width),
             by_rows(width),
             norm_rows(),
         ]
         + [weight_at(i) for i in range(3)],
-        [found_rows(width), sums_out()],
-        [struct(base.shape, jnp.bfloat16), struct((8, MODEL), jnp.float32)],
-        6 * base.size * MODEL,
-        prefetch=1,
-    )(held, grads, tokens, base, norms, weights, weights, weights)
-
-
-def source_back_kernel(grads_ref, wk, wv, out_ref):
+        [found_rows(width), sums_out()] + [slots_at(3)] * 2,
+        [struct(base.shape, jnp.bfloat16), struct((8, MODEL), jnp.float32)]
+        + [buffer_of(3)] * 2,
+        12 * base.size * MODEL,
+        scratch=[pltpu.VMEM((3, MODEL, MODEL), jnp.float32)],
+        prefetch=2,
+    )(held, place, grads, first, tokens, base, norms, weights, weights, weights)
+
+
+def source_back_kernel(
+    place, grads_ref, source_ref, wk, wv, out_ref, keep_ref, send_ref, weight_ref
+):
+    clear(weight_ref)
+    source = source_ref[...].T
+    for i in range(2):
+        weight_ref[i] += dot(source, grads_ref[i])
     grad = dot(grads_ref[0], gathered(wk), NT) + dot(grads_ref[1], gathered(wv), NT)
     out_ref[...] = short(grad)
 
-
-def source_back(grads, weights, width):
+    @at_end
+    def _():
+        for i in range(2):
+            deal(place, False, keep_ref, send_ref, shard_pieces(weight_ref.at[i], i))
+
+
+def source_back(place, grads, source, weights, width):
     rows = grads.shape[1]
     return call(
         source_back_kernel,
         (rows // width,),
-        [pl.BlockSpec((2, width, MODEL), lambda i: (0, i, 0)), weight_at(5), weight_at(6)],
-        [by_rows(width)],
-        [struct((rows, MODEL), jnp.bfloat16)],
-        4 * rows * MODEL * MODEL,
-    )(grads, weights, weights)[0]
-
-
-def weight_grad_kernel(turned, place_ref, left_ref, right_ref, *refs):
-    keep_ref, send_ref = refs[-2:]
-    right = right_ref[0] if len(right_ref.shape) == 3 else right_ref[...]
-    product = short(dot(left_ref[...], right, TN))
-    for owner in range(TILE // 64):
-        for y in range(2):
-            start = owner * 64 + y * 32
-            deal(
-                place_ref, turned, keep_ref, send_ref, product[start : start + 32],
-                owner % 2, owner // 2 % 2, y, (owner // 4, 0),
+        [
+            pl.BlockSpec((2, width, MODEL), lambda i, *_: (0, i, 0)),
+            by_rows(width),
+            weight_at(5),
+            weight_at(6),
+        ],
+        [
+            pl.BlockSpec(
+                (width, MODEL), lambda i, place: (jnp.bitwise_xor(i, place[2]), 0)
             )
-
-
-def weight_grad(place, left, right, turned, held=None, slot=0, slots=1):
-    rows = left.shape[0]
-    several = right.ndim == 3
-    count = right.shape[0] if several else 1
-    shape = struct((2, 2, 4, slots, 32, MODEL), jnp.bfloat16)
-    held = () if held is None else tuple(held)
-    return call(
-        functools.partial(weight_grad_kernel, turned),
-        (count, MODEL // TILE),
-        [
-            pl.BlockSpec((rows, TILE), lambda n, t, place: (0, t)),
-            pl.BlockSpec((1, rows, MODEL), lambda n, t, place: (n, 0, 0))
-            if several
-            else pl.BlockSpec((rows, MODEL), lambda n, t, place: (0, 0)),
         ]
-        + [pl.BlockSpec(memory_space=pl.ANY)] * len(held),
-        [pl.BlockSpec((2, 2, 2, 1, 32, MODEL), lambda n, t, place: (0, 0, t, slot + n, 0, 0))] * 2,
-        [shape] * 2,
-        2 * rows * MODEL * MODEL * count,
+        + [slots_at(2)] * 2,
+        [struct((rows, MODEL), jnp.bfloat16)] + [buffer_of(2)] * 2,
+        8 * rows * MODEL * MODEL,
+        scratch=[pltpu.VMEM((2, MODEL, MODEL), jnp.float32)],
         prefetch=1,
-        aliases={3 + i: i for i in range(len(held))},
-    )(place, left, right, *held)
+    )(place, grads, source, weights, weights)
 
 
 def pairs(bit):
@@ -1131,52 +1204,171 @@
     return lax.ppermute(values, "ctx", [(0, 1), (1, 0)])
 
 
-def reduce_to_owner(keep, send, turned, z):
-    def over_x(values):
-        return lax.ppermute(values, "fsdp", pairs(2))
-
-    one, two = (swap, over_x) if turned else (over_x, swap)
-    core = lax.ppermute(send, "fsdp", pairs(1))
-    first = short(wide(keep[1]) + wide(core[1]))
-    first = yield (first,)
-    first = one(first[0])
-    second = short(wide(keep[0, 1]) + wide(core[0, 1]) + wide(first[1]))
-    second = yield (second,)
-    second = two(second[0])
-
-    def share(index):
-        terms = (keep[0, 0], core[0, 0], first[0], second)
-        return sum(wide(lax.dynamic_index_in_dim(term, index, 0, False)) for term in terms)
-
-    away = yield tuple(short(share((z + hop) % 4)) for hop in range(1, 4))
-    total = share(z)
-    for hop, values in enumerate(away, 1):
-        cycle = [(i, (i + 4 * hop) % 16) for i in range(16)]
-        total = total + wide(lax.ppermute(values, "fsdp", cycle))
-    (total,) = yield (short(total),)
-    other = swap(total)
+def over_x(values):
+    return lax.ppermute(values, "fsdp", pairs(2))
+
+
+def over_core(values):
+    return lax.ppermute(values, "fsdp", pairs(1))
+
+
+def tie(*values):
+    return lax.optimization_barrier(values)
+
+
+def lot_specs(lot, first, second, spread, z_of, depth=1):
+    specs = []
+    for keep, _ in lot:
+        slots, rows = keep.shape[3:5]
+        block = (1, spread, depth, slots, rows, MODEL)
+        specs += [
+            pl.BlockSpec(block, lambda i, place: (first, second, z_of(i, place), 0, 0, 0))
+        ] * 2
+    return specs
+
+
+def slots_of(lot):
+    return sum(keep.shape[3] for keep, _ in lot)
+
+
+def in_order(i, place):
+    return i
+
+
+def from_own(i, place):
+    return lax.rem(place[3] + i, 4)
+
+
+def pair_sums(refs, count):
+    return [wide(refs[2 * i][...]) + wide(refs[2 * i + 1][...]) for i in range(count)]
+
+
+def depth_of(lots):
+    return 4 if sum(slots_of(lot) for lot in lots) < 4 else 1
+
+
+def first_sums(place, lots):
+    def kernel(place_ref, *refs):
+        refs = list(refs)
+        outs = refs[-len(lots) :]
+        for lot, out in zip(lots, outs):
+            start = 0
+            for value in pair_sums([refs.pop(0) for _ in range(2 * len(lot))], len(lot)):
+                end = start + value.shape[3]
+                out[:, :, start:end] = short(value[0])
+                start = end
+
+    depth = depth_of(lots)
+    specs = [spec for lot in lots for spec in lot_specs(lot, 1, 0, 2, in_order, depth)]
+    shapes = [(2, 4, slots_of(lot), 32, MODEL) for lot in lots]
+    return call(
+        kernel,
+        (4 // depth,),
+        specs,
+        [
+            pl.BlockSpec((2, depth) + shape[2:], lambda i, place: (0, i, 0, 0, 0))
+            for shape in shapes
+        ],
+        [struct(shape, jnp.bfloat16) for shape in shapes],
+        1 << 20,
+        prefetch=1,
+    )(place, *[array for lot in lots for pair in lot for array in pair])
+
+
+def second_sums(place, lots, firsts):
+    def kernel(place_ref, *refs):
+        refs = list(refs)
+        outs = refs[-len(lots) :]
+        for lot, out in zip(lots, outs):
+            sources = [refs.pop(0) for _ in range(2 * len(lot))]
+            received = refs.pop(0)
+            start = 0
+            for value in pair_sums(sources, len(lot)):
+                end = start + value.shape[3]
+                out[:, start:end] = short(value[0, 0] + wide(received[0, :, start:end]))
+                start = end
+
+    depth = depth_of(lots)
+    specs, shapes, arrays = ([], [], [])
+    for lot, first in zip(lots, firsts):
+        specs += lot_specs(lot, 0, 1, 1, in_order, depth)
+        specs.append(
+            pl.BlockSpec((1, depth) + first.shape[2:], lambda i, place: (1, i, 0, 0, 0))
+        )
+        shapes.append(first.shape[1:])
+        arrays += [array for pair in lot for array in pair] + [first]
+    return call(
+        kernel,
+        (4 // depth,),
+        specs,
+        [pl.BlockSpec((depth,) + shape[1:], lambda i, place: (i, 0, 0, 0)) for shape in shapes],
+        [struct(shape, jnp.bfloat16) for shape in shapes],
+        1 << 20,
+        prefetch=1,
+    )(place, *arrays)
+
+
+def third_sums(place, lots, firsts, seconds):
+    def kernel(place_ref, *refs):
+        refs = list(refs)
+        outs = refs[-4:]
+        start = 0
+        for lot in lots:
+            sources = [refs.pop(0) for _ in range(2 * len(lot))]
+            received = wide(refs.pop(0)[0, 0]) + wide(refs.pop(0)[0])
+            spot = 0
+            for value in pair_sums(sources, len(lot)):
+                count = value.shape[3]
+                total = value[0, 0, 0] + received[spot : spot + count]
+                for hop in range(4):
+
+                    @pl.when(pl.program_id(0) == hop)
+                    def _(out=outs[hop], total=total, start=start, end=start + count):
+                        out[start:end] = total.astype(out.dtype)
+
+                start, spot = (start + count, spot + count)
+
+    specs, arrays = ([], [])
+    for lot, first, second in zip(lots, firsts, seconds):
+        specs += lot_specs(lot, 0, 0, 1, from_own)
+        specs.append(
+            pl.BlockSpec(
+                (1, 1) + first.shape[2:], lambda i, place: (0, from_own(i, place), 0, 0, 0)
+            )
+        )
+        specs.append(
+            pl.BlockSpec(
+                (1,) + second.shape[1:], lambda i, place: (from_own(i, place), 0, 0, 0)
+            )
+        )
+        arrays += [array for pair in lot for array in pair] + [first, second]
+    shape = (sum(slots_of(lot) for lot in lots), 32, MODEL)
+    return call(
+        kernel,
+        (4,),
+        specs,
+        [once(shape, lambda i, place: (0, 0, 0)) for _ in range(4)],
+        [struct(shape, jnp.bfloat16 if hop else jnp.float32) for hop in range(4)],
+        1 << 20,
+        prefetch=1,
+    )(place, *arrays)
+
+
+def cycled(hop, values):
+    return lax.ppermute(values, "fsdp", [(i, (i + 4 * hop) % 16) for i in range(16)])
+
+
+def over_z(shares):
+    return [shares[0]] + [cycled(hop, shares[hop]) for hop in range(1, 4)]
+
+
+def whole(shares):
+    return short(shares[0] + sum(wide(share) for share in shares[1:]))
+
+
+def both_parts(total, other):
     low = lax.axis_index("ctx") == 0
-    yield (
-        wide(jnp.stack([jnp.where(low, total, other), jnp.where(low, other, total)], axis=1)),
-    )
-
-
-class Steps:
-    def __init__(self, steps):
-        self.steps = steps
-        self.held = next(steps)
-
-    def advance(self):
-        self.held = self.steps.send(self.held)
-
-
-def before(value, *transfers):
-    flat = tuple(item for transfer in transfers for item in transfer.held)
-    value, *flat = lax.optimization_barrier((value,) + flat)
-    for transfer in transfers:
-        count = len(transfer.held)
-        transfer.held, flat = (tuple(flat[:count]), flat[count:])
-    return value
+    return wide(jnp.stack([jnp.where(low, total, other), jnp.where(low, other, total)], axis=1))
 
 
 def columns(shares, start, stop):
@@ -1189,10 +1381,6 @@
     inner = jnp.stack(inner, axis=2).reshape(64, 4 * MODEL)
     outer = [lot[2:].transpose(1, 0, 2, 3).reshape(128, MODEL) for lot in lots]
     return inner, jnp.concatenate(outer)
-
-
-def after_all(value, *others):
-    return lax.optimization_barrier((value,) + others)[0]
 
 
 def whole_packs(mesh):
@@ -1223,7 +1411,7 @@
     mine = lax.axis_index("ctx")
     spot = lax.axis_index("fsdp")
     z = spot // 4
-    place = jnp.stack([spot % 2, spot // 2 % 2, mine]).astype(jnp.int32)
+    place = jnp.stack([spot % 2, spot // 2 % 2, mine, z]).astype(jnp.int32)
     part = self_project.shape[0]
 
     norms = jnp.pad(jnp.concatenate([norm_gain, norm_bias]), ((0, 10), (0, MODEL - part)))
@@ -1248,17 +1436,10 @@
         low = mine == 0
         return jnp.stack([jnp.where(low, own, other), jnp.where(low, other, own)])[:, None]
 
-    def to_slots(halves):
-        return from_both(halves[:rows], swap(halves[rows:]))
-
     halves = jnp.concatenate(both_halves(tokens))
     own, other = both_halves(encoded)
     source = jnp.concatenate([jnp.where(mine == 0, own, other), jnp.where(mine == 0, other, own)])
-    grad_out = jnp.concatenate(both_halves(cotangent))
-    feed_shard = after_all(feed_shard, halves, source, grad_out)
-    grad_out = jnp.concatenate(
-        [lax.dynamic_slice_in_dim(grad_out, held[p] * width, width) for p in range(4)]
-    )
+    feed_shard, halves, source = tie(feed_shard, halves, source)
     feed_weights = lax.all_gather(feed_shard, "fsdp", axis=0)
 
     lengths = lax.dynamic_index_in_dim(target_lengths, mine, 0, False)[0]
@@ -1272,31 +1453,31 @@
     reach = source_rows // 2
 
     first, query, keys, values = enter(held, halves, norms, weights, width)
-    plan = self_plan(first_rows, pack_rows, width, False)
+    query, cotangent = tie(query, cotangent)
+    cotangents = both_halves(cotangent)
+    plan = self_plan(first_rows, pack_rows, width)
     self_mixed, self_extra = attend(plan, query, keys, values, marks, target_marks)
+    self_mixed, source = tie(self_mixed, source)
     cross_keys, cross_values = source_pairs(source, weights, source_rows // 2)
     after_self, second, cross_queries = between(held, self_mixed, halves, norms, weights, width)
-    plan = cross_plan(first_rows, pack_rows, reach, source_rows, width, False)
+    plan = cross_plan(first_rows, pack_rows, reach, source_rows, width // 2)
     cross_mixed, cross_extra = attend(
         plan, cross_queries, cross_keys, cross_values, marks, source_marks
     )
-    after_cross, third = before_feed(cross_mixed, after_self, norms, weights, width)
-
-    out_a, back_a, *sent = feed(place, third, grad_out, feed_weights, 0, False)
-    first_lot = Steps(reduce_to_owner(*sent, False, z))
-    out_b, back_b, *sent = feed(place, after_all(third, *sent), grad_out, feed_weights, 1, True)
-    second_lot = Steps(reduce_to_owner(*sent, True, z))
-    after_cross = before(after_cross, first_lot)
-    result, grad_after_cross, cross_branch, grad_cross_mixed, sums_two = after_feed(
-        held, after_cross, (out_a, out_b), (back_a, back_b), grad_out, norms, weights, width
-    )
-    result = to_slots(result)
-
-    first_lot.advance()
-    others = weight_grad(place, cross_mixed, cross_branch, False, slots=5)
-    grad_cross_mixed = before(after_all(grad_cross_mixed, *others), second_lot)
-    second_lot.advance()
-    plan = cross_plan(first_rows, pack_rows, reach, source_rows, source_rows // 4, True)
+    after_cross, third, grad_out = before_feed(
+        held, cross_mixed, after_self, *cotangents, norms, weights, width
+    )
+
+    out, back, lot_a, lot_b = feed(place, third, grad_out, feed_weights)
+    lot_a, lot_b = ([(lot[0], over_core(lot[1]))] for lot in (lot_a, lot_b))
+    result, grad_after_cross, grad_cross_mixed, sums_two, *part_out = after_feed(
+        held, place, after_cross, out, back, grad_out, cross_mixed, norms, weights, width
+    )
+    first_ab = first_sums(place, [lot_a, lot_b])
+    grad_cross_mixed, part_out[1], *first_ab = tie(grad_cross_mixed, part_out[1], *first_ab)
+    first_ab = (over_x(first_ab[0]), swap(first_ab[1]))
+    part_out[1] = over_core(part_out[1])
+    plan = cross_plan(first_rows, pack_rows, reach, source_rows, width)
     grad_cross_queries, grad_source = attend_back(
         plan,
         cross_queries,
@@ -1308,29 +1489,38 @@
         grad_cross_mixed,
         False,
     )
-    grad_source = before(grad_source, first_lot, second_lot)
-    first_lot.advance()
-    second_lot.advance()
-    others = weight_grad(place, source, grad_source, False, others, 1, 5)
-    others = weight_grad(
-        place, second, after_all(grad_cross_queries, *others), False, others, 3, 5
-    )
-    grad_after_self, self_branch, grad_self_mixed, sums_one = middle(
-        grad_cross_queries, after_self, grad_after_cross, norms, weights, width
-    )
-    others = weight_grad(place, self_mixed, self_branch, False, others, 4, 5)
-    other_weights = Steps(reduce_to_owner(*others, False, z))
-    grad_encoded = source_back(after_all(grad_source, *others), weights, source_rows // 2)
-    grad_self_mixed = after_all(grad_self_mixed, grad_encoded)
-    grad_self_mixed = before(grad_self_mixed, first_lot, second_lot, other_weights)
-    low, high = (grad_encoded[:reach], grad_encoded[reach:])
-    grad_encoded = from_both(
-        jnp.where(mine == 0, low, high), swap(jnp.where(mine == 0, high, low))
-    )
-    first_lot.advance()
-    second_lot.advance()
-    other_weights.advance()
-    plan = self_plan(first_rows, pack_rows, width, True)
+    grad_source, part_out[1], *first_ab = tie(grad_source, part_out[1], *first_ab)
+    grad_encoded, *part_source = source_back(place, grad_source, source, weights, source_rows // 2)
+    encoded_own = grad_encoded[: source_rows // 2]
+    away = jnp.concatenate([result[rows:], grad_encoded[source_rows // 2 :]])
+    second_ab = second_sums(place, [lot_a, lot_b], first_ab)
+    grad_cross_queries, encoded_own, away, *second_ab = tie(
+        grad_cross_queries, encoded_own, away, *second_ab
+    )
+    second_ab = (swap(second_ab[0]), over_x(second_ab[1]))
+    grad_after_self, grad_self_mixed, sums_one, *part_middle = middle(
+        place,
+        grad_cross_queries,
+        second,
+        after_self,
+        grad_after_cross,
+        self_mixed,
+        norms,
+        weights,
+        width,
+    )
+    grad_self_mixed, part_source[1], part_middle[1], *second_ab = tie(
+        grad_self_mixed, part_source[1], part_middle[1], *second_ab
+    )
+    part_source[1], part_middle[1] = (over_core(part_source[1]), over_core(part_middle[1]))
+    third_ab = third_sums(place, [lot_a, lot_b], first_ab, second_ab)
+    lot_c = [part_out, part_source, part_middle]
+    (first_c,) = first_sums(place, [lot_c])
+    grad_self_mixed, first_c, away, *third_ab = tie(grad_self_mixed, first_c, away, *third_ab)
+    first_c = over_x(first_c)
+    away = swap(away)
+    third_ab = over_z(third_ab)
+    plan = self_plan(first_rows, pack_rows, width)
     grads = attend_back(
         plan,
         query,
@@ -1342,40 +1532,61 @@
         grad_self_mixed,
         True,
     )
-    grads = before(grads, first_lot, second_lot, other_weights)
-    first_lot.advance()
-    second_lot.advance()
-    other_weights.advance()
-    project = weight_grad(place, first, grads, True, slots=3)
-    last = Steps(reduce_to_owner(*project, True, z))
-    feed_in_grad, feed_out_grad = feed_shares((first_lot.held[0], second_lot.held[0]))
-    grads = before(after_all(grads, feed_in_grad, feed_out_grad), last)
-    last.advance()
-    grad_tokens, sums_zero = finish(
-        held, grads, halves, grad_after_self, norms, weights, width
-    )
-    grad_tokens = to_slots(grad_tokens)
-
+    grads, first_c, away, *third_ab = tie(grads, first_c, away, *third_ab)
+    (second_c,) = second_sums(place, [lot_c], [first_c])
+    total_ab = whole(third_ab)
+    grads, second_c, total_ab = tie(grads, second_c, total_ab)
+    second_c, other_ab = (swap(second_c), swap(total_ab))
+    grad_tokens, sums_zero, *lot_d = finish(
+        held, place, grads, first, halves, grad_after_self, norms, weights, width
+    )
+    grad_tokens, sums_zero, second_c, other_ab, *lot_d = tie(
+        grad_tokens, sums_zero, second_c, other_ab, *lot_d
+    )
     sums = jnp.concatenate([sums_zero[:2], sums_one[:2], sums_two[:2]])
-    for bit in (1, 2, 4, 8):
+    lot_d = [(lot_d[0], over_core(lot_d[1]))]
+    third_c = third_sums(place, [lot_c], [first_c], [second_c])
+    (first_d,) = first_sums(place, [lot_d])
+    first_d, grad_tokens, result, encoded_own, away, sums, *third_c = tie(
+        first_d, grad_tokens, result, encoded_own, away, sums, *third_c
+    )
+    first_d = over_x(first_d)
+    tokens_other = swap(grad_tokens[rows:])
+    third_c = over_z(third_c)
+    share_ab = both_parts(total_ab, other_ab)
+    feed_in_grad, feed_out_grad = feed_shares((share_ab[:4], share_ab[4:]))
+    result = from_both(result[:rows], away[:rows])
+    grad_encoded = from_both(encoded_own, away[rows:])
+    sums = sums + over_core(sums)
+    total_c = whole(third_c)
+    (second_d,) = second_sums(place, [lot_d], [first_d])
+    second_d, total_c, sums, result, grad_encoded, feed_in_grad, feed_out_grad = tie(
+        second_d, total_c, sums, result, grad_encoded, feed_in_grad, feed_out_grad
+    )
+    second_d = swap(second_d)
+    for bit in (4, 8):
         sums = sums + lax.ppermute(sums, "fsdp", pairs(bit))
+    third_d = third_sums(place, [lot_d], [first_d], [second_d])
+    sums, tokens_other, *third_d = tie(sums, tokens_other, *third_d)
+    sums = sums + over_x(sums)
+    total_d = whole(over_z(third_d))
+    total = jnp.concatenate([total_c, total_d])
     sums = sums + swap(sums)
+    share_cd = both_parts(total, swap(total))
+    share_c, share_d = (share_cd[:5], share_cd[5:])
+
     sums = lax.dynamic_slice_in_dim(sums, spot * part, part, 1)
-    for _ in range(2):
-        other_weights.advance()
-    for _ in range(3):
-        last.advance()
-    others_share, project_share = (other_weights.held[0], last.held[0])
+    grad_tokens = from_both(grad_tokens[:rows], tokens_other)
 
     return (
         result,
         grad_tokens,
         grad_encoded,
-        columns(project_share, 0, 3),
-        columns(others_share, 4, 5),
-        columns(others_share, 3, 4),
-        columns(others_share, 1, 3),
-        columns(others_share, 0, 1),
+        columns(share_d, 0, 3),
+        columns(share_c, 4, 5),
+        columns(share_c, 3, 4),
+        columns(share_c, 1, 3),
+        columns(share_c, 0, 1),
         feed_in_grad,
         feed_out_grad,
         sums[0::2],

time: 864 us -> 736 us (0.85)
  other arithmetic: 79.4 us -> 32.7 us
  waiting for transfers between devices: 173 us -> 138 us
  starting transfers between devices: 65.1 us -> 38.2 us
  local copies, waits for them, and re-layouts: 46.3 us -> 34 us
    ppermute x15 -> x12, waiting for transfers between devices: 150 us -> 82.4 us  [swap(): return lax.ppermute(values, 'ctx', [(0, 1), (1, 0)])]
    convert_element_type x16 -> x3, other arithmetic: 45.5 us -> 3.47 us  [short(): return values.astype(jnp.bfloat16)]
    ppermute x16, starting transfers between devices: 42.5 us -> 16.7 us  [the longest x9 15.4 us: cycled(): lax.ppermute(values, 'fsdp', [(i, (i + 4 * hop) % 16) for i in range(16)])]
    all_gather x1, waiting for transfers between devices: 0.01 us -> 23.6 us  [whole_pack_body(): weights = lax.all_gather(attention_shard, 'fsdp', axis=0)]
    pallas_call x1, Pallas kernels: 20.5 us -> 36.1 us  [finish(): call(finish_kernel, (base.shape[0] // width,), [pl.BlockSpec((3, width, M...]
    pallas_call x2, Pallas kernels: 110 us -> 94.9 us  [attend_back(): pl.pallas_call(functools.partial(attend_back_kernel, plan), grid=(model /...]
    slice x15 -> x3, local copies, waits for them, and re-layouts: 23.4 us -> 8.14 us  [the longest x2 5.45 us: whole_pack_body(): away = jnp.concatenate([result[rows:], grad_encoded[source_rows // 2:]])]
    pallas_call x9 -> x12, Pallas kernels: 221 us -> 208 us  [the longest x1 113 us: feed(): call(feed_kernel, (8,), [once((rows, MODEL), lambda t, place: (0, 0)), on...]
  transfers between devices with their start and end apart: 41 -> 37, of which waited for: 15 -> 13; matrix products, arithmetic and copies ran while one was open for 13% -> 6% of each run, Pallas kernels for 44% -> 42%
where the time goes in v2:
time: 736 us; the launch traced here: 725 us
  Pallas kernels  467 us (63%)
  waiting for transfers between devices  138 us (19%)
  starting transfers between devices  38.2 us (5%)
  local copies, waits for them, and re-layouts  34 us (5%)
  other arithmetic  32.7 us (4%)
  between operations  14.9 us (2%)
    pallas_call x1, Pallas kernels, feed(): call(feed_kernel, (8,), [once((rows, MODEL), lambda t, place: (0, 0)), on...  113 us
    pallas_call x2, Pallas kernels, attend_back(): pl.pallas_call(functools.partial(attend_back_kernel, plan), grid=(model /...  94.9 us
    ppermute x12, waiting for transfers between devices, swap(): return lax.ppermute(values, 'ctx', [(0, 1), (1, 0)])  82.4 us
    pallas_call x2, Pallas kernels, attend(): pl.pallas_call(functools.partial(attend_kernel, plan), grid=(model // 128...  54.7 us
    pallas_call x1, Pallas kernels, finish(): call(finish_kernel, (base.shape[0] // width,), [pl.BlockSpec((3, width, M...  36.1 us
    pallas_call x1, Pallas kernels, middle(): call(middle_kernel, (after.shape[0] // width,), [by_rows(width)] * 5 + [n...  26.2 us
    all_gather x1, waiting for transfers between devices, whole_pack_body(): weights = lax.all_gather(attention_shard, 'fsdp', axis=0)  23.6 us
    pallas_call x1, Pallas kernels, after_feed(): call(after_feed_kernel, (after.shape[0] // width,), [by_rows(width)] * 5...  20.7 us
  transfers between devices with their start and end apart: 37, of which 13 were waited for; matrix products, arithmetic and copies ran while one was open for 6% of the time, Pallas kernels for 42%

profile of v2, /device:TPU:0, one launch (start us, length us, event | category | flops | bytes accessed | tf_op | source)
XLA Modules:
  0.0 725.0 jit_solution(8349290889443118316)
XLA Ops:
  8.6 3.1 shard_map.246
  11.7 3.5 dynamic-slice_bitcast_fusion.3
  15.2 3.0 collective-permute-start
  19.2 56.1 %collective-permute-done.1 = bf16[512,1024]{1,0:T(8,128)(2,1)} collective-permute-done((bf16[512,1024]{1,0:T(8,128)(2,1)}, bf16[512,1024]{1,0:T(8,128)(2,1)}, u32[]{:S(2)}, u32[]{:S(2)}) %collective-permute-start.1) | collective-permute-done | bytes 1048608 | tf_op jit(solution)/shard_map/ppermute | solution.py:1204
  75.4 1.8 bitcast_select_fusion.1
  77.1 1.5 pad_maximum_fusion.2.source_ref
  78.6 2.0 pad_maximum_fusion.tokens_ref
  82.5 23.6 %all-gather.5.cloned.1.call-done = bf16[8448,1024]{1,0:T(8,128)(2,1)} async-done(((bf16[528,1024]{1,0:T(8,128)(2,1)}), bf16[8448,1024]{1,0:T(8,128)(2,1)}) %all-gather.5.cloned.1.call-update) | async-done | bytes 17301520 | tf_op jit(solution)/shard_map/all_gather | solution.py:1422
  107.5 17.0 %shard_map.247 = (bf16[1536,1024]{1,0:T(8,128)(2,1)}, bf16[1536,1024]{1,0:T(8,128)(2,1)}, bf16[1536,1024]{1,0:T(8,128)(2,1)}, bf16[1536,1024]{1,0:T(8,128)(2,1)}) custom-call(s32[4]{0:T(128)} %compare_select_fusion.3.held, bf16[1536,1024]{1,0:T(8,128)(2,1)} %pad_maximum_fusion.tokens_ref, f32[8,1024]{1,0:T(8,128)} %reshape.150.norm_ref, ...), custom_call_target="tpu_custom_call" | custom-call | flops 1024 | bytes 1024 | tf_op jit(solution)/shard_map/pallas_call | solution.py:784
  131.2 28.0 %shard_map.248 = (bf16[1536,1024]{1,0:T(8,128)(2,1)}, bf16[1536,1024]{1,0:T(8,128)(2,1)}) custom-call(bf16[1536,1024]{1,0:T(8,128)(2,1)} %get-tuple-element.150.q_ref, bf16[1536,1024]{1,0:T(8,128)(2,1)} %get-tuple-element.151.k_ref, bf16[1536,1024]{1,0:T(8,128)(2,1)} %get-tuple-element.152.v_ref, bf16[1536,128]{1,0:T(8,128)(2,1)} %fusion.qd_ref, ...), custom_call_target="tpu_custom_call" | custom-call | flops 1024 | bytes 1024 | tf_op jit(solution)/shard_map/pallas_call | solution.py:591
  159.2 8.4 %shard_map.250 = (bf16[1024,1024]{1,0:T(8,128)(2,1)}, bf16[1024,1024]{1,0:T(8,128)(2,1)}) custom-call(bf16[1024,1024]{1,0:T(8,128)(2,1)} %pad_maximum_fusion.2.source_ref, bf16[16,528,1024]{2,1,0:T(8,128)(2,1)} %bitcast.105, bf16[16,528,1024]{2,1,0:T(8,128)(2,1)} %bitcast.106), custom_call_target="tpu_custom_call" | custom-call | flops 1024 | bytes 1024 | tf_op jit(solution)/shard_map/pallas_call | solution.py:802
  167.6 13.5 %shard_map.249 = (f32[1536,1024]{1,0:T(8,128)}, bf16[1536,1024]{1,0:T(8,128)(2,1)}, bf16[1536,1024]{1,0:T(8,128)(2,1)}) custom-call(s32[4]{0:T(128)} %compare_select_fusion.3.held, bf16[1536,1024]{1,0:T(8,128)(2,1)} %get-tuple-element.156.mixed_ref.self_ref.out_ref, bf16[1536,1024]{1,0:T(8,128)(2,1)} %pad_maximum_fusion.tokens_ref, ...), custom_call_target="tpu_custom_call" | custom-call | flops 1024 | bytes 1024 | tf_op jit(solution)/shard_map/pallas_call | solution.py:821
  181.1 26.7 %shard_map.251 = (bf16[1536,1024]{1,0:T(8,128)(2,1)}, bf16[1536,1024]{1,0:T(8,128)(2,1)}) custom-call(bf16[1536,1024]{1,0:T(8,128)(2,1)} %get-tuple-element.157.q_ref, bf16[1024,1024]{1,0:T(8,128)(2,1)} %get-tuple-element.159.k_ref, bf16[1024,1024]{1,0:T(8,128)(2,1)} %get-tuple-element.160.v_ref, bf16[1536,128]{1,0:T(8,128)(2,1)} %fusion.qd_ref, ...), custom_call_target="tpu_custom_call" | custom-call | flops 1024 | bytes 1024 | tf_op jit(solution)/shard_map/pallas_call | solution.py:591
  209.0 14.0 %shard_map.252 = (f32[1536,1024]{1,0:T(8,128)}, bf16[1536,1024]{1,0:T(8,128)(2,1)}, bf16[1536,1024]{1,0:T(8,128)(2,1)}) custom-call(s32[4]{0:T(128)} %compare_select_fusion.3.held, bf16[1536,1024]{1,0:T(8,128)(2,1)} %get-tuple-element.162.mixed_ref.cross_ref.out_ref, f32[1536,1024]{1,0:T(8,128)} %get-tuple-element.163.base_ref.after_ref, ...), custom_call_target="tpu_custom_call" | custom-call | flops 1024 | bytes 1024 | tf_op jit(solution)/shard_map/pallas_call | solution.py:850
  223.0 113.3 %shard_map.253 = (f32[1536,1024]{1,0:T(8,128)}, f32[1536,1024]{1,0:T(8,128)}, bf16[2,2,4,4,32,1024]{5,4,3,2,1,0:T(8,128)(2,1)}, bf16[2,2,4,4,32,1024]{5,4,3,2,1,...) custom-call(s32[4]{0:T(128)} %pad_add_fusion.place_ref.place, ...), custom_call_target="tpu_custom_call" | custom-call | flops 1024 | bytes 1024 | tf_op jit(solution)/shard_map/pallas_call | solution.py:972
  336.8 20.7 %shard_map.254 = (bf16[1536,1024]{1,0:T(8,128)(2,1)}, f32[1536,1024]{1,0:T(8,128)}, bf16[1536,1024]{1,0:T(8,128)(2,1)}, f32[8,1024]{1,0:T(8,128)}, bf16[2,2,4,1,...) custom-call(s32[4]{0:T(128)} %compare_select_fusion.3.held, s32[4]{0:T(128)} %pad_add_fusion.place_ref.place, ...), custom_call_target="tpu_custom_call" | custom-call | flops 1024 | bytes 1024 | tf_op jit(solution)/shard_map/pallas_call | solution.py:1051
  357.6 1.9 copy-done.2
  359.5 6.7 shard_map.255
  367.1 2.7 slice.95
  369.8 45.2 %shard_map.256 = (bf16[1536,1024]{1,0:T(8,128)(2,1)}, bf16[2,1024,1024]{2,1,0:T(8,128)(2,1)}) custom-call(bf16[1536,1024]{1,0:T(8,128)(2,1)} %get-tuple-element.157.q_ref, bf16[1024,1024]{1,0:T(8,128)(2,1)} %get-tuple-element.159.k_ref, bf16[1024,1024]{1,0:T(8,128)(2,1)} %get-tuple-element.160.v_ref, bf16[1536,1024]{1,0:T(8,128)(2,1)} %get-tuple-element.161.extra_ref, ...), custom_call_target="tpu_custom_call" | custom-call | flops 1024 | bytes 1024 | tf_op jit(solution)/shard_map/pallas_call | solution.py:613
  415.1 17.4 %shard_map.257 = (bf16[1024,1024]{1,0:T(8,128)(2,1)}, bf16[2,2,4,2,32,1024]{5,4,3,2,1,0:T(8,128)(2,1)}, bf16[2,2,4,2,32,1024]{5,4,3,2,1,0:T(8,128)(2,1)}) custom-call(s32[4]{0:T(128)} %pad_add_fusion.place_ref.place, bf16[2,1024,1024]{2,1,0:T(8,128)(2,1)} %get-tuple-element.185.grads_ref, bf16[1024,1024]{1,0:T(8,128)(2,1)} %pad_maximum_fusion.2.source_ref, ...), custom_call_target="tpu_custom_call" | custom-call | flops 1024 | bytes 1024 | tf_op jit(solution)/shard_map/pallas_call | solution.py:1177
  432.5 2.8 fusion.13
  435.3 1.8 pad_maximum_fusion.1
  437.0 5.4 shard_map.258
  442.4 2.1 collective-permute-start.8
  445.6 26.2 %shard_map.259 = (f32[1536,1024]{1,0:T(8,128)}, bf16[1536,1024]{1,0:T(8,128)(2,1)}, f32[8,1024]{1,0:T(8,128)}, bf16[2,2,4,2,32,1024]{5,4,3,2,1,0:T(8,128)(2,1)}, bf16[2,2,4,2,32,1024]{5,4,3,2,1,0:T(8,128)(2,1)}) custom-call(s32[4]{0:T(128)} %pad_add_fusion.place_ref.place, bf16[1536,1024]{1,0:T(8,128)(2,1)} %get-tuple-element.192.grad_ref, ...), custom_call_target="tpu_custom_call" | custom-call | flops 1024 | bytes 1024 | tf_op jit(solution)/shard_map/pallas_call | solution.py:1094
  473.4 7.0 shard_map.261
  482.6 5.8 shard_map.260
  489.4 1.8 collective-permute-start.14
  491.2 1.5 collective-permute-start.15
  492.7 2.3 collective-permute-start.16
  495.1 49.6 %shard_map.262.grads_ref = bf16[3,1536,1024]{2,1,0:T(8,128)(2,1)} custom-call(bf16[1536,1024]{1,0:T(8,128)(2,1)} %get-tuple-element.150.q_ref, bf16[1536,1024]{1,0:T(8,128)(2,1)} %get-tuple-element.151.k_ref, bf16[1536,1024]{1,0:T(8,128)(2,1)} %get-tuple-element.152.v_ref, bf16[1536,1024]{1,0:T(8,128)(2,1)} %get-tuple-element.153.extra_ref, ...), custom_call_target="tpu_custom_call" | custom-call | flops 1024 | bytes 1024 | tf_op jit(solution)/shard_map/pallas_call | solution.py:613
  544.7 2.6 collective-permute-done.12.refs_6_
  548.0 3.2 add_convert_fusion
  551.2 4.9 shard_map.263
  556.5 1.7 collective-permute-start.18
  558.2 36.1 %shard_map.264 = (bf16[1536,1024]{1,0:T(8,128)(2,1)}, f32[8,1024]{1,0:T(8,128)}, bf16[2,2,4,3,32,1024]{5,4,3,2,1,0:T(8,128)(2,1)}, bf16[2,2,4,3,32,1024]{5,4,3,2,1,0:T(8,128)(2,1)}) custom-call(s32[4]{0:T(128)} %compare_select_fusion.3.held, s32[4]{0:T(128)} %pad_add_fusion.place_ref.place, bf16[3,1536,1024]{2,1,0:T(8,128)(2,1)} %shard_map.262.grads_ref, ...), custom_call_target="tpu_custom_call" | custom-call | flops 1024 | bytes 1024 | tf_op jit(solution)/shard_map/pallas_call | solution.py:1139
  594.3 3.2 collective-permute-done.18
  600.0 5.7 shard_map.266
  608.2 1.7 copy-done.3
  609.8 4.1 shard_map.265
  615.8 1.8 reshape.146
  617.6 2.3 pad_maximum_fusion.4
  620.1 2.0 collective-permute-start.21
  623.3 2.7 slice.108
  626.5 1.6 select_bitcast_fusion.3
  629.6 2.8 collective-permute-start.23
  632.4 1.5 maximum_bitcast_fusion.2
  633.9 1.9 maximum_bitcast_fusion
  635.9 10.5 %collective-permute-done.22 = bf16[5,32,1024]{2,1,0:T(8,128)(2,1)S(1)} collective-permute-done((bf16[5,32,1024]{2,1,0:T(8,128)(2,1)S(1)}, bf16[5,32,1024]{2,1,0:T(8,128)(2,1)S(1)}, u32[]{:S(2)}, u32[]{:S(2)}) %collective-permute-start.22) | collective-permute-done | bytes 327712 | tf_op jit(solution)/shard_map/ppermute | solution.py:1358
  646.6 4.3 collective-permute-done.20.refs_2_
  652.1 3.4 shard_map.267
  656.1 3.2 collective-permute-start.25
  659.3 1.9 collective-permute-done.25
  661.2 1.8 collective-permute-start.26
  663.0 3.0 collective-permute-done.26
  666.0 13.3 %collective-permute-done.28.refs_3_ = bf16[4,3,32,1024]{3,2,1,0:T(8,128)(2,1)} collective-permute-done((bf16[4,3,32,1024]{3,2,1,0:T(8,128)(2,1)}, bf16[4,3,32,1024]{3,2,1,0:T(8,128)(2,1)}, u32[]{:S(2)}, u32[]{:S(2)}) %collective-permute-start.28) | collective-permute-done | bytes 786464 | tf_op jit(solution)/shard_map/ppermute | solution.py:1204
  679.3 4.7 shard_map.268
  687.7 1.6 collective-permute-start.31
  689.3 1.6 select_bitcast_fusion.1
  691.5 3.8 collective-permute-done.29
  695.4 6.0 collective-permute-done.30
  702.2 1.9 maximum_bitcast_fusion.1
  705.9 9.1 %collective-permute-done.32 = bf16[8,32,1024]{2,1,0:T(8,128)(2,1)S(1)} collective-permute-done((bf16[8,32,1024]{2,1,0:T(8,128)(2,1)S(1)}, bf16[8,32,1024]{2,1,0:T(8,128)(2,1)S(1)}, u32[]{:S(2)}, u32[]{:S(2)}) %collective-permute-start.32) | collective-permute-done | bytes 524320 | tf_op jit(solution)/shard_map/ppermute | solution.py:1204
  (165 shorter events, 43.7 us)
Async XLA Ops:
  7.2 73.9 %copy-start = (s32[2,1,1536]{2,1,0:T(1,128)S(1)}, s32[2,1,1536]{2,1,0:T(1,128)}, u32[]{:S(2)}) copy-start(s32[2,1,1536]{2,1,0:T(1,128)} %param.18) | copy-start | bytes 36868
  7.2 98.9 %all-gather.5.cloned.1.call-start = ((), (), s32[]{:S(2)}) async-start(), calls=%async_computation | async-start | bytes 18382848 | tf_op jit(solution)/shard_map/all_gather | solution.py:1422
  11.7 211.3 %all-gather.7.cloned.1.call-start = ((), (), s32[]{:S(2)}) async-start(), calls=%async_computation.1 | async-start | bytes 18382848 | tf_op jit(solution)/shard_map/all_gather | solution.py:1443
  11.7 6.5 copy-start.17
  15.2 63.4 %collective-permute-start = (bf16[768,1024]{1,0:T(8,128)(2,1)}, bf16[768,1024]{1,0:T(8,128)(2,1)S(1)}, u32[]{:S(2)}, u32[]{:S(2)}) collective-permute-start(bf16[768,1024]{1,0:T(8,128)(2,1)} %get-tuple-element.353), channel_id=1, source_target_pairs={{0,16},{16,0},{1,17},{17,1},{2,18},{18,2},{3,19},{19,3},{4,20},{20... | collective-permute-start | bytes 4718600 | tf_op jit(solution)/shard_map/ppermute | solution.py:1204
  19.2 56.1 %collective-permute-start.1 = (bf16[512,1024]{1,0:T(8,128)(2,1)}, bf16[512,1024]{1,0:T(8,128)(2,1)}, u32[]{:S(2)}, u32[]{:S(2)}) collective-permute-start(bf16[512,1024]{1,0:T(8,128)(2,1)} %dynamic-slice_bitcast_fusion.4), channel_id=1, source_target_pairs={{0,16},{16,0},{1,17},{17,1},{2,18},{18,2},{3,19},{19,3},{4,20},{20... | collective-permute-start | bytes 3145736 | tf_op jit(solution)/shard_map/ppermute | solution.py:1204
  78.6 2.0 copy-start.25
  78.6 2.0 copy-start.26
  107.5 17.0 %copy-start.15 = (bf16[2,1,768,1024]{3,2,1,0:T(8,128)(2,1)S(1)}, bf16[2,1,768,1024]{3,2,1,0:T(8,128)(2,1)}, u32[]{:S(2)}) copy-start(bf16[2,1,768,1024]{3,2,1,0:T(8,128)(2,1)} %param.17) | copy-start | bytes 9437188
  126.0 81.8 %collective-permute-start.2 = (bf16[768,1024]{1,0:T(8,128)(2,1)S(1)}, bf16[768,1024]{1,0:T(8,128)(2,1)S(1)}, u32[]{:S(2)}, u32[]{:S(2)}) collective-permute-start(bf16[768,1024]{1,0:T(8,128)(2,1)S(1)} %get-tuple-element.348), channel_id=1, source_target_pairs={{0,16},{16,0},{1,17},{17,1},{2,18},{18,2},{3,19},{19,3},{4,20},{20... | collective-permute-start | bytes 4718600 | tf_op jit(solution)/shard_map/ppermute | solution.py:1204
  207.9 1.2 copy-start.18
  336.3 21.2 %collective-permute-start.3 = (bf16[2,2,4,4,32,1024]{5,4,3,2,1,0:T(8,128)(2,1)}, bf16[2,2,4,4,32,1024]{5,4,3,2,1,0:T(8,128)(2,1)S(1)}, u32[]{:S(2)}, u32[]{:S(2)}) collective-permute-start(bf16[2,2,4,4,32,1024]{5,4,3,2,1,0:T(8,128)(2,1)} %get-tuple-element.174), channel_id=1, source_target_pairs={{0,1},{1,0},{2,3},{3,2},{4,5},{5,4},{6,7},{7,6},{8,9},{9,8},{10,11... | collective-permute-start | bytes 12582920 | tf_op jit(solution)/shard_map/ppermute | solution.py:1212
  336.3 21.2 %collective-permute-start.4 = (bf16[2,2,4,4,32,1024]{5,4,3,2,1,0:T(8,128)(2,1)}, bf16[2,2,4,4,32,1024]{5,4,3,2,1,0:T(8,128)(2,1)}, u32[]{:S(2)}, u32[]{:S(2)}) collective-permute-start(bf16[2,2,4,4,32,1024]{5,4,3,2,1,0:T(8,128)(2,1)} %get-tuple-element.176), channel_id=1, source_target_pairs={{0,1},{1,0},{2,3},{3,2},{4,5},{5,4},{6,7},{7,6},{8,9},{9,8},{10,11... | collective-permute-start | bytes 12582920 | tf_op jit(solution)/shard_map/ppermute | solution.py:1212
  357.6 1.9 copy-start.2
  366.2 48.9 %collective-permute-start.6 = (bf16[2,4,4,32,1024]{4,3,2,1,0:T(8,128)(2,1)}, bf16[2,4,4,32,1024]{4,3,2,1,0:T(8,128)(2,1)S(1)}, u32[]{:S(2)}, u32[]{:S(2)}) collective-permute-start(bf16[2,4,4,32,1024]{4,3,2,1,0:T(8,128)(2,1)} %get-tuple-element.183), channel_id=1, source_target_pairs={{0,2},{1,3},{2,0},{3,1},{4,6},{5,7},{6,4},{7,5},{8,10},{9,11},{10,... | collective-permute-start | bytes 6291464 | tf_op jit(solution)/shard_map/ppermute | solution.py:1208
  367.1 48.0 %collective-permute-start.7 = (bf16[2,4,4,32,1024]{4,3,2,1,0:T(8,128)(2,1)}, bf16[2,4,4,32,1024]{4,3,2,1,0:T(8,128)(2,1)S(1)}, u32[]{:S(2)}, u32[]{:S(2)}) collective-permute-start(bf16[2,4,4,32,1024]{4,3,2,1,0:T(8,128)(2,1)} %get-tuple-element.184), channel_id=1, source_target_pairs={{0,16},{16,0},{1,17},{17,1},{2,18},{18,2},{3,19},{19,3},{4,20},{20... | collective-permute-start | bytes 6291464 | tf_op jit(solution)/shard_map/ppermute | solution.py:1204
  367.1 47.9 %collective-permute-start.5 = (bf16[2,2,4,1,32,1024]{5,4,3,2,1,0:T(8,128)(2,1)}, bf16[2,2,4,1,32,1024]{5,4,3,2,1,0:T(8,128)(2,1)S(1)}, u32[]{:S(2)}, u32[]{:S(2)}) collective-permute-start(bf16[2,2,4,1,32,1024]{5,4,3,2,1,0:T(8,128)(2,1)} %get-tuple-element.182), channel_id=1, source_target_pairs={{0,1},{1,0},{2,3},{3,2},{4,5},{5,4},{6,7},{7,6},{8,9},{9,8},{10,11... | collective-permute-start | bytes 3145736 | tf_op jit(solution)/shard_map/ppermute | solution.py:1212
  415.0 17.4 %copy-start.7 = (bf16[2,2,4,1,32,1024]{5,4,3,2,1,0:T(8,128)(2,1)}, bf16[2,2,4,1,32,1024]{5,4,3,2,1,0:T(8,128)(2,1)S(1)}, u32[]{:S(2)}) copy-start(bf16[2,2,4,1,32,1024]{5,4,3,2,1,0:T(8,128)(2,1)S(1)} %collective-permute-done.5.refs_1_) | copy-start | bytes 3145732
  415.1 17.4 %copy-start.8 = (bf16[2,4,4,32,1024]{4,3,2,1,0:T(8,128)(2,1)}, bf16[2,4,4,32,1024]{4,3,2,1,0:T(8,128)(2,1)S(1)}, u32[]{:S(2)}) copy-start(bf16[2,4,4,32,1024]{4,3,2,1,0:T(8,128)(2,1)S(1)} %collective-permute-done.6.refs_2_) | copy-start | bytes 6291460
  415.1 17.4 %copy-start.9 = (bf16[2,4,4,32,1024]{4,3,2,1,0:T(8,128)(2,1)}, bf16[2,4,4,32,1024]{4,3,2,1,0:T(8,128)(2,1)S(1)}, u32[]{:S(2)}) copy-start(bf16[2,4,4,32,1024]{4,3,2,1,0:T(8,128)(2,1)S(1)} %collective-permute-done.7.refs_5_.refs_6_) | copy-start | bytes 6291460
  432.5 2.8 copy-start.10
  442.4 29.5 %collective-permute-start.8 = (bf16[4,4,32,1024]{3,2,1,0:T(8,128)(2,1)}, bf16[4,4,32,1024]{3,2,1,0:T(8,128)(2,1)S(1)}, u32[]{:S(2)}, u32[]{:S(2)}) collective-permute-start(bf16[4,4,32,1024]{3,2,1,0:T(8,128)(2,1)} %get-tuple-element.198), channel_id=1, source_target_pairs={{0,16},{16,0},{1,17},{17,1},{2,18},{18,2},{3,19},{19,3},{4,20},{20... | collective-permute-start | bytes 3145736 | tf_op jit(solution)/shard_map/ppermute | solution.py:1204
  444.6 27.3 %collective-permute-start.9 = (bf16[4,4,32,1024]{3,2,1,0:T(8,128)(2,1)}, bf16[4,4,32,1024]{3,2,1,0:T(8,128)(2,1)S(1)}, u32[]{:S(2)}, u32[]{:S(2)}) collective-permute-start(bf16[4,4,32,1024]{3,2,1,0:T(8,128)(2,1)} %get-tuple-element.199), channel_id=1, source_target_pairs={{0,2},{1,3},{2,0},{3,1},{4,6},{5,7},{6,4},{7,5},{8,10},{9,11},{10,... | collective-permute-start | bytes 3145736 | tf_op jit(solution)/shard_map/ppermute | solution.py:1208
  471.9 1.6 copy-start.20
  472.9 7.5 %collective-permute-start.10 = (bf16[2,2,4,2,32,1024]{5,4,3,2,1,0:T(8,128)(2,1)}, bf16[2,2,4,2,32,1024]{5,4,3,2,1,0:T(8,128)(2,1)S(1)}, u32[]{:S(2)}, u32[]{:S(2)}) collective-permute-start(bf16[2,2,4,2,32,1024]{5,4,3,2,1,0:T(8,128)(2,1)} %get-tuple-element.204), channel_id=1, source_target_pairs={{0,1},{1,0},{2,3},{3,2},{4,5},{5,4},{6,7},{7,6},{8,9},{9,8},{10,11... | collective-permute-start | bytes 6291464 | tf_op jit(solution)/shard_map/ppermute | solution.py:1212
  472.9 7.6 %collective-permute-start.11 = (bf16[2,2,4,2,32,1024]{5,4,3,2,1,0:T(8,128)(2,1)}, bf16[2,2,4,2,32,1024]{5,4,3,2,1,0:T(8,128)(2,1)S(1)}, u32[]{:S(2)}, u32[]{:S(2)}) collective-permute-start(bf16[2,2,4,2,32,1024]{5,4,3,2,1,0:T(8,128)(2,1)} %get-tuple-element.206), channel_id=1, source_target_pairs={{0,1},{1,0},{2,3},{3,2},{4,5},{5,4},{6,7},{7,6},{8,9},{9,8},{10,11... | collective-permute-start | bytes 6291464 | tf_op jit(solution)/shard_map/ppermute | solution.py:1212
  480.5 1.3 copy-start.4
  480.5 2.1 copy-start.5
  488.4 59.0 %collective-permute-start.12 = (bf16[2,4,5,32,1024]{4,3,2,1,0:T(8,128)(2,1)}, bf16[2,4,5,32,1024]{4,3,2,1,0:T(8,128)(2,1)S(1)}, u32[]{:S(2)}, u32[]{:S(2)}) collective-permute-start(bf16[2,4,5,32,1024]{4,3,2,1,0:T(8,128)(2,1)} %shard_map.260), channel_id=1, source_target_pairs={{0,2},{1,3},{2,0},{3,1},{4,6},{5,7},{6,4},{7,5},{8,10},{9,11},{10,... | collective-permute-start | bytes 7864328 | tf_op jit(solution)/shard_map/ppermute | solution.py:1208
  489.3 58.7 %collective-permute-start.13 = (bf16[1280,1024]{1,0:T(8,128)(2,1)}, bf16[1280,1024]{1,0:T(8,128)(2,1)S(1)}, u32[]{:S(2)}, u32[]{:S(2)}) collective-permute-start(bf16[1280,1024]{1,0:T(8,128)(2,1)} %pad_maximum_fusion.1), channel_id=1, source_target_pairs={{0,16},{16,0},{1,17},{17,1},{2,18},{18,2},{3,19},{19,3},{4,20},{20... | collective-permute-start | bytes 7864328 | tf_op jit(solution)/shard_map/ppermute | solution.py:1204
  489.4 55.3 %collective-permute-start.14 = (bf16[8,32,1024]{2,1,0:T(8,128)(2,1)}, bf16[8,32,1024]{2,1,0:T(8,128)(2,1)S(1)}, u32[]{:S(2)}, u32[]{:S(2)}) collective-permute-start(bf16[8,32,1024]{2,1,0:T(8,128)(2,1)} %get-tuple-element.218), channel_id=1, source_target_pairs={{0,4},{1,5},{2,6},{3,7},{4,8},{5,9},{6,10},{7,11},{8,12},{9,13},{1... | collective-permute-start | bytes 1572872 | tf_op jit(solution)/shard_map/ppermute | solution.py:1358
  491.2 53.5 %collective-permute-start.15 = (bf16[8,32,1024]{2,1,0:T(8,128)(2,1)}, bf16[8,32,1024]{2,1,0:T(8,128)(2,1)}, u32[]{:S(2)}, u32[]{:S(2)}) collective-permute-start(bf16[8,32,1024]{2,1,0:T(8,128)(2,1)} %get-tuple-element.219), channel_id=1, source_target_pairs={{0,8},{1,9},{2,10},{3,11},{4,12},{5,13},{6,14},{7,15},{8,0},{9,1},... | collective-permute-start | bytes 1572872 | tf_op jit(solution)/shard_map/ppermute | solution.py:1358
  492.7 52.0 %collective-permute-start.16 = (bf16[8,32,1024]{2,1,0:T(8,128)(2,1)}, bf16[8,32,1024]{2,1,0:T(8,128)(2,1)}, u32[]{:S(2)}, u32[]{:S(2)}) collective-permute-start(bf16[8,32,1024]{2,1,0:T(8,128)(2,1)} %get-tuple-element.220), channel_id=1, source_target_pairs={{0,12},{1,13},{2,14},{3,15},{4,0},{5,1},{6,2},{7,3},{8,4},{9,5},{1... | collective-permute-start | bytes 1572872 | tf_op jit(solution)/shard_map/ppermute | solution.py:1358
  544.7 2.7 copy-start.23
  547.4 3.8 copy-start.6
  548.0 8.1 %copy-start.16 = (bf16[1280,1024]{1,0:T(8,128)(2,1)}, bf16[1280,1024]{1,0:T(8,128)(2,1)S(1)}, u32[]{:S(2)}) copy-start(bf16[1280,1024]{1,0:T(8,128)(2,1)S(1)} %collective-permute-done.13) | copy-start | bytes 7864324
  556.1 41.3 %collective-permute-start.17 = (bf16[4,5,32,1024]{3,2,1,0:T(8,128)(2,1)}, bf16[4,5,32,1024]{3,2,1,0:T(8,128)(2,1)S(1)}, u32[]{:S(2)}, u32[]{:S(2)}) collective-permute-start(bf16[4,5,32,1024]{3,2,1,0:T(8,128)(2,1)} %shard_map.263), channel_id=1, source_target_pairs={{0,16},{16,0},{1,17},{17,1},{2,18},{18,2},{3,19},{19,3},{4,20},{20... | collective-permute-start | bytes 3932168 | tf_op jit(solution)/shard_map/ppermute | solution.py:1204
  556.5 41.0 %collective-permute-start.18 = (bf16[8,32,1024]{2,1,0:T(8,128)(2,1)S(1)}, bf16[8,32,1024]{2,1,0:T(8,128)(2,1)S(1)}, u32[]{:S(2)}, u32[]{:S(2)}) collective-permute-start(bf16[8,32,1024]{2,1,0:T(8,128)(2,1)S(1)} %add_convert_fusion), channel_id=1, source_target_pairs={{0,16},{16,0},{1,17},{17,1},{2,18},{18,2},{3,19},{19,3},{4,20},{20... | collective-permute-start | bytes 1572872 | tf_op jit(solution)/shard_map/ppermute | solution.py:1204
  598.5 9.7 %collective-permute-start.19 = (bf16[2,2,4,3,32,1024]{5,4,3,2,1,0:T(8,128)(2,1)}, bf16[2,2,4,3,32,1024]{5,4,3,2,1,0:T(8,128)(2,1)S(1)}, u32[]{:S(2)}, u32[]{:S(2)}) collective-permute-start(bf16[2,2,4,3,32,1024]{5,4,3,2,1,0:T(8,128)(2,1)} %get-tuple-element.237), channel_id=1, source_target_pairs={{0,1},{1,0},{2,3},{3,2},{4,5},{5,4},{6,7},{7,6},{8,9},{9,8},{10,11... | collective-permute-start | bytes 9437192 | tf_op jit(solution)/shard_map/ppermute | solution.py:1212
  608.2 1.7 copy-start.3
  613.9 37.0 %collective-permute-start.20 = (bf16[2,4,3,32,1024]{4,3,2,1,0:T(8,128)(2,1)}, bf16[2,4,3,32,1024]{4,3,2,1,0:T(8,128)(2,1)S(1)}, u32[]{:S(2)}, u32[]{:S(2)}) collective-permute-start(bf16[2,4,3,32,1024]{4,3,2,1,0:T(8,128)(2,1)} %shard_map.265), channel_id=1, source_target_pairs={{0,2},{1,3},{2,0},{3,1},{4,6},{5,7},{6,4},{7,5},{8,10},{9,11},{10,... | collective-permute-start | bytes 4718600 | tf_op jit(solution)/shard_map/ppermute | solution.py:1208
  615.7 6.4 copy-start.28
  617.6 8.9 %copy-start.13 = (bf16[1536,1024]{1,0:T(8,128)(2,1)S(1)}, bf16[1536,1024]{1,0:T(8,128)(2,1)}, u32[]{:S(2)}) copy-start(bf16[1536,1024]{1,0:T(8,128)(2,1)} %get-tuple-element.255) | copy-start | bytes 9437188
  619.9 9.7 %collective-permute-start.24 = (f32[6,1024]{1,0:T(8,128)S(1)}, f32[6,1024]{1,0:T(8,128)S(1)}, u32[]{:S(2)}, u32[]{:S(2)}) collective-permute-start(f32[6,1024]{1,0:T(8,128)S(1)} %pad_maximum_fusion.8), channel_id=1, source_target_pairs={{0,1},{1,0},{2,3},{3,2},{4,5},{5,4},{6,7},{7,6},{8,9},{9,8},{10,11... | collective-permute-start | bytes 73736 | tf_op jit(solution)/shard_map/ppermute | solution.py:1212
  620.1 15.7 %collective-permute-start.21 = (bf16[5,32,1024]{2,1,0:T(8,128)(2,1)}, bf16[5,32,1024]{2,1,0:T(8,128)(2,1)S(1)}, u32[]{:S(2)}, u32[]{:S(2)}) collective-permute-start(bf16[5,32,1024]{2,1,0:T(8,128)(2,1)} %get-tuple-element.251), channel_id=1, source_target_pairs={{0,4},{1,5},{2,6},{3,7},{4,8},{5,9},{6,10},{7,11},{8,12},{9,13},{1... | collective-permute-start | bytes 983048 | tf_op jit(solution)/shard_map/ppermute | solution.py:1358
  622.2 24.2 %collective-permute-start.22 = (bf16[5,32,1024]{2,1,0:T(8,128)(2,1)S(1)}, bf16[5,32,1024]{2,1,0:T(8,128)(2,1)S(1)}, u32[]{:S(2)}, u32[]{:S(2)}) collective-permute-start(bf16[5,32,1024]{2,1,0:T(8,128)(2,1)S(1)} %copy-done.28), channel_id=1, source_target_pairs={{0,8},{1,9},{2,10},{3,11},{4,12},{5,13},{6,14},{7,15},{8,0},{9,1},... | collective-permute-start | bytes 983048 | tf_op jit(solution)/shard_map/ppermute | solution.py:1358
  625.9 2.2 copy-start.12
  625.9 58.0 %collective-permute-start.27 = (bf16[768,1024]{1,0:T(8,128)(2,1)}, bf16[768,1024]{1,0:T(8,128)(2,1)}, u32[]{:S(2)}, u32[]{:S(2)}) collective-permute-start(bf16[768,1024]{1,0:T(8,128)(2,1)} %slice.108), channel_id=1, source_target_pairs={{0,16},{16,0},{1,17},{17,1},{2,18},{18,2},{3,19},{19,3},{4,20},{20... | collective-permute-start | bytes 4718600 | tf_op jit(solution)/shard_map/ppermute | solution.py:1204
  628.1 1.4 copy-start.27
  629.6 16.8 %collective-permute-start.23 = (bf16[5,32,1024]{2,1,0:T(8,128)(2,1)S(1)}, bf16[5,32,1024]{2,1,0:T(8,128)(2,1)S(1)}, u32[]{:S(2)}, u32[]{:S(2)}) collective-permute-start(bf16[5,32,1024]{2,1,0:T(8,128)(2,1)S(1)} %copy-done.27), channel_id=1, source_target_pairs={{0,12},{1,13},{2,14},{3,15},{4,0},{5,1},{6,2},{7,3},{8,4},{9,5},{1... | collective-permute-start | bytes 983048 | tf_op jit(solution)/shard_map/ppermute | solution.py:1358
  633.9 12.5 %copy-start.22 = (f32[5,32,1024]{2,1,0:T(8,128)S(1)}, f32[5,32,1024]{2,1,0:T(8,128)}, u32[]{:S(2)}) copy-start(f32[5,32,1024]{2,1,0:T(8,128)} %get-tuple-element.250) | copy-start | bytes 1966084
  650.9 1.2 copy-start.11
  655.5 23.8 %collective-permute-start.28 = (bf16[4,3,32,1024]{3,2,1,0:T(8,128)(2,1)}, bf16[4,3,32,1024]{3,2,1,0:T(8,128)(2,1)}, u32[]{:S(2)}, u32[]{:S(2)}) collective-permute-start(bf16[4,3,32,1024]{3,2,1,0:T(8,128)(2,1)} %shard_map.267), channel_id=1, source_target_pairs={{0,16},{16,0},{1,17},{17,1},{2,18},{18,2},{3,19},{19,3},{4,20},{20... | collective-permute-start | bytes 2359304 | tf_op jit(solution)/shard_map/ppermute | solution.py:1204
  656.1 5.1 collective-permute-start.25
  661.2 4.8 collective-permute-start.26
  666.0 23.2 %copy-start.14 = (bf16[1536,1024]{1,0:T(8,128)(2,1)S(1)}, bf16[1536,1024]{1,0:T(8,128)(2,1)}, u32[]{:S(2)}) copy-start(bf16[1536,1024]{1,0:T(8,128)(2,1)} %get-tuple-element.260) | copy-start | bytes 9437188
  684.0 17.4 %copy-start.24 = (f32[3,32,1024]{2,1,0:T(8,128)S(1)}, f32[3,32,1024]{2,1,0:T(8,128)}, u32[]{:S(2)}) copy-start(f32[3,32,1024]{2,1,0:T(8,128)} %get-tuple-element.270) | copy-start | bytes 1179652
  684.0 6.9 collective-permute-start.33
  685.4 9.9 %collective-permute-start.29 = (bf16[3,32,1024]{2,1,0:T(8,128)(2,1)}, bf16[3,32,1024]{2,1,0:T(8,128)(2,1)S(1)}, u32[]{:S(2)}, u32[]{:S(2)}) collective-permute-start(bf16[3,32,1024]{2,1,0:T(8,128)(2,1)} %get-tuple-element.271), channel_id=1, source_target_pairs={{0,4},{1,5},{2,6},{3,7},{4,8},{5,9},{6,10},{7,11},{8,12},{9,13},{1... | collective-permute-start | bytes 589832 | tf_op jit(solution)/shard_map/ppermute | solution.py:1358
  686.4 15.0 %collective-permute-start.30 = (bf16[3,32,1024]{2,1,0:T(8,128)(2,1)}, bf16[3,32,1024]{2,1,0:T(8,128)(2,1)S(1)}, u32[]{:S(2)}, u32[]{:S(2)}) collective-permute-start(bf16[3,32,1024]{2,1,0:T(8,128)(2,1)} %get-tuple-element.272), channel_id=1, source_target_pairs={{0,8},{1,9},{2,10},{3,11},{4,12},{5,13},{6,14},{7,15},{8,0},{9,1},... | collective-permute-start | bytes 589832 | tf_op jit(solution)/shard_map/ppermute | solution.py:1358
  687.7 13.7 %collective-permute-start.31 = (bf16[3,32,1024]{2,1,0:T(8,128)(2,1)}, bf16[3,32,1024]{2,1,0:T(8,128)(2,1)S(1)}, u32[]{:S(2)}, u32[]{:S(2)}) collective-permute-start(bf16[3,32,1024]{2,1,0:T(8,128)(2,1)} %get-tuple-element.273), channel_id=1, source_target_pairs={{0,12},{1,13},{2,14},{3,15},{4,0},{5,1},{6,2},{7,3},{8,4},{9,5},{1... | collective-permute-start | bytes 589832 | tf_op jit(solution)/shard_map/ppermute | solution.py:1358
  690.9 13.2 %collective-permute-start.34 = (f32[6,1024]{1,0:T(8,128)S(1)}, f32[6,1024]{1,0:T(8,128)S(1)}, u32[]{:S(2)}, u32[]{:S(2)}) collective-permute-start(f32[6,1024]{1,0:T(8,128)S(1)} %add.136), channel_id=1, source_target_pairs={{0,16},{16,0},{1,17},{17,1},{2,18},{18,2},{3,19},{19,3},{4,20},{20... | collective-permute-start | bytes 73736 | tf_op jit(solution)/shard_map/ppermute | solution.py:1204
  701.5 13.4 %collective-permute-start.32 = (bf16[8,32,1024]{2,1,0:T(8,128)(2,1)S(1)}, bf16[8,32,1024]{2,1,0:T(8,128)(2,1)S(1)}, u32[]{:S(2)}, u32[]{:S(2)}) collective-permute-start(bf16[8,32,1024]{2,1,0:T(8,128)(2,1)S(1)} %pad_maximum_fusion.6), channel_id=1, source_target_pairs={{0,16},{16,0},{1,17},{17,1},{2,18},{18,2},{3,19},{19,3},{4,20},{20... | collective-permute-start | bytes 1572872 | tf_op jit(solution)/shard_map/ppermute | solution.py:1204
  715.0 2.9 copy-start.1
  (2 other events, 2.1 us)
Sparse Core Ops, SparseCore 0:
  11.8 94.2 all-gather.4
  107.7 91.5 all-gather.6
